TPU v7x, 32 devices: a whole 2x2x4 slice. The times are simulated.
32 devices in a mesh: dp: 8 (over y, x, core), tensor: 4 (over z).
Axes of the slice: x: 2, y: 2, z: 4, core: 2. Of those that a mesh axis runs over, the one named last changes fastest.
Arguments:
- stream: float32 [16384, 768], P(('dp', 'tensor')), may hold values from -6 to 6
- cotangent: float32 [16384, 768], P(('dp', 'tensor')), may hold values from -6 to 6
- gain_attention: float32 [768], replicated, may hold values from 0.5 to 1.5
- w_inputs: bfloat16 [3, 768, 768], P(None, None, 'tensor'), may hold values from -0.21875 to 0.21875
- w_output: bfloat16 [768, 768], P('tensor'), may hold values from -0.625 to 0.625
- gain_experts: float32 [768], replicated, may hold values from 0.5 to 1.5
- w_router: bfloat16 [768, 10], replicated, may hold values from -0.109375 to 0.109375
- w_carry: float32 [10, 10], replicated, may hold values from -2 to 2
- w_gate_up: bfloat16 [6, 768, 2, 2048], P(None, None, None, 'tensor'), may hold values from -0.21875 to 0.21875
- w_down: bfloat16 [6, 2048, 768], P(None, 'tensor'), may hold values from -0.1875 to 0.1875
- w_constant: float32 [2, 2, 768], replicated, may hold values from -0.21875 to 0.21875
- constant_vectors: float32 [2, 768], replicated, may hold values from -6 to 6
- previous_logits: float32 [16384, 10], P('dp'), may hold values from -3 to 3
- routes: int32 [16384, 2], P('dp'), may hold values from 0 to 9, all different within a row; in each aligned block of 2048 rows (0 to 2047, 2048 to 4095, ...) at most 768 rows name the same one
- valid: int32 [16384], P('dp'), may hold values from 0 to 1
- prefix: int32 [16], P('dp'), may hold values from 1 to 1024
Outputs:
- block_out: float32 [16384, 768], P(('dp', 'tensor'))
- grad_stream: float32 [16384, 768], P(('dp', 'tensor'))
- grad_gain_attention: float32 [768], replicated
- grad_inputs: float32 [3, 768, 768], P(None, None, 'tensor')
- grad_output: float32 [768, 768], P('tensor')
- grad_gain_experts: float32 [768], replicated
- grad_router: float32 [768, 10], replicated
- grad_carry: float32 [10, 10], replicated
- grad_gate_up: float32 [6, 768, 2, 2048], P(None, None, None, 'tensor')
- grad_down: float32 [6, 2048, 768], P(None, 'tensor')
- grad_constant: float32 [2, 2, 768], replicated
- grad_vectors: float32 [2, 768], replicated
- grad_previous: float32 [16384, 10], P(('dp', 'tensor'))
- rms_values: float32 [3], replicated
Inputs may be any that keep to these rules, and one draw needn't show every extreme that they name: `routes`: each row names two different experts: 0 to 5 feed-forward, 6 zero, 7 copy, the last two constant; among the rows of one index of dp no expert is named more than 768 times.
All inputs are finite; a program needn't handle non-finite values.
Results may differ from a plain program's by a relative error of at most 0.022.
Values may be sent and summed in bfloat16 or wider, within the bound.
No kernel may reach another device: no remote copies, remote signals or barrier semaphores. Data moves between devices by JAX's collectives and lax.ppermute only.
A program may use at most 192 MiB of HBM per device.

v0:
```python
import functools

import jax
import jax.numpy as jnp
from jax import lax
from jax.experimental import pallas as pl
from jax.experimental.pallas import tpu as pltpu
from jax.sharding import PartitionSpec as P

HEAD_DIM = 64
EXP_FFN = 6
SEQ_LEN = 1024
EPSILON = 1e-05
HIGHEST = lax.Precision.HIGHEST
F32 = jnp.float32
BF16 = jnp.bfloat16
I32 = jnp.int32

LANES = 128
TILE = 128
QUERY_BLOCK = 1024
GROUP = 4
GATHER = 3
COST_FORWARD, COST_BACKWARD, COST_EXPERT, COST_GRADS, COST_WIDEN, COST_ADD = 20, 32, 20, 11, 3, 3


def lasting(microseconds):
    return pl.CostEstimate(flops=0, bytes_accessed=microseconds * 3 * 10**6, transcendentals=0)


SIDE = ((0, 1), (1, 0), (2, 3), (3, 2))
CROSS = ((0, 2), (1, 3), (2, 0), (3, 1))
MIDDLE = ((1, 2), (2, 1))
OUTWARD = ((1, 0), (2, 3))
INWARD = ((0, 1), (3, 2))


def dot(left, right):
    return jnp.dot(left, right, preferred_element_type=F32)


def dot_nt(left, right):
    return lax.dot_general(left, right, (((1,), (1,)), ((), ())), preferred_element_type=F32)


def dot_tn(left, right):
    return lax.dot_general(left, right, (((0,), (0,)), ((), ())), preferred_element_type=F32)


def norm_forward(values, gain):
    inverse = lax.rsqrt(jnp.mean(values * values, axis=-1, keepdims=True) + EPSILON)
    return (values * inverse * gain, inverse)


def norm_backward(values, inverse, gain, grad):
    scaled = grad * gain
    inner = jnp.mean(scaled * values, axis=-1, keepdims=True)
    return inverse * scaled - values * inverse**3 * inner


def along_z(value, pairs):
    return lax.ppermute(value, "tensor", pairs)


def along_dp(value, bit, size):
    return lax.ppermute(value, "dp", [(i, i ^ (1 << bit)) for i in range(size)])


def behind(value, earlier):
    return lax.optimization_barrier((value, earlier))[0]


def slot_chunks(here):
    table = jnp.array([[0, 1, 2, 3], [1, 0, 2, 3], [2, 3, 1, 0], [3, 2, 1, 0]], I32)
    return lax.dynamic_slice_in_dim(table, here, 1, 0)[0]


def reduce_blocks(value, bits, index, size):
    for bit in bits:
        half = value.shape[0] // 2
        mine = (index >> bit) & 1
        sent = lax.dynamic_slice_in_dim(value, (1 - mine) * half, half, 0)
        kept = lax.dynamic_slice_in_dim(value, mine * half, half, 0)
        value = kept + along_dp(sent, bit, size)
    return value


def spread_blocks(value, bits, index, size):
    for bit in reversed(bits):
        mine = (index >> bit) & 1
        other = along_dp(value, bit, size)
        value = jnp.where(
            mine == 0,
            jnp.concatenate([value, other], axis=0),
            jnp.concatenate([other, value], axis=0),
        )
    return value


def sum_everywhere(value, bits, size):
    for bit in bits:
        value = value + along_dp(value, bit, size)
    value = value + along_z(value, SIDE)
    return value + along_z(value, CROSS)


def piece_place(index, order):
    place = 0
    for bit in order:
        place = 2 * place + ((index >> bit) & 1)
    return place


def rope_tables(offset):
    lane = jnp.arange(LANES, dtype=I32)
    row = jnp.arange(SEQ_LEN, dtype=I32)
    position = jnp.where(row < SEQ_LEN // 2, row + offset, row - offset).astype(F32)
    half = HEAD_DIM // 2
    frequency = 10000.0 ** (-(lane % half).astype(F32) / half)
    angles = position[:, None] * frequency[None, :]
    sign = jnp.where(lane % HEAD_DIM < half, -1.0, 1.0)
    return (jnp.cos(angles), jnp.sin(angles) * sign[None, :])


def swap_halves(value):
    half = HEAD_DIM // 2
    lane = lax.broadcasted_iota(I32, value.shape, 1)
    return jnp.where(
        lane % HEAD_DIM < half,
        pltpu.roll(value, LANES - half, 1),
        pltpu.roll(value, half, 1),
    )


def fill_bias(scalars, valid_ref, bias):
    offset, prefix = scalars[0], scalars[1]
    keys = lax.broadcasted_iota(I32, (SEQ_LEN, 1), 0)
    keys = jnp.where(keys < SEQ_LEN // 2, keys + offset, keys - offset)
    queries = lax.broadcasted_iota(I32, (1, SEQ_LEN), 1)
    queries = jnp.where(queries < SEQ_LEN // 2, queries + offset, queries - offset)
    seen = jnp.where(valid_ref[...] > 0, keys, SEQ_LEN)
    shown = ((seen <= queries) | (seen < prefix)) | (keys == queries)
    bias[...] = jnp.where(shown, 0.0, -1e30)


def head_lanes(value, head):
    lane = lax.broadcasted_iota(I32, value.shape, 1)
    return jnp.where((lane >= head * HEAD_DIM) & (lane < (head + 1) * HEAD_DIM), value, 0)


def attention_kernel(
    scalars, own, other, weights, w_out, cosine, sine, valid, *refs
):
    part_own, part_other, queries, keys, values, mixed, totals = refs[-11:-4]
    bias, key_rows, value_columns, total = refs[-4:]
    step = pl.program_id(0)
    half = SEQ_LEN // 2
    upper, lower = pl.ds(0, half), pl.ds(half, half)

    @pl.when(step == 0)
    def _():
        fill_bias(scalars, valid, bias)
        total[...] = jnp.zeros_like(total)

    for source, rows in ((own, upper), (other, lower)):
        x = source[...]
        for kind, target in ((0, queries), (1, keys), (2, values)):
            y = dot_nt(x, weights[kind])
            if kind < 2:
                y = y * cosine[rows, :] + swap_halves(y) * sine[rows, :]
            target[rows, :] = y.astype(BF16)
    key_rows[...] = keys[...]
    value_columns[...] = values[...].T

    @pl.loop(0, SEQ_LEN // QUERY_BLOCK)
    def _(index):
        columns = pl.ds(pl.multiple_of(index * QUERY_BLOCK, QUERY_BLOCK), QUERY_BLOCK)
        query = queries[columns, :] * 0.125
        outs = []
        for head in range(2):
            scores = dot_nt(key_rows[...], head_lanes(query, head)) + bias[:, columns]
            top = jnp.max(scores, axis=0, keepdims=True)
            raw = jnp.exp(scores - top)
            summed = jnp.sum(raw, axis=0, keepdims=True)
            shares = (raw * (1.0 / summed)).astype(BF16)
            outs.append(dot(value_columns[head * HEAD_DIM : (head + 1) * HEAD_DIM, :], shares))
            totals[0, head : head + 1, columns] = top + jnp.log(summed)
        mixed[columns, :] = jnp.concatenate(outs, axis=0).T.astype(BF16)

    total[...] += dot(mixed[...], w_out[...])

    @pl.when(step == pl.num_programs(0) - 1)
    def _():
        part_own[...] = total[upper, :].astype(BF16)
        part_other[...] = total[lower, :].astype(BF16)


def attention_specs(pairs, width):
    whole = lambda *shape: pl.BlockSpec(shape, lambda p, s: (0,) * len(shape))
    half = SEQ_LEN // 2
    rows = whole(half, width)
    weights = pl.BlockSpec((3, LANES, width), lambda p, s: (0, p, 0))
    w_out = pl.BlockSpec((LANES, width), lambda p, s: (p, 0))
    table = whole(SEQ_LEN, LANES)
    column = pl.BlockSpec((SEQ_LEN, LANES), lambda p, s: (0, p))
    totals = pl.BlockSpec((1, 8, SEQ_LEN), lambda p, s: (p, 0, 0))
    return (rows, weights, w_out, table, whole(SEQ_LEN, 1), column, totals)


def attention_forward(scalars, own, other, weights, w_out, cosine, sine, valid, ready):
    width = own.shape[1]
    pairs = weights.shape[1] // LANES
    rows, spec_w, spec_o, table, spec_v, column, totals = attention_specs(pairs, width)
    half = SEQ_LEN // 2
    shape = jax.ShapeDtypeStruct
    return pl.pallas_call(
        attention_kernel,
        grid_spec=pltpu.PrefetchScalarGridSpec(
            num_scalar_prefetch=1,
            grid=(pairs,),
            in_specs=[rows, rows, spec_w, spec_o, table, table, spec_v]
            + [pl.BlockSpec(memory_space=pl.ANY)] * len(ready),
            out_specs=[rows, rows, column, column, column, column, totals],
            scratch_shapes=[
                pltpu.VMEM((SEQ_LEN, SEQ_LEN), F32),
                pltpu.VMEM((SEQ_LEN, LANES), BF16),
                pltpu.VMEM((LANES, SEQ_LEN), BF16),
                pltpu.VMEM((SEQ_LEN, width), F32),
            ],
        ),
        out_shape=[
            shape((half, width), BF16),
            pltpu.HBM((half, width), BF16),
            *[pltpu.HBM((SEQ_LEN, pairs * LANES), BF16)] * 4,
            shape((pairs, 8, SEQ_LEN), F32),
        ],
        compiler_params=pltpu.CompilerParams(vmem_limit_bytes=48 * 2**20),
        cost_estimate=lasting(COST_FORWARD),
        name="attention_forward",
    )(scalars, own, other, weights, w_out, cosine, sine, valid, *ready)


def attention_back_kernel(
    scalars, own, other, weights, w_out, cosine, sine, valid,
    grad_own, grad_other, queries, keys, values, mixed, totals, *refs
):
    part_own, part_other, grad_w, grad_o, gain_row = refs[-12:-7]
    bias, grad_rows, key_columns, total, grad_q, grad_k, grad_v = refs[-7:]
    step = pl.program_id(0)
    half = SEQ_LEN // 2
    upper, lower = pl.ds(0, half), pl.ds(half, half)

    @pl.when(step == 0)
    def _():
        fill_bias(scalars, valid, bias)
        total[...] = jnp.zeros_like(total)

    grad_rows[upper, :] = dot_nt(grad_own[...], w_out[...]).astype(BF16)
    grad_rows[lower, :] = dot_nt(grad_other[...], w_out[...]).astype(BF16)
    columns_mixed = mixed[...].T
    grad_o[...] = (
        dot(columns_mixed[:, :half], grad_own[...]) + dot(columns_mixed[:, half:], grad_other[...])
    ).astype(BF16)
    key_columns[...] = keys[...].T
    grad_k[...] = jnp.zeros_like(grad_k)
    grad_v[...] = jnp.zeros_like(grad_v)

    @pl.loop(0, SEQ_LEN // QUERY_BLOCK)
    def _(index):
        columns = pl.ds(pl.multiple_of(index * QUERY_BLOCK, QUERY_BLOCK), QUERY_BLOCK)
        query = queries[columns, :] * 0.125
        grad = grad_rows[columns, :]
        outs = []
        for head in range(2):
            query_head = head_lanes(query, head)
            grad_head = head_lanes(grad, head)
            scores = dot_nt(keys[...], query_head) + bias[:, columns]
            shares = jnp.exp(scores - totals[0, head : head + 1, columns])
            grad_shares = dot_nt(values[...], grad_head)
            grad_v[...] += dot(shares.astype(BF16), grad_head)
            product = shares * grad_shares
            inner = jnp.sum(product, axis=0, keepdims=True)
            grad_scores = (product - shares * inner).astype(BF16)
            grad_k[...] += dot(grad_scores, query_head)
            outs.append(dot(key_columns[head * HEAD_DIM : (head + 1) * HEAD_DIM, :], grad_scores))
        grad_q[columns, :] = jnp.concatenate(outs, axis=0).T * 0.125

    for kind, source in ((0, grad_q), (1, grad_k), (2, grad_v)):
        y = source[...]
        if kind < 2:
            y = y * cosine[...] - swap_halves(y) * sine[...]
        y = y.astype(BF16)
        total[...] += dot(y, weights[kind])
        columns_y = y.T
        grad_w[kind] = (
            dot(columns_y[:, :half], own[...]) + dot(columns_y[:, half:], other[...])
        ).astype(BF16)

    @pl.when(step == pl.num_programs(0) - 1)
    def _():
        part_own[...] = total[upper, :].astype(BF16)
        part_other[...] = total[lower, :].astype(BF16)
        product = total[upper, :] * own[...].astype(F32) + total[lower, :] * other[...].astype(F32)
        gain_row[...] = jnp.sum(product.reshape(half // 8, 8, product.shape[1]), axis=0)


def attention_backward(
    scalars, own, other, weights, w_out, cosine, sine, valid, grad_own, grad_other, saved, ready
):
    width = own.shape[1]
    pairs = weights.shape[1] // LANES
    rows, spec_w, spec_o, table, spec_v, column, totals = attention_specs(pairs, width)
    half = SEQ_LEN // 2
    shape = jax.ShapeDtypeStruct
    return pl.pallas_call(
        attention_back_kernel,
        grid_spec=pltpu.PrefetchScalarGridSpec(
            num_scalar_prefetch=1,
            grid=(pairs,),
            in_specs=[
                rows, rows, spec_w, spec_o, table, table, spec_v,
                rows, rows, column, column, column, column, totals,
                *[pl.BlockSpec(memory_space=pl.ANY)] * len(ready),
            ],
            out_specs=[
                rows,
                rows,
                spec_w,
                spec_o,
                pl.BlockSpec((8, width), lambda p, s: (0, 0)),
            ],
            scratch_shapes=[
                pltpu.VMEM((SEQ_LEN, SEQ_LEN), F32),
                pltpu.VMEM((SEQ_LEN, LANES), BF16),
                pltpu.VMEM((LANES, SEQ_LEN), BF16),
                pltpu.VMEM((SEQ_LEN, width), F32),
                *[pltpu.VMEM((SEQ_LEN, LANES), F32)] * 3,
            ],
        ),
        out_shape=[
            shape((half, width), BF16),
            pltpu.HBM((half, width), BF16),
            shape((3, pairs * LANES, width), BF16),
            shape((pairs * LANES, width), BF16),
            shape((8, width), F32),
        ],
        compiler_params=pltpu.CompilerParams(vmem_limit_bytes=48 * 2**20),
        cost_estimate=lasting(COST_BACKWARD),
        name="attention_backward",
    )(
        scalars, own, other, weights, w_out, cosine, sine, valid, grad_own, grad_other, *saved, *ready
    )


def most_tiles(rows):
    return (2 * rows + EXP_FFN * (TILE - 1)) // TILE


def most_groups(tiles, experts):
    return (tiles + experts * (GROUP - 1)) // GROUP


def expert_plan(routes, valid, chunks):
    tokens = routes.shape[0]
    rows = tokens // chunks
    tiles = most_tiles(rows)
    numbers = jnp.arange(8, dtype=I32)[:, None]
    named = ((routes[:, 0][None, :] == numbers) | (routes[:, 1][None, :] == numbers)) & (
        valid[None, :] > 0
    )
    named = (named & (numbers < EXP_FFN)).reshape(8 * chunks, rows)
    before = (jnp.arange(rows)[:, None] < jnp.arange(rows)[None, :]).astype(BF16)
    place = dot(named.astype(BF16), before).astype(I32)
    place = jnp.where(named, place, -1).reshape(8, chunks, rows)
    count = jnp.sum(named.astype(I32), axis=1).reshape(8, chunks)[:EXP_FFN]
    number = (count + TILE - 1) // TILE
    number = jnp.where(jnp.arange(chunks)[None, :] == 0, jnp.maximum(number, 1), number)
    earlier = jnp.arange(EXP_FFN)[:, None] > jnp.arange(EXP_FFN)[None, :]
    first = jnp.sum(jnp.where(earlier[:, :, None], number[None], 0), axis=1)
    total = jnp.sum(number, axis=0)
    slot = jnp.arange(tiles, dtype=I32)
    expert = jnp.sum((first + number)[:, :, None] <= slot, axis=0)
    expert = jnp.minimum(expert, EXP_FFN - 1)
    pick = jnp.arange(EXP_FFN)[:, None, None] == expert[None]
    base = (slot - jnp.sum(jnp.where(pick, first[:, :, None], 0), axis=0)) * TILE
    meta = jnp.concatenate([expert, base, total[:, None], first.T, number.T], axis=1).astype(I32)
    return (place.transpose(1, 0, 2), meta.reshape(-1), number, first)


def expert_kernel(
    tiles, span, sources, meta, chunk, place, carry, routes, w_router, w_up_all, w_down_all, *refs
):
    taken = refs[: sum(map(len, sources))]
    part, feed, x_out, hidden_out, grad_out, both_out = refs[-18:-12]
    rows = feed.shape[0]
    width = feed.shape[1]
    table, hits, picked, back, total, hidden_rows, grad_rows, both_rows = refs[-12:-4]
    w_up, w_down, load_sems, save_sems = refs[-4:]
    hidden_width = w_down.shape[1]
    offset = chunk[0] * span
    number = meta[offset + 2 * tiles]
    groups = (number + GATHER - 1) // GATHER
    span_rows = GATHER * TILE

    def loads(expert):
        slot = lax.rem(expert, 2)
        return (
            pltpu.make_async_copy(w_up_all.at[expert], w_up.at[slot], load_sems.at[slot, 0]),
            pltpu.make_async_copy(w_down_all.at[expert], w_down.at[slot], load_sems.at[slot, 1]),
        )

    def saves(tile):
        source = pl.ds(pl.multiple_of(tile * TILE, TILE), TILE)
        goal = pl.ds(pl.multiple_of((chunk[0] * tiles + tile) * TILE, TILE), TILE)
        pairs = (
            (picked.at[source, pl.ds(0, width)], x_out),
            (hidden_rows.at[source], hidden_out),
            (grad_rows.at[source], grad_out),
            (both_rows.at[source], both_out),
        )
        return [
            pltpu.make_async_copy(ref, out.at[goal], save_sems.at[tile, k])
            for k, (ref, out) in enumerate(pairs)
        ]

    for copy in loads(0):
        copy.start()

    first = 0
    for option, group in enumerate(sources):
        refs_here = taken[first : first + len(group)]
        first += len(group)

        @pl.when(chunk[1] == option)
        def _(refs_here=refs_here, group=group):
            at = {"x": 0, "cot": 0}
            for ref, kind in zip(refs_here, group):
                columns = pl.ds(0 if kind == "x" else width + LANES, width)
                table[pl.ds(at[kind], ref.shape[0]), columns] = ref[...]
                at[kind] += ref.shape[0]

    logits = dot(table[:, :width], w_router[...]) + carry[0]
    lane = lax.broadcasted_iota(I32, logits.shape, 1)
    one, two = lane == routes[0, :, 0:1], lane == routes[0, :, 1:2]
    score_one = jnp.sum(jnp.where(one, logits, 0.0), axis=1, keepdims=True)
    score_two = jnp.sum(jnp.where(two, logits, 0.0), axis=1, keepdims=True)
    top = jnp.maximum(score_one, score_two)
    score_one, score_two = jnp.exp(score_one - top), jnp.exp(score_two - top)
    both = score_one + score_two
    gates = jnp.where(one, score_one / both, 0.0) + jnp.where(two, score_two / both, 0.0)
    high = gates.astype(BF16).astype(F32)
    low = gates - high
    table[:, width : width + LANES] = (high + pltpu.roll(low, LANES // 2, 1)).astype(BF16)
    total[...] = jnp.zeros_like(total)

    @pl.loop(0, groups)
    def _(group):
        for at in range(GATHER):
            tile = group * GATHER + at
            slot = jnp.minimum(tile, tiles - 1)
            base = jnp.where(tile < number, meta[offset + tiles + slot], rows)
            row = lax.broadcasted_iota(I32, (TILE, rows), 0) + base
            hit = place[0, pl.ds(meta[offset + slot], 1), :] == row
            goal = pl.ds(pl.multiple_of(tile * TILE, TILE), TILE)
            hits[goal, :] = jnp.where(hit, 1.0, 0.0).astype(BF16)

            @pl.when(tile >= number)
            def _():
                back[goal, :] = jnp.zeros((TILE, back.shape[1]), BF16)

        here = pl.ds(pl.multiple_of(group * span_rows, TILE), span_rows)
        picked[here, :] = dot(hits[here, :], table[...]).astype(BF16)

    @pl.loop(0, EXP_FFN)
    def _(expert):
        slot = lax.rem(expert, 2)
        for copy in loads(expert):
            copy.wait()

        @pl.when(expert + 1 < EXP_FFN)
        def _():
            for copy in loads(expert + 1):
                copy.start()

        start = meta[offset + 2 * tiles + 1 + expert]
        amount = meta[offset + 2 * tiles + 1 + EXP_FFN + expert]

        @pl.loop(start, start + amount)
        def _(tile):
            mine = pl.ds(pl.multiple_of(tile * TILE, TILE), TILE)
            inputs = picked[mine, :width]
            lane = lax.broadcasted_iota(I32, (TILE, LANES), 1)
            own = (lane == expert) | (lane == expert + LANES // 2)
            scale = jnp.sum(
                jnp.where(own, picked[mine, width : width + LANES].astype(F32), 0.0),
                axis=1,
                keepdims=True,
            )
            upstream = picked[mine, width + LANES :].astype(F32)
            both = dot(inputs, w_up[slot])
            gate, up = both[:, :hidden_width], both[:, hidden_width:]
            sigma = 1.0 / (1.0 + jnp.exp(-gate))
            active = gate * sigma
            hidden = (active * up).astype(BF16)
            outputs = dot(hidden, w_down[slot])
            gate_term = jnp.sum(upstream * outputs, axis=1, keepdims=True)
            grad_row = (upstream * scale).astype(BF16)
            grad_hidden = dot_nt(grad_row, w_down[slot])
            grad_gate = (grad_hidden * up * sigma * (1.0 + gate * (1.0 - sigma))).astype(BF16)
            grad_up = (grad_hidden * active).astype(BF16)
            grad_both = jnp.concatenate([grad_gate, grad_up], axis=1)
            grad_x = dot_nt(grad_both, w_up[slot])
            hidden_rows[mine, :] = hidden
            grad_rows[mine, :] = grad_row
            both_rows[mine, :] = grad_both
            for copy in saves(tile):
                copy.start()
            back[mine, :width] = (outputs * scale).astype(BF16)
            back[mine, width : 2 * width] = grad_x.astype(BF16)
            back[mine, 2 * width :] = jnp.where(lane == expert, gate_term, 0.0).astype(BF16)

    @pl.loop(0, groups)
    def _(group):
        here = pl.ds(pl.multiple_of(group * span_rows, TILE), span_rows)
        total[...] += dot_tn(hits[here, :], back[here, :])

    feed[...] = total[:, :width].astype(BF16)
    part[:rows, :] = total[:, width : 2 * width].astype(BF16)
    terms = total[:, 2 * width :].T[:16]
    part[rows:, :] = jnp.concatenate([terms, jnp.zeros((16, width - rows), F32)], axis=1).astype(
        BF16
    )

    @pl.loop(0, number)
    def _(tile):
        for copy in saves(tile):
            copy.wait()


def expert_chunk(meta, chunk, options, place, carry, routes, w_router, w_up, w_down, saved):
    rows, width = options[0]["x"][0].shape
    sources = [[kind for kind in ("x", "cot") for _ in option[kind]] for option in options]
    taken = [ref for option in options for kind in ("x", "cot") for ref in option[kind]]
    chunks = place.shape[0]
    hidden_width = w_down.shape[1]
    tiles = most_tiles(rows)
    span = 2 * tiles + 1 + 2 * EXP_FFN
    held = (tiles + GATHER - 1) // GATHER * GATHER * TILE
    shape = jax.ShapeDtypeStruct
    whole = lambda *dims: pl.BlockSpec(dims, lambda i, m, c: (0,) * len(dims))
    mine = lambda *dims: pl.BlockSpec((1, *dims), lambda i, m, c: (c[0], 0, 0))
    stay = pl.BlockSpec(memory_space=pl.ANY)
    columns = (width, hidden_width, width, 2 * hidden_width)
    extra = () if saved is None else tuple(saved)
    return pl.pallas_call(
        functools.partial(expert_kernel, tiles, span, sources),
        grid_spec=pltpu.PrefetchScalarGridSpec(
            num_scalar_prefetch=2,
            grid=(1,),
            in_specs=[
                mine(8, rows),
                mine(rows, LANES),
                mine(rows, 2),
                whole(width, LANES),
                stay,
                stay,
                *[whole(*ref.shape) for ref in taken],
                *[stay] * len(extra),
            ],
            out_specs=[whole(rows + 16, width), whole(rows, width), *[stay] * len(columns)],
            scratch_shapes=[
                pltpu.VMEM((rows, 2 * width + LANES), BF16),
                pltpu.VMEM((held, rows), BF16),
                pltpu.VMEM((held, 2 * width + LANES), BF16),
                pltpu.VMEM((held, 2 * width + LANES), BF16),
                pltpu.VMEM((rows, 2 * width + LANES), F32),
                *[pltpu.VMEM((held, c), BF16) for c in columns[1:]],
                pltpu.VMEM((2, width, 2 * hidden_width), BF16),
                pltpu.VMEM((2, hidden_width, width), BF16),
                pltpu.SemaphoreType.DMA((2, 2)),
                pltpu.SemaphoreType.DMA((tiles, len(columns))),
            ],
        ),
        out_shape=[
            pltpu.HBM((rows + 16, width), BF16),
            pltpu.HBM((rows, width), BF16),
            *[shape((chunks * tiles * TILE, c), BF16) for c in columns],
        ],
        input_output_aliases={8 + len(taken) + k: 2 + k for k in range(len(extra))},
        compiler_params=pltpu.CompilerParams(vmem_limit_bytes=52 * 2**20),
        cost_estimate=lasting(COST_EXPERT),
        name="expert_chunk",
    )(meta, chunk, place, carry, routes, w_router, w_up, w_down, *taken, *extra)


def grad_walk(number, first, tiles, half):
    experts, chunks = number.shape[0] // 2, number.shape[1]
    number = lax.dynamic_slice_in_dim(number, half * experts, experts, 0)
    first = lax.dynamic_slice_in_dim(first, half * experts, experts, 0)
    flat = number.reshape(-1)
    groups = flat.shape[0]
    earlier = jnp.arange(groups)[:, None] > jnp.arange(groups)[None, :]
    start = jnp.sum(jnp.where(earlier, flat[None, :], 0), axis=1)
    held = jnp.sum(number, axis=1)
    held_groups = (held + GROUP - 1) // GROUP
    earlier = jnp.arange(experts)[:, None] > jnp.arange(experts)[None, :]
    held_start = jnp.sum(jnp.where(earlier, held[None, :], 0), axis=1)
    group_start = jnp.sum(jnp.where(earlier, held_groups[None, :], 0), axis=1)
    steps = most_groups(chunks * tiles, experts)
    everything = jnp.sum(held_groups)
    step = jnp.minimum(jnp.arange(steps, dtype=I32), everything - 1)
    owner = jnp.sum((group_start + held_groups)[:, None] <= step[None, :], axis=0)
    pick = jnp.arange(experts)[:, None] == owner[None, :]
    look = lambda values: jnp.sum(jnp.where(pick, values[:, None], 0), axis=0)
    done = (step - look(group_start)) * GROUP
    left = look(held) - done
    place_in = done[:, None] + jnp.minimum(jnp.arange(GROUP)[None, :], left[:, None] - 1)
    spot = (look(held_start)[:, None] + place_in).reshape(-1)
    group = jnp.sum((start + flat)[:, None] <= spot[None, :], axis=0)
    pick = jnp.arange(groups)[:, None] == group[None, :]
    offset = jnp.arange(chunks)[None, :] * tiles + first
    block = jnp.sum(jnp.where(pick, (offset.reshape(-1) - start)[:, None], 0), axis=0) + spot
    return jnp.concatenate([owner, block, left, everything[None]]).astype(I32)


def weight_grad_kernel(steps, walk, *refs):
    kept, (grad_up, grad_down) = refs[:4], refs[4:6]
    rows, (sum_up, sum_down, out_up, out_down, load_sems, save_sems) = refs[6:10], refs[10:]
    number = walk[(2 + GROUP) * steps]
    width, hidden_width = sum_up.shape[0], sum_down.shape[0]

    def loads(step):
        slot = lax.rem(step, 2)
        copies = []
        for at in range(GROUP):
            block = walk[steps + step * GROUP + at]
            source = pl.ds(pl.multiple_of(block * TILE, TILE), TILE)
            for kind in range(4):
                copies.append(
                    pltpu.make_async_copy(
                        kept[kind].at[source],
                        rows[kind].at[slot, pl.ds(at * TILE, TILE)],
                        load_sems.at[slot, at, kind],
                    )
                )
        return copies

    def saves(expert):
        slot = lax.rem(expert, 2)
        up_rows = pl.ds(pl.multiple_of(expert * width, width), width)
        down_rows = pl.ds(pl.multiple_of(expert * hidden_width, hidden_width), hidden_width)
        return (
            pltpu.make_async_copy(out_up.at[slot], grad_up.at[up_rows], save_sems.at[slot, 0]),
            pltpu.make_async_copy(out_down.at[slot], grad_down.at[down_rows], save_sems.at[slot, 1]),
        )

    for copy in loads(0):
        copy.start()

    @pl.loop(0, number)
    def _(step):
        slot = lax.rem(step, 2)
        expert = walk[step]
        left = walk[(1 + GROUP) * steps + step]
        for copy in loads(step):
            copy.wait()

        @pl.when(step + 1 < number)
        def _():
            for copy in loads(step + 1):
                copy.start()

        row = lax.broadcasted_iota(I32, (GROUP * TILE, 1), 0)
        live = row < left * TILE
        side = lax.rem(expert, 2)

        def products():
            return (
                dot_tn(jnp.where(live, rows[0][slot], 0), rows[3][slot]),
                dot_tn(jnp.where(live, rows[1][slot], 0), rows[2][slot]),
            )

        fresh = (step == 0) | (walk[jnp.maximum(step - 1, 0)] != expert)
        done = (step == number - 1) | (walk[jnp.minimum(step + 1, steps - 1)] != expert)

        @pl.when(done & (expert >= 2))
        def _():
            for copy in saves(expert - 2):
                copy.wait()

        @pl.when(fresh & done)
        def _():
            up, down = products()
            out_up[side], out_down[side] = up.astype(BF16), down.astype(BF16)

        @pl.when(fresh & jnp.logical_not(done))
        def _():
            sum_up[...], sum_down[...] = products()

        @pl.when(jnp.logical_not(fresh | done))
        def _():
            up, down = products()
            sum_up[...] += up
            sum_down[...] += down

        @pl.when(jnp.logical_not(fresh) & done)
        def _():
            up, down = products()
            out_up[side] = (sum_up[...] + up).astype(BF16)
            out_down[side] = (sum_down[...] + down).astype(BF16)

        @pl.when(done)
        def _():
            for copy in saves(expert):
                copy.start()

    for expert in (EXP_FFN // 2 - 2, EXP_FFN // 2 - 1):
        for copy in saves(expert):
            copy.wait()


def weight_grads(walk, saved):
    width, hidden_width = saved[0].shape[1], saved[1].shape[1]
    experts = EXP_FFN // 2
    steps = most_groups(saved[0].shape[0] // TILE, experts)
    shape = jax.ShapeDtypeStruct
    stay = pl.BlockSpec(memory_space=pl.ANY)
    return pl.pallas_call(
        functools.partial(weight_grad_kernel, steps),
        grid_spec=pltpu.PrefetchScalarGridSpec(
            num_scalar_prefetch=1,
            grid=(1,),
            in_specs=[stay] * 4,
            out_specs=[stay] * 2,
            scratch_shapes=[
                *[pltpu.VMEM((2, GROUP * TILE, kept.shape[1]), BF16) for kept in saved],
                pltpu.VMEM((width, 2 * hidden_width), F32),
                pltpu.VMEM((hidden_width, width), F32),
                pltpu.VMEM((2, width, 2 * hidden_width), BF16),
                pltpu.VMEM((2, hidden_width, width), BF16),
                pltpu.SemaphoreType.DMA((2, GROUP, 4)),
                pltpu.SemaphoreType.DMA((2, 2)),
            ],
        ),
        out_shape=[
            shape((experts * width, 2 * hidden_width), BF16),
            shape((experts * hidden_width, width), BF16),
        ],
        compiler_params=pltpu.CompilerParams(vmem_limit_bytes=48 * 2**20),
        cost_estimate=lasting(COST_GRADS),
        name="weight_grads",
    )(walk, *saved)


def combine_kernel(scalars, own_send, far_send, own_keep, far_keep, *refs):
    send, keep = refs[-2:]
    send[...] = own_send[...] + far_send[...]
    keep[...] = own_keep[...] + far_keep[...]


def combine(own, far, bit, start, rows, ready):
    columns = own.shape[1]
    half = rows // 2
    block = min(half, 384)
    number = half // block
    place = lambda side: pl.BlockSpec(
        (block, columns), lambda i, b: (start // block + (b[0] if side else 1 - b[0]) * number + i, 0)
    )
    out = pl.BlockSpec((block, columns), lambda i, b: (i, 0))
    shape = jax.ShapeDtypeStruct((half, columns), own.dtype)
    return pl.pallas_call(
        combine_kernel,
        grid_spec=pltpu.PrefetchScalarGridSpec(
            num_scalar_prefetch=1,
            grid=(number,),
            in_specs=[place(False), place(False), place(True), place(True)]
            + [pl.BlockSpec(memory_space=pl.ANY)] * len(ready),
            out_specs=[out, out],
        ),
        out_shape=[shape, shape],
        compiler_params=pltpu.CompilerParams(vmem_limit_bytes=32 * 2**20),
        cost_estimate=lasting(COST_ADD),
        name="combine",
    )(bit, own, far, own, far, *ready)


def widen_kernel(source, *refs):
    refs[-1][...] = source[...].astype(F32)


def widen(source, half, target):
    rows, columns = source.shape
    block = 768
    number = rows // block
    extra = () if target is None else (target,)
    return pl.pallas_call(
        widen_kernel,
        grid=(number,),
        in_specs=[pl.BlockSpec((block, columns), lambda i: (i, 0))]
        + [pl.BlockSpec(memory_space=pl.ANY)] * len(extra),
        out_specs=pl.BlockSpec((block, columns), lambda i: (half * number + i, 0)),
        out_shape=jax.ShapeDtypeStruct((2 * rows, columns), F32),
        input_output_aliases={1: 0} if extra else {},
        compiler_params=pltpu.CompilerParams(vmem_limit_bytes=48 * 2**20),
        cost_estimate=lasting(COST_WIDEN),
        name="widen",
    )(source, *extra)


def widen_pairs_kernel(source, *refs):
    target = refs[-1]
    rows, columns = source.shape
    for row in range(columns // LANES):
        at = row % 2 * (columns // 2) + row // 2 * LANES
        target[pl.ds(row, rows, stride=columns // LANES), :] = source[:, at : at + LANES].astype(F32)


def widen_pairs(source, half, target):
    rows, columns = source.shape
    block = 768
    number = rows // block
    extra = () if target is None else (target,)
    split = columns // LANES
    return pl.pallas_call(
        widen_pairs_kernel,
        grid=(number,),
        in_specs=[pl.BlockSpec((block, columns), lambda i: (i, 0))]
        + [pl.BlockSpec(memory_space=pl.ANY)] * len(extra),
        out_specs=pl.BlockSpec((block * split, LANES), lambda i: (half * number + i, 0)),
        out_shape=jax.ShapeDtypeStruct((2 * rows * split, LANES), F32),
        input_output_aliases={1: 0} if extra else {},
        compiler_params=pltpu.CompilerParams(vmem_limit_bytes=48 * 2**20),
        cost_estimate=lasting(COST_WIDEN),
        name="widen_pairs",
    )(source, *extra)


def shards(
    dp_size,
    stream,
    cotangent,
    gain_attention,
    w_inputs,
    w_output,
    gain_experts,
    w_router,
    w_carry,
    w_gate_up,
    w_down,
    w_constant,
    constant_vectors,
    previous_logits,
    routes,
    valid,
    prefix,
):
    rows, width = stream.shape
    tokens = routes.shape[0]
    chunks = tokens // rows
    head_columns = w_inputs.shape[2]
    here = lax.axis_index("tensor")
    index = lax.axis_index("dp")
    outer = (here == 0) | (here == chunks - 1)
    bits = list(range(dp_size.bit_length() - 1))
    first_row = here * rows
    valid_all = valid.astype(F32)
    cut = lambda array, at: lax.dynamic_slice_in_dim(array, at, rows, 0)
    valid_here = cut(valid_all, first_row)
    routes_here = cut(routes, first_row)
    previous_here = cut(previous_logits, first_row)

    w_in_rows = w_inputs.transpose(0, 2, 1)
    packed = jnp.concatenate([w_in_rows, w_output[None]], axis=0).reshape(-1, width)
    piece_rows = packed.shape[0] // dp_size
    position = (index >> 1) | ((index & 1) << (len(bits) - 1))
    piece = lax.dynamic_slice_in_dim(packed, position * piece_rows, piece_rows, 0)
    normed_here, inverse_one = norm_forward(stream, gain_attention)
    normed_low = normed_here.astype(BF16)
    normed_other = along_z(normed_low, SIDE)
    piece = along_z(piece, CROSS)
    cot_low = behind(cotangent, piece).astype(BF16)
    cot_side, cot_middle = along_z(cot_low, SIDE), along_z(cot_low, MIDDLE)
    for level, bit in enumerate([*bits[1:], bits[0]]):
        if level == 0:
            place, meta, number, first = expert_plan(*behind((routes, valid), piece), chunks)
        if level == 1:
            number, first = behind((number, first), piece)
            walks = [grad_walk(number, first, most_tiles(rows), half) for half in range(2)]
        other = along_dp(piece, bit, dp_size)
        piece = jnp.where(
            (index >> bit) & 1 == 0,
            jnp.concatenate([piece, other], axis=0),
            jnp.concatenate([other, piece], axis=0),
        )
    carry = jnp.dot(behind(previous_logits, place), w_carry, precision=HIGHEST, preferred_element_type=F32)
    columns = carry.shape[1]
    carry_wide = jnp.pad(carry, ((0, 0), (0, LANES - columns))).reshape(chunks, rows, LANES)
    routes_live = jnp.where(valid[:, None] > 0, routes, -1).reshape(chunks, rows, 2)
    router_wide = jnp.pad(w_router, ((0, 0), (0, LANES - columns)))
    partner = piece.reshape(4, head_columns, width)
    both_in = jnp.concatenate([w_in_rows, partner[:3]], axis=1)
    both_out = jnp.concatenate([w_output, partner[3]], axis=0)

    core = index & 1
    offset = (here % 2) * rows
    sequence = here // 2
    scalars = jnp.stack([offset, prefix[sequence]]).astype(I32)
    cosine, sine = rope_tables(offset)
    valid_rows = jnp.concatenate([cut(valid, first_row), cut(valid, (here ^ 1) * rows)])[:, None]
    fixed = (both_in, both_out, cosine, sine, valid_rows)
    ready = (place, meta, *walks, cot_side, cot_middle, carry_wide, routes_live, router_wide)
    part_own, part_other, *saved_attention = attention_forward(
        scalars, normed_low, normed_other, *fixed, ready
    )
    attention_other = along_z(part_other, SIDE)

    cot_far, cot_across = along_z(cot_middle, OUTWARD), along_z(cot_side, MIDDLE)
    cot_far, cot_across = behind((cot_far, cot_across), part_own)
    w_up = behind(w_gate_up, (part_own, cot_far, cot_across)).reshape(EXP_FFN, width, -1)
    attention_other = behind(attention_other, w_up)
    attention = part_own.astype(F32) + attention_other.astype(F32)
    middle = stream + attention
    second, inverse_two = norm_forward(middle, gain_experts)
    second_low = second.astype(BF16)

    which = slot_chunks(here)

    def chunk(slot, options, saved):
        choice = outer.astype(I32) * (len(options) - 1)
        return expert_chunk(
            meta,
            jnp.stack([which[slot], choice]),
            options,
            place,
            carry_wide,
            routes_live,
            router_wide,
            w_up,
            w_down,
            saved,
        )

    third_rows = rows // 3 // 16 * 16
    cuts = (0, third_rows, 2 * third_rows, rows)
    cot_pieces = [cot_across[low:high] for low, high in zip(cuts[:-1], cuts[1:])]
    side, middle_rows = along_z(second_low, SIDE), along_z(second_low, MIDDLE)
    cot_last = [along_z(behind(cot_pieces[0], second_low), OUTWARD)]
    part_0, feed_0, *saved = chunk(0, [{"x": [second_low], "cot": [cot_low]}], None)
    side, middle_rows, cot_last[0] = behind((side, middle_rows, cot_last[0]), part_0)
    far, across = along_z(middle_rows, OUTWARD), along_z(side, MIDDLE)
    cot_last.append(along_z(behind(cot_pieces[1], part_0), OUTWARD))
    part_1, feed_1, *saved = chunk(1, [{"x": [side], "cot": [cot_side]}], saved)
    near = along_z(part_1, INWARD)
    far, across, cot_last[1] = behind((far, across, cot_last[1]), part_1)
    last = along_z(across, OUTWARD)
    cot_last.append(along_z(behind(cot_pieces[2], part_1), OUTWARD))
    part_2, feed_2, *saved = chunk(
        2, [{"x": [middle_rows], "cot": [cot_middle]}, {"x": [far], "cot": [cot_far]}], saved
    )
    third = along_z(part_2, INWARD)
    last, cot_last[2] = behind((last, cot_last[2]), part_2)
    part_3, feed_3, *saved = chunk(
        3,
        [{"x": [across], "cot": [cot_across]}, {"x": [last], "cot": cot_last}],
        saved,
    )

    inward = along_z(part_3, INWARD)
    up_low, down_low = weight_grads(walks[0], saved)
    inward = part_3 + behind(inward, up_low)
    inward = along_z(inward, MIDDLE)
    third = along_z(part_2 + third, MIDDLE)
    up_high, down_high = weight_grads(walks[1], saved)
    outward_sum = part_1 + behind(inward, up_high)
    outward = along_z(outward_sum, OUTWARD)
    up_low, up_high, down_low, down_high = lax.psum((up_low, up_high, down_low, down_high), "dp")
    summed = part_0.astype(F32) + near.astype(F32) + third.astype(F32) + outward.astype(F32)

    logits = dot(second_low, w_router) + cut(carry, first_row)
    picked = routes_here[:, :, None] == jnp.arange(columns, dtype=I32)[None, None, :]
    chosen = jnp.sum(jnp.where(picked, logits[:, None, :], 0.0), axis=-1)
    gates_here = jax.nn.softmax(chosen, axis=-1)
    live_gates = gates_here * valid_here[:, None]
    copy_gate = jnp.sum(jnp.where(routes_here == EXP_FFN + 1, live_gates, 0.0), axis=-1)
    constant_gates = jnp.stack(
        [
            jnp.sum(jnp.where(routes_here == EXP_FFN + 2 + number, live_gates, 0.0), axis=-1)
            for number in range(2)
        ],
        axis=1,
    )
    alphas = jax.nn.softmax(
        jnp.einsum("td,cad->tca", second, w_constant, precision=HIGHEST, preferred_element_type=F32),
        axis=-1,
    )
    constant_out = (
        alphas[:, :, 0:1] * second[:, None, :] + alphas[:, :, 1:2] * constant_vectors[None, :, :]
    )
    extra = copy_gate[:, None] * second + jnp.sum(
        constant_gates[:, :, None] * constant_out, axis=1
    )
    copy_terms = jnp.sum(cotangent * second, axis=-1)
    constant_terms = jnp.sum(cotangent[:, None, :] * constant_out, axis=-1)
    grad_constant_out = constant_gates[:, :, None] * cotangent[:, None, :]
    grad_vectors = jnp.sum(alphas[:, :, 1:2] * grad_constant_out, axis=0)
    grad_alphas = jnp.stack(
        [
            jnp.sum(grad_constant_out * second[:, None, :], axis=-1),
            jnp.sum(grad_constant_out * constant_vectors[None, :, :], axis=-1),
        ],
        axis=-1,
    )
    grad_mix = alphas * (grad_alphas - jnp.sum(alphas * grad_alphas, axis=-1, keepdims=True))
    grad_constant = jnp.einsum(
        "tca,td->cad", grad_mix, second, precision=HIGHEST, preferred_element_type=F32
    )
    grad_local = (
        copy_gate[:, None] * cotangent
        + jnp.sum(alphas[:, :, 0:1] * grad_constant_out, axis=1)
        + jnp.einsum(
            "tca,cad->td", grad_mix, w_constant, precision=HIGHEST, preferred_element_type=F32
        )
    )

    gate_grads = summed[rows : rows + EXP_FFN, :rows].T
    gate_table = jnp.concatenate(
        [gate_grads, jnp.zeros((rows, 1), F32), copy_terms[:, None], constant_terms], axis=1
    )
    grad_gates = jnp.sum(jnp.where(picked, gate_table[:, None, :], 0.0), axis=-1)
    grad_gates = grad_gates * valid_here[:, None]
    grad_chosen = gates_here * (
        grad_gates - jnp.sum(gates_here * grad_gates, axis=-1, keepdims=True)
    )
    grad_logits = jnp.sum(jnp.where(picked, grad_chosen[:, :, None], 0.0), axis=1)
    grad_router = jnp.dot(
        second_low.astype(F32).T, grad_logits, precision=HIGHEST, preferred_element_type=F32
    )
    grad_carry = jnp.dot(
        previous_here.T, grad_logits, precision=HIGHEST, preferred_element_type=F32
    )
    grad_previous = jnp.dot(
        grad_logits, w_carry.T, precision=HIGHEST, preferred_element_type=F32
    )
    grad_second = (
        summed[:rows]
        + grad_local
        + jnp.dot(
            grad_logits, w_router.astype(F32).T, precision=HIGHEST, preferred_element_type=F32
        )
    )
    grad_gain_experts = jnp.sum(grad_second * middle * inverse_two, axis=0)
    grad_middle = cotangent + norm_backward(middle, inverse_two, gain_experts, grad_second)

    grad_low = grad_middle.astype(BF16)
    grad_other = along_z(grad_low, SIDE)

    part_own, part_other, grad_w, grad_o, gain_rows = attention_backward(
        scalars, normed_low, normed_other, *fixed, grad_low, grad_other, saved_attention, ()
    )
    grad_normed = part_own.astype(F32) + along_z(part_other, SIDE).astype(F32)
    grad_stream = grad_middle + norm_backward(stream, inverse_one, gain_attention, grad_normed)

    feed_1, feed_2, feed_3 = behind((feed_1, feed_2, feed_3), grad_low)
    near = along_z(feed_1, INWARD)
    third = along_z(feed_2 + along_z(feed_2, INWARD), MIDDLE)
    outward = along_z(feed_3 + along_z(feed_3, INWARD), MIDDLE)
    outward = along_z(feed_1 + outward, OUTWARD)
    feed = feed_0.astype(F32) + near.astype(F32) + third.astype(F32) + outward.astype(F32)
    experts = feed + extra
    block_out = middle + experts
    squares = [
        jnp.sum(valid_here[:, None] * part * part) for part in (block_out, attention, experts)
    ]
    squares = jnp.stack([*squares, jnp.sum(valid_here)])

    grad_down = widen(down_high, 1, widen(down_low, 0, None))
    grad_down = grad_down.reshape(EXP_FFN, -1, width)
    grad_gate_up = widen_pairs(up_high, 1, widen_pairs(up_low, 0, None))
    tiles = up_low.shape[1] // (2 * LANES)
    grad_gate_up = grad_gate_up.reshape(EXP_FFN, width, tiles, 2, LANES).transpose(0, 1, 3, 2, 4)
    grad_gate_up = grad_gate_up.reshape(EXP_FFN, width, 2, -1)

    own_grads = jnp.concatenate([grad_w[:, :head_columns], grad_o[None, :head_columns]], axis=0)
    far_grads = jnp.concatenate([grad_w[:, head_columns:], grad_o[None, head_columns:]], axis=0)
    order = bits
    own_piece = reduce_blocks(own_grads.reshape(-1, width), order, index, dp_size)
    far_piece = reduce_blocks(far_grads.reshape(-1, width), order, index, dp_size)
    own_piece = own_piece + along_z(far_piece, CROSS)
    attention_grads = spread_blocks(own_piece, order, index, dp_size).astype(F32)
    attention_grads = attention_grads.reshape(4, head_columns, width)
    grad_inputs = attention_grads[:3].transpose(0, 2, 1)
    grad_output = attention_grads[3]

    wide = lambda array: jnp.pad(array, ((0, 0), (0, width - array.shape[1])))
    small = jnp.concatenate(
        [
            grad_gain_experts[None],
            grad_router.T,
            wide(grad_carry),
            grad_constant.reshape(-1, width),
            grad_vectors,
            wide(squares[None]),
            jnp.sum(gain_rows, axis=0, keepdims=True) / gain_attention[None],
        ],
        axis=0,
    )
    small = sum_everywhere(small, bits, dp_size)
    at = 1 + 2 * columns
    squares = small[at + 6, :3]
    counted = small[at + 6, 3]
    rms_values = jnp.sqrt(squares / (jnp.maximum(counted, 1.0) * width))
    return (
        block_out,
        grad_stream,
        small[at + 7],
        grad_inputs,
        grad_output,
        small[0],
        small[1 : 1 + columns].T,
        small[1 + columns : at, :columns],
        grad_gate_up,
        grad_down,
        small[at : at + 4].reshape(2, 2, width),
        small[at + 4 : at + 6],
        grad_previous,
        rms_values,
    )


def solution(mesh):
    return jax.shard_map(
        functools.partial(shards, mesh.shape["dp"]),
        mesh=mesh,
        in_specs=(
            P(("dp", "tensor"), None),
            P(("dp", "tensor"), None),
            P(),
            P(None, None, "tensor"),
            P("tensor", None),
            P(),
            P(),
            P(),
            P(None, None, None, "tensor"),
            P(None, "tensor", None),
            P(),
            P(),
            P("dp", None),
            P("dp", None),
            P("dp"),
            P("dp"),
        ),
        out_specs=(
            P(("dp", "tensor"), None),
            P(("dp", "tensor"), None),
            P(),
            P(None, None, "tensor"),
            P("tensor", None),
            P(),
            P(),
            P(),
            P(None, None, None, "tensor"),
            P(None, "tensor", None),
            P(),
            P(),
            P(("dp", "tensor"), None),
            P(),
        ),
        check_vma=False,
    )
```

profile of v0, /device:TPU:0, one launch (start us, length us, event | category | flops | bytes accessed | tf_op | source)
XLA Modules:
  0.0 514.0 jit_solution(5376113266744249940)
XLA Ops:
  9.4 4.0 collective-permute-start.1
  14.5 1.6 collective-permute-start
  17.6 1.9 fusion.18
  22.4 2.4 convert_element_type.114.refs_1_
  31.9 2.3 pad.16.clone
  41.2 3.5 collective-permute-done.3
  49.3 3.2 collective-permute-done.5.refs_4_.refs_1_
  53.4 1.7 maximum_select_fusion
  57.7 20.8 %attention_forward.1 = (bf16[512,768]{1,0:T(8,128)(2,1)S(1)}, bf16[512,768]{1,0:T(8,128)(2,1)}, bf16[1024,384]{1,0:T(8,128)(2,1)}, bf16[1024,384]{1,0:T(8,128)(2...) custom-call(s32[2]{0:T(128)S(1)} %pad_add_fusion.3.scalars, ...), custom_call_target="tpu_custom_call" | custom-call | bytes 60000000 | tf_op jit(solution)/shard_map/attention_forward/pallas_call | solution.py:216
  80.0 2.4 collective-permute-start.7
  84.2 16.0 %reshape.618.w_up_all = bf16[6,768,1024]{2,1,0:T(8,128)(2,1)} reshape(bf16[6,768,2,512]{3,2,1,0:T(2,128)(2,1)} %param.25) | data formatting | bytes 18874368 | tf_op jit(solution)/shard_map/reshape | solution.py:919
  100.3 2.1 multiply_reduce_fusion.6
  105.3 1.6 collective-permute-start.10
  113.8 18.9 %expert_chunk.4 = (bf16[528,768]{1,0:T(8,128)(2,1)}, bf16[512,768]{1,0:T(8,128)(2,1)}, bf16[6656,768]{1,0:T(8,128)(2,1)}, bf16[6656,512]{1,0:T(8,128)(2,1)}, bf1...) custom-call(s32[156]{0:T(256)S(1)} %reshape.613.refs_1_.meta, s32[2]{0:T(128)S(1)} %pad_add_fusion.2.chunk, ...), custom_call_target="tpu_custom_call" | custom-call | bytes 60000000 | tf_op jit(solution)/shard_map/expert_chunk/pallas_call | solution.py:555
  138.3 18.9 %expert_chunk.5 = (bf16[528,768]{1,0:T(8,128)(2,1)}, bf16[512,768]{1,0:T(8,128)(2,1)}, bf16[6656,768]{1,0:T(8,128)(2,1)}, bf16[6656,512]{1,0:T(8,128)(2,1)}, bf1...) custom-call(s32[156]{0:T(256)S(1)} %reshape.613.refs_1_.meta, ...), custom_call_target="tpu_custom_call", output_to_operand_aliasing={{2}: (10, {}), {3}: (11, {}), {4}: (12, {}), {5}: (13, {})} | custom-call | bytes 60000000 | tf_op jit(solution)/shard_map/expert_chunk/pallas_call | solution.py:555
  157.1 1.9 collective-permute-done.15.refs_4_
  161.0 1.7 slice.135
  166.3 19.4 %expert_chunk.6 = (bf16[528,768]{1,0:T(8,128)(2,1)}, bf16[512,768]{1,0:T(8,128)(2,1)}, bf16[6656,768]{1,0:T(8,128)(2,1)}, bf16[6656,512]{1,0:T(8,128)(2,1)}, bf1...) custom-call(s32[156]{0:T(256)S(1)} %reshape.613.refs_1_.meta, ...), custom_call_target="tpu_custom_call", output_to_operand_aliasing={{2}: (12, {}), {3}: (13, {}), {4}: (14, {}), {5}: (15, {})} | custom-call | bytes 60000000 | tf_op jit(solution)/shard_map/expert_chunk/pallas_call | solution.py:555
  187.1 19.6 %expert_chunk.7 = (bf16[528,768]{1,0:T(8,128)(2,1)}, bf16[512,768]{1,0:T(8,128)(2,1)}, bf16[6656,768]{1,0:T(8,128)(2,1)}, bf16[6656,512]{1,0:T(8,128)(2,1)}, bf1...) custom-call(s32[156]{0:T(256)S(1)} %reshape.613.refs_1_.meta, ...), custom_call_target="tpu_custom_call", output_to_operand_aliasing={{2}: (14, {}), {3}: (15, {}), {4}: (16, {}), {5}: (17, {})} | custom-call | bytes 60000000 | tf_op jit(solution)/shard_map/expert_chunk/pallas_call | solution.py:555
  206.7 5.7 %collective-permute-start.21 = (bf16[528,768]{1,0:T(8,128)(2,1)}, bf16[528,768]{1,0:T(8,128)(2,1)S(1)}, u32[]{:S(2)}, u32[]{:S(2)}) collective-permute-start(bf16[528,768]{1,0:T(8,128)(2,1)} %get-tuple-element.122), channel_id=1, source_target_pairs={{0,1},{3,2},{4,5},{7,6},{8,9},{11,10},{12,13},{15,14},{16,17},{19,... | collective-permute-start | bytes 2433032 | tf_op jit(solution)/shard_map/ppermute | solution.py:62
  215.7 2.2 collective-permute-start.19
  217.9 9.5 %weight_grads.2 = (bf16[2304,1024]{1,0:T(8,128)(2,1)}, bf16[1536,768]{1,0:T(8,128)(2,1)S(1)}) custom-call(s32[91]{0:T(128)S(1)} %pad_add_fusion.4.refs_2_.walk, bf16[6656,768]{1,0:T(8,128)(2,1)} %get-tuple-element.123.refs_0_, bf16[6656,512]{1,0:T(8,128)(2,1)} %get-tuple-element.124.refs_1_, bf16[6656,768]{1,0:T(8,128)(2,1)} %get-tuple-element.125.refs_2_, ...), custom_call_target="tpu_custom_call" | custom-call | bytes 33000000 | tf_op jit(solution)/shard_map/weight_grads/pallas_call | solution.py:728
  228.8 2.4 collective-permute-done.21
  234.0 6.2 %collective-permute-start.18 = (bf16[528,768]{1,0:T(8,128)(2,1)}, bf16[528,768]{1,0:T(8,128)(2,1)}, u32[]{:S(2)}, u32[]{:S(2)}) collective-permute-start(bf16[528,768]{1,0:T(8,128)(2,1)} %get-tuple-element.103), channel_id=1, source_target_pairs={{0,1},{3,2},{4,5},{7,6},{8,9},{11,10},{12,13},{15,14},{16,17},{19,... | collective-permute-start | bytes 2433032 | tf_op jit(solution)/shard_map/ppermute | solution.py:62
  240.2 9.5 %weight_grads.3 = (bf16[2304,1024]{1,0:T(8,128)(2,1)}, bf16[1536,768]{1,0:T(8,128)(2,1)S(1)}) custom-call(s32[91]{0:T(128)S(1)} %pad_add_fusion.5.refs_3_.walk, bf16[6656,768]{1,0:T(8,128)(2,1)} %get-tuple-element.123.refs_0_, bf16[6656,512]{1,0:T(8,128)(2,1)} %get-tuple-element.124.refs_1_, bf16[6656,768]{1,0:T(8,128)(2,1)} %get-tuple-element.125.refs_2_, ...), custom_call_target="tpu_custom_call" | custom-call | bytes 33000000 | tf_op jit(solution)/shard_map/weight_grads/pallas_call | solution.py:728
  249.7 3.4 add.465
  253.1 1.7 collective-permute-start.20
  254.8 2.2 add.468
  259.1 4.5 fusion.2
  263.7 9.3 %collective-permute-done.23 = bf16[528,768]{1,0:T(8,128)(2,1)} collective-permute-done((bf16[528,768]{1,0:T(8,128)(2,1)}, bf16[528,768]{1,0:T(8,128)(2,1)}, u32[]{:S(2)}, u32[]{:S(2)}) %collective-permute-start.23) | collective-permute-done | bytes 811040 | tf_op jit(solution)/shard_map/ppermute | solution.py:62
  273.0 2.4 convert_add_fusion
  276.9 2.4 multiply_reduce_fusion.2
  279.3 1.8 fusion.45
  281.2 2.3 fusion.9
  284.1 3.9 collective-permute-start.25
  289.6 9.9 %collective-permute-done.30.grad_other = bf16[512,768]{1,0:T(8,128)(2,1)} collective-permute-done((bf16[512,768]{1,0:T(8,128)(2,1)}, bf16[512,768]{1,0:T(8,128)(2,1)}, u32[]{:S(2)}, u32[]{:S(2)}) %collective-permute-start.30) | collective-permute-done | bytes 786464 | tf_op jit(solution)/shard_map/ppermute | solution.py:62
  300.5 32.0 %attention_backward.1 = (bf16[512,768]{1,0:T(8,128)(2,1)S(1)}, bf16[512,768]{1,0:T(8,128)(2,1)}, bf16[3,384,768]{2,1,0:T(8,128)(2,1)}, bf16[384,768]{1,0:T(8,128)(2,1)S(1)}, f32[8,768]{1,0:T(8,128)S(1)}) custom-call(s32[2]{0:T(128)S(1)} %pad_add_fusion.3.scalars, bf16[512,768]{1,0:T(8,128)(2,1)S(1)} %multiply_convert_fusion.own, ...), custom_call_target="tpu_custom_call" | custom-call | bytes 96000000 | tf_op jit(solution)/shard_map/attention_backward/pallas_call | solution.py:315
  332.6 1.8 fusion.51
  337.6 7.8 %collective-permute-start.24 = (bf16[512,768]{1,0:T(8,128)(2,1)}, bf16[512,768]{1,0:T(8,128)(2,1)}, u32[]{:S(2)}, u32[]{:S(2)}) collective-permute-start(bf16[512,768]{1,0:T(8,128)(2,1)} %get-tuple-element.131), channel_id=1, source_target_pairs={{0,1},{3,2},{4,5},{7,6},{8,9},{11,10},{12,13},{15,14},{16,17},{19,... | collective-permute-start | bytes 2359304 | tf_op jit(solution)/shard_map/ppermute | solution.py:62
  350.2 1.6 collective-permute-start.38
  351.8 2.2 add.481
  355.5 9.7 %collective-permute-done.41 = bf16[192,768]{1,0:T(8,128)(2,1)S(1)} collective-permute-done((bf16[192,768]{1,0:T(8,128)(2,1)S(1)}, bf16[192,768]{1,0:T(8,128)(2,1)S(1)}, u32[]{:S(2)}, u32[]{:S(2)}) %collective-permute-start.41) | collective-permute-done | bytes 294944 | tf_op jit(solution)/shard_map/ppermute | solution.py:66
  365.3 14.4 %collective-permute-start.42 = (bf16[96,768]{1,0:T(8,128)(2,1)S(1)}, bf16[96,768]{1,0:T(8,128)(2,1)S(1)}, u32[]{:S(2)}, u32[]{:S(2)}) collective-permute-start(bf16[96,768]{1,0:T(8,128)(2,1)S(1)} %constant_dynamic-slice_fusion), channel_id=1, source_target_pairs={{0,16},{4,20},{8,24},{12,28},{16,0},{20,4},{24,8},{28,12},{1,17},{... | collective-permute-start | bytes 442376 | tf_op jit(solution)/shard_map/ppermute | solution.py:66
  380.5 5.6 %collective-permute-start.39 = (bf16[96,768]{1,0:T(8,128)(2,1)S(1)}, bf16[96,768]{1,0:T(8,128)(2,1)S(1)}, u32[]{:S(2)}, u32[]{:S(2)}) collective-permute-start(bf16[96,768]{1,0:T(8,128)(2,1)S(1)} %constant_dynamic-slice_fusion.3), channel_id=1, source_target_pairs={{0,16},{4,20},{8,24},{12,28},{16,0},{20,4},{24,8},{28,12},{1,17},{... | collective-permute-start | bytes 442376 | tf_op jit(solution)/shard_map/ppermute | solution.py:66
  386.8 2.4 collective-permute-start.43
  392.8 3.6 collective-permute-done.43
  398.0 5.9 %fusion.5 = (f32[]{:T(128)}, f32[]{:T(128)}, f32[]{:T(128)}, f32[512,768]{1,0:T(8,128)}) fusion(f32[512]{0:T(512)S(1)} %convert_element_type.123, bf16[512,768]{1,0:T(8,128)(2,1)} %collective-permute-done.7, bf16[512,768]{1,0:T(8,128)(2,1)S(1)} %copy-done.8, f32[512,768]{1,0:T(8,128)} %copy-done.31, f32[512,768]{1,0:T(8,128)} %get-tuple-element.150, ...), kind=kLoop, calls=%fused_computation.17 | loop fusion | flops 9043965 | bytes 11014156 | tf_op jit(solution)/shard_map/reduce_sum | solution.py:1072
  404.0 2.7 maximum_bitcast_fusion
  406.7 3.3 concatenate.83
  411.1 8.2 %collective-permute-start.45 = (bf16[192,768]{1,0:T(8,128)(2,1)S(1)}, bf16[192,768]{1,0:T(8,128)(2,1)S(1)}, u32[]{:S(2)}, u32[]{:S(2)}) collective-permute-start(bf16[192,768]{1,0:T(8,128)(2,1)S(1)} %maximum_select_fusion.5), channel_id=1, source_target_pairs={{0,8},{4,12},{8,0},{12,4},{16,24},{20,28},{24,16},{28,20},{1,9},{5... | collective-permute-start | bytes 884744 | tf_op jit(solution)/shard_map/ppermute | solution.py:66
  419.6 2.0 multiply_reduce_fusion.3
  421.7 13.4 %collective-permute-done.33 = f32[29,768]{1,0:T(8,128)S(1)} collective-permute-done((f32[29,768]{1,0:T(8,128)S(1)}, f32[29,768]{1,0:T(8,128)S(1)}, u32[]{:S(2)}, u32[]{:S(2)}) %collective-permute-start.33) | collective-permute-done | bytes 89120 | tf_op jit(solution)/shard_map/ppermute | solution.py:66
  435.1 1.8 collective-permute-start.34
  436.9 5.3 %collective-permute-done.34 = f32[29,768]{1,0:T(8,128)S(1)} collective-permute-done((f32[29,768]{1,0:T(8,128)S(1)}, f32[29,768]{1,0:T(8,128)S(1)}, u32[]{:S(2)}, u32[]{:S(2)}) %collective-permute-start.34) | collective-permute-done | bytes 89120 | tf_op jit(solution)/shard_map/ppermute | solution.py:66
  442.5 4.3 collective-permute-done.35
  447.3 1.7 subtract_add_fusion
  449.0 4.0 collective-permute-done.36
  460.2 27.0 %all-reduce.7.cloned.1.call-done = (bf16[2304,1024]{1,0:T(8,128)(2,1)}, bf16[2304,1024]{1,0:T(8,128)(2,1)}, bf16[1536,768]{1,0:T(8,128)(2,1)}, bf16[1536,768]{1,0:T(8,128)(2,1)}) async-done(((bf16[2304,1024]{1,0:T(8,128)(2,1)}, bf16[2304,1024]{1,0:T(8,128)(2,1)}, bf16[1536,768]{1,0:T(8,128)(2,1)}, bf16[1536,768]{1,0:T(8,128)(2,1)}), (bf16[2304,1024]{1,0:T(8,128)(2,1)}, bf16[2304,1024]{1,0:T(8,128)(2,1)}, ...) | async-done | bytes 14155792 | tf_op jit(solution)/shard_map/psum | solution.py:976
  487.2 1.7 copy-done.15
  488.9 2.6 widen.2.refs_0_
  491.5 2.7 copy-done.1
  494.2 5.1 widen_pairs.2.refs_0_
  499.3 2.3 widen.3
  501.6 5.1 widen_pairs.3
  (403 shorter events, 92.8 us)
Async XLA Ops:
  7.2 23.0 %copy-start = (f32[2048,10]{0,1:T(8,128)S(1)}, f32[2048,10]{0,1:T(8,128)}, u32[]{:S(2)}) copy-start(f32[2048,10]{0,1:T(8,128)} %param.29) | copy-start | bytes 245764
  7.2 480.0 %all-reduce.7.cloned.1.call-start = ((), (), s32[]{:S(2)}) async-start(), calls=%async_computation | async-start | bytes 28311552 | tf_op jit(solution)/shard_map/psum | solution.py:976
  9.4 12.9 %collective-permute-start.1 = (bf16[96,768]{1,0:T(8,128)(2,1)}, bf16[96,768]{1,0:T(8,128)(2,1)}, u32[]{:S(2)}, u32[]{:S(2)}) collective-permute-start(bf16[96,768]{1,0:T(8,128)(2,1)} %constant_dynamic-slice_fusion.8), channel_id=1, source_target_pairs={{0,2},{1,3},{2,0},{3,1},{4,6},{5,7},{6,4},{7,5},{8,10},{9,11},{10,... | collective-permute-start | bytes 442376 | tf_op jit(solution)/shard_map/ppermute | solution.py:62
  14.5 43.1 %collective-permute-start = (bf16[512,768]{1,0:T(8,128)(2,1)S(1)}, bf16[512,768]{1,0:T(8,128)(2,1)}, u32[]{:S(2)}, u32[]{:S(2)}) collective-permute-start(bf16[512,768]{1,0:T(8,128)(2,1)S(1)} %multiply_convert_fusion.own), channel_id=1, source_target_pairs={{0,1},{1,0},{2,3},{3,2},{4,5},{5,4},{6,7},{7,6},{8,9},{9,8},{10,11... | collective-permute-start | bytes 2359304 | tf_op jit(solution)/shard_map/ppermute | solution.py:62
  20.8 36.9 %copy-start.2 = (s32[1024,1]{1,0:T(8,128)}, s32[1024,1]{1,0:T(8,128)S(1)}, u32[]{:S(2)}) copy-start(s32[1024,1]{1,0:T(8,128)S(1)} %copy.87.valid) | copy-start | bytes 12292
  24.8 27.7 %collective-permute-start.5 = (bf16[512,768]{1,0:T(8,128)(2,1)}, bf16[512,768]{1,0:T(8,128)(2,1)}, u32[]{:S(2)}, u32[]{:S(2)}) collective-permute-start(bf16[512,768]{1,0:T(8,128)(2,1)} %convert_element_type.114.refs_1_), channel_id=1, source_target_pairs={{0,1},{1,0},{2,3},{3,2},{4,5},{5,4},{6,7},{7,6},{8,9},{9,8},{10,11... | collective-permute-start | bytes 2359304 | tf_op jit(solution)/shard_map/ppermute | solution.py:62
  25.3 22.8 %collective-permute-start.6 = (bf16[512,768]{1,0:T(8,128)(2,1)}, bf16[512,768]{1,0:T(8,128)(2,1)}, u32[]{:S(2)}, u32[]{:S(2)}) collective-permute-start(bf16[512,768]{1,0:T(8,128)(2,1)} %convert_element_type.114.refs_1_), channel_id=1, source_target_pairs={{1,2},{2,1},{5,6},{6,5},{9,10},{10,9},{13,14},{14,13},{17,18},{18,... | collective-permute-start | bytes 2359304 | tf_op jit(solution)/shard_map/ppermute | solution.py:62
  28.6 29.0 %copy-start.9 = (s32[8,4,512]{2,0,1:T(8,128)}, s32[8,4,512]{2,0,1:T(8,128)S(1)}, u32[]{:S(2)}) copy-start(s32[8,4,512]{2,0,1:T(8,128)S(1)} %copy.96) | copy-start | bytes 196612
  28.7 5.5 %collective-permute-start.2 = (bf16[96,768]{1,0:T(8,128)(2,1)}, bf16[96,768]{1,0:T(8,128)(2,1)S(1)}, u32[]{:S(2)}, u32[]{:S(2)}) collective-permute-start(bf16[96,768]{1,0:T(8,128)(2,1)} %collective-permute-done.1), channel_id=1, source_target_pairs={{0,8},{4,12},{8,0},{12,4},{16,24},{20,28},{24,16},{28,20},{1,9},{5... | collective-permute-start | bytes 442376 | tf_op jit(solution)/shard_map/ppermute | solution.py:66
  36.9 7.8 %collective-permute-start.3 = (bf16[192,768]{1,0:T(8,128)(2,1)S(1)}, bf16[192,768]{1,0:T(8,128)(2,1)}, u32[]{:S(2)}, u32[]{:S(2)}) collective-permute-start(bf16[192,768]{1,0:T(8,128)(2,1)S(1)} %maximum_select_fusion.4), channel_id=1, source_target_pairs={{0,16},{4,20},{8,24},{12,28},{16,0},{20,4},{24,8},{28,12},{1,17},{... | collective-permute-start | bytes 884744 | tf_op jit(solution)/shard_map/ppermute | solution.py:66
  46.0 7.3 %collective-permute-start.4 = (bf16[384,768]{1,0:T(8,128)(2,1)S(1)}, bf16[384,768]{1,0:T(8,128)(2,1)}, u32[]{:S(2)}, u32[]{:S(2)}) collective-permute-start(bf16[384,768]{1,0:T(8,128)(2,1)S(1)} %maximum_select_fusion.2), channel_id=1, source_target_pairs={{0,4},{4,0},{8,12},{12,8},{16,20},{20,16},{24,28},{28,24},{1,5},{5... | collective-permute-start | bytes 1769480 | tf_op jit(solution)/shard_map/ppermute | solution.py:66
  48.1 34.3 %collective-permute-start.8 = (bf16[512,768]{1,0:T(8,128)(2,1)}, bf16[512,768]{1,0:T(8,128)(2,1)S(1)}, u32[]{:S(2)}, u32[]{:S(2)}) collective-permute-start(bf16[512,768]{1,0:T(8,128)(2,1)} %collective-permute-done.6.refs_5_.refs_1_), channel_id=1, source_target_pairs={{1,0},{2,3},{5,4},{6,7},{9,8},{10,11},{13,12},{14,15},{17,16},{18,... | collective-permute-start | bytes 2359304 | tf_op jit(solution)/shard_map/ppermute | solution.py:62
  52.5 29.9 %collective-permute-start.9 = (bf16[512,768]{1,0:T(8,128)(2,1)}, bf16[512,768]{1,0:T(8,128)(2,1)S(1)}, u32[]{:S(2)}, u32[]{:S(2)}) collective-permute-start(bf16[512,768]{1,0:T(8,128)(2,1)} %collective-permute-done.5.refs_4_.refs_1_), channel_id=1, source_target_pairs={{1,2},{2,1},{5,6},{6,5},{9,10},{10,9},{13,14},{14,13},{17,18},{18,... | collective-permute-start | bytes 2359304 | tf_op jit(solution)/shard_map/ppermute | solution.py:62
  80.0 20.4 %collective-permute-start.7 = (bf16[512,768]{1,0:T(8,128)(2,1)}, bf16[512,768]{1,0:T(8,128)(2,1)}, u32[]{:S(2)}, u32[]{:S(2)}) collective-permute-start(bf16[512,768]{1,0:T(8,128)(2,1)} %get-tuple-element.87), channel_id=1, source_target_pairs={{0,1},{1,0},{2,3},{3,2},{4,5},{5,4},{6,7},{7,6},{8,9},{9,8},{10,11... | collective-permute-start | bytes 2359304 | tf_op jit(solution)/shard_map/ppermute | solution.py:62
  105.3 28.1 %collective-permute-start.10 = (bf16[512,768]{1,0:T(8,128)(2,1)S(1)}, bf16[512,768]{1,0:T(8,128)(2,1)}, u32[]{:S(2)}, u32[]{:S(2)}) collective-permute-start(bf16[512,768]{1,0:T(8,128)(2,1)S(1)} %convert_element_type.117.refs_0_), channel_id=1, source_target_pairs={{0,1},{1,0},{2,3},{3,2},{4,5},{5,4},{6,7},{7,6},{8,9},{9,8},{10,11... | collective-permute-start | bytes 2359304 | tf_op jit(solution)/shard_map/ppermute | solution.py:62
  106.9 26.5 %collective-permute-start.11 = (bf16[512,768]{1,0:T(8,128)(2,1)S(1)}, bf16[512,768]{1,0:T(8,128)(2,1)}, u32[]{:S(2)}, u32[]{:S(2)}) collective-permute-start(bf16[512,768]{1,0:T(8,128)(2,1)S(1)} %convert_element_type.117.refs_0_), channel_id=1, source_target_pairs={{1,2},{2,1},{5,6},{6,5},{9,10},{10,9},{13,14},{14,13},{17,18},{18,... | collective-permute-start | bytes 2359304 | tf_op jit(solution)/shard_map/ppermute | solution.py:62
  109.6 23.1 %collective-permute-start.12 = (bf16[160,768]{1,0:T(8,128)(2,1)S(1)}, bf16[160,768]{1,0:T(8,128)(2,1)S(1)}, u32[]{:S(2)}, u32[]{:S(2)}) collective-permute-start(bf16[160,768]{1,0:T(8,128)(2,1)S(1)} %get-tuple-element.93), channel_id=1, source_target_pairs={{1,0},{2,3},{5,4},{6,7},{9,8},{10,11},{13,12},{14,15},{17,16},{18,... | collective-permute-start | bytes 737288 | tf_op jit(solution)/shard_map/ppermute | solution.py:62
  133.4 26.3 %collective-permute-start.13 = (bf16[512,768]{1,0:T(8,128)(2,1)}, bf16[512,768]{1,0:T(8,128)(2,1)}, u32[]{:S(2)}, u32[]{:S(2)}) collective-permute-start(bf16[512,768]{1,0:T(8,128)(2,1)} %collective-permute-done.11.refs_0_), channel_id=1, source_target_pairs={{1,0},{2,3},{5,4},{6,7},{9,8},{10,11},{13,12},{14,15},{17,16},{18,... | collective-permute-start | bytes 2359304 | tf_op jit(solution)/shard_map/ppermute | solution.py:62
  134.7 25.0 %collective-permute-start.14 = (bf16[512,768]{1,0:T(8,128)(2,1)}, bf16[512,768]{1,0:T(8,128)(2,1)}, u32[]{:S(2)}, u32[]{:S(2)}) collective-permute-start(bf16[512,768]{1,0:T(8,128)(2,1)} %collective-permute-done.10.refs_0_), channel_id=1, source_target_pairs={{1,2},{2,1},{5,6},{6,5},{9,10},{10,9},{13,14},{14,13},{17,18},{18,... | collective-permute-start | bytes 2359304 | tf_op jit(solution)/shard_map/ppermute | solution.py:62
  136.3 22.7 %collective-permute-start.15 = (bf16[160,768]{1,0:T(8,128)(2,1)S(1)}, bf16[160,768]{1,0:T(8,128)(2,1)S(1)}, u32[]{:S(2)}, u32[]{:S(2)}) collective-permute-start(bf16[160,768]{1,0:T(8,128)(2,1)S(1)} %get-tuple-element.102), channel_id=1, source_target_pairs={{1,0},{2,3},{5,4},{6,7},{9,8},{10,11},{13,12},{14,15},{17,16},{18,... | collective-permute-start | bytes 737288 | tf_op jit(solution)/shard_map/ppermute | solution.py:62
  159.7 27.3 %collective-permute-start.16 = (bf16[512,768]{1,0:T(8,128)(2,1)}, bf16[512,768]{1,0:T(8,128)(2,1)}, u32[]{:S(2)}, u32[]{:S(2)}) collective-permute-start(bf16[512,768]{1,0:T(8,128)(2,1)} %collective-permute-done.14.refs_0_), channel_id=1, source_target_pairs={{1,0},{2,3},{5,4},{6,7},{9,8},{10,11},{13,12},{14,15},{17,16},{18,... | collective-permute-start | bytes 2359304 | tf_op jit(solution)/shard_map/ppermute | solution.py:62
  162.7 24.3 %collective-permute-start.17 = (bf16[192,768]{1,0:T(8,128)(2,1)}, bf16[192,768]{1,0:T(8,128)(2,1)}, u32[]{:S(2)}, u32[]{:S(2)}) collective-permute-start(bf16[192,768]{1,0:T(8,128)(2,1)} %slice.135), channel_id=1, source_target_pairs={{1,0},{2,3},{5,4},{6,7},{9,8},{10,11},{13,12},{14,15},{17,16},{18,... | collective-permute-start | bytes 884744 | tf_op jit(solution)/shard_map/ppermute | solution.py:62
  187.0 25.4 %copy-start.65 = (s32[512]{0:T(512)S(1)}, s32[512]{0:T(512)}, u32[]{:S(2)}) copy-start(s32[512]{0:T(512)} %copy-done.64) | copy-start | bytes 6148
  187.0 26.1 %copy-start.47 = (bf16[768,10]{0,1:T(8,128)(2,1)S(1)}, bf16[768,10]{0,1:T(8,128)(2,1)}, u32[]{:S(2)}) copy-start(bf16[768,10]{0,1:T(8,128)(2,1)} %param.23) | copy-start | bytes 46084
  187.0 27.2 %copy-start.23 = (f32[512,768]{1,0:T(8,128)S(1)}, f32[512,768]{1,0:T(8,128)}, u32[]{:S(2)}) copy-start(f32[512,768]{1,0:T(8,128)} %copy-done.22) | copy-start | bytes 4718596
  187.1 27.2 %copy-start.55 = (f32[2,2,768]{2,1,0:T(2,128)S(1)}, f32[2,2,768]{2,1,0:T(2,128)}, u32[]{:S(2)}) copy-start(f32[2,2,768]{2,1,0:T(2,128)} %param.27) | copy-start | bytes 36868
  206.7 24.5 %collective-permute-start.21 = (bf16[528,768]{1,0:T(8,128)(2,1)}, bf16[528,768]{1,0:T(8,128)(2,1)S(1)}, u32[]{:S(2)}, u32[]{:S(2)}) collective-permute-start(bf16[528,768]{1,0:T(8,128)(2,1)} %get-tuple-element.122), channel_id=1, source_target_pairs={{0,1},{3,2},{4,5},{7,6},{8,9},{11,10},{12,13},{15,14},{16,17},{19,... | collective-permute-start | bytes 2433032 | tf_op jit(solution)/shard_map/ppermute | solution.py:62
  215.7 34.0 %collective-permute-start.19 = (bf16[528,768]{1,0:T(8,128)(2,1)}, bf16[528,768]{1,0:T(8,128)(2,1)}, u32[]{:S(2)}, u32[]{:S(2)}) collective-permute-start(bf16[528,768]{1,0:T(8,128)(2,1)} %get-tuple-element.112), channel_id=1, source_target_pairs={{0,1},{3,2},{4,5},{7,6},{8,9},{11,10},{12,13},{15,14},{16,17},{19,... | collective-permute-start | bytes 2433032 | tf_op jit(solution)/shard_map/ppermute | solution.py:62
  232.2 22.5 %collective-permute-start.22 = (bf16[528,768]{1,0:T(8,128)(2,1)}, bf16[528,768]{1,0:T(8,128)(2,1)}, u32[]{:S(2)}, u32[]{:S(2)}) collective-permute-start(bf16[528,768]{1,0:T(8,128)(2,1)} %add.467), channel_id=1, source_target_pairs={{1,2},{2,1},{5,6},{6,5},{9,10},{10,9},{13,14},{14,13},{17,18},{18,... | collective-permute-start | bytes 2433032 | tf_op jit(solution)/shard_map/ppermute | solution.py:62
  234.0 29.7 %collective-permute-start.18 = (bf16[528,768]{1,0:T(8,128)(2,1)}, bf16[528,768]{1,0:T(8,128)(2,1)}, u32[]{:S(2)}, u32[]{:S(2)}) collective-permute-start(bf16[528,768]{1,0:T(8,128)(2,1)} %get-tuple-element.103), channel_id=1, source_target_pairs={{0,1},{3,2},{4,5},{7,6},{8,9},{11,10},{12,13},{15,14},{16,17},{19,... | collective-permute-start | bytes 2433032 | tf_op jit(solution)/shard_map/ppermute | solution.py:62
  253.1 10.6 %collective-permute-start.20 = (bf16[528,768]{1,0:T(8,128)(2,1)}, bf16[528,768]{1,0:T(8,128)(2,1)}, u32[]{:S(2)}, u32[]{:S(2)}) collective-permute-start(bf16[528,768]{1,0:T(8,128)(2,1)} %add.465), channel_id=1, source_target_pairs={{1,2},{2,1},{5,6},{6,5},{9,10},{10,9},{13,14},{14,13},{17,18},{18,... | collective-permute-start | bytes 2433032 | tf_op jit(solution)/shard_map/ppermute | solution.py:62
  257.0 16.0 %collective-permute-start.23 = (bf16[528,768]{1,0:T(8,128)(2,1)}, bf16[528,768]{1,0:T(8,128)(2,1)}, u32[]{:S(2)}, u32[]{:S(2)}) collective-permute-start(bf16[528,768]{1,0:T(8,128)(2,1)} %add.468), channel_id=1, source_target_pairs={{1,0},{2,3},{5,4},{6,7},{9,8},{10,11},{13,12},{14,15},{17,16},{18,... | collective-permute-start | bytes 2433032 | tf_op jit(solution)/shard_map/ppermute | solution.py:62
  281.2 18.3 %collective-permute-start.30 = (bf16[512,768]{1,0:T(8,128)(2,1)}, bf16[512,768]{1,0:T(8,128)(2,1)}, u32[]{:S(2)}, u32[]{:S(2)}) collective-permute-start(bf16[512,768]{1,0:T(8,128)(2,1)} %get-tuple-element.179.grad_own), channel_id=1, source_target_pairs={{0,1},{1,0},{2,3},{3,2},{4,5},{5,4},{6,7},{7,6},{8,9},{9,8},{10,11... | collective-permute-start | bytes 2359304 | tf_op jit(solution)/shard_map/ppermute | solution.py:62
  284.1 62.5 %collective-permute-start.25 = (bf16[512,768]{1,0:T(8,128)(2,1)}, bf16[512,768]{1,0:T(8,128)(2,1)S(1)}, u32[]{:S(2)}, u32[]{:S(2)}) collective-permute-start(bf16[512,768]{1,0:T(8,128)(2,1)} %get-tuple-element.132), channel_id=1, source_target_pairs={{0,1},{3,2},{4,5},{7,6},{8,9},{11,10},{12,13},{15,14},{16,17},{19,... | collective-permute-start | bytes 2359304 | tf_op jit(solution)/shard_map/ppermute | solution.py:62
  288.0 47.8 %collective-permute-start.27 = (bf16[512,768]{1,0:T(8,128)(2,1)}, bf16[512,768]{1,0:T(8,128)(2,1)S(1)}, u32[]{:S(2)}, u32[]{:S(2)}) collective-permute-start(bf16[512,768]{1,0:T(8,128)(2,1)} %get-tuple-element.133), channel_id=1, source_target_pairs={{0,1},{3,2},{4,5},{7,6},{8,9},{11,10},{12,13},{15,14},{16,17},{19,... | collective-permute-start | bytes 2359304 | tf_op jit(solution)/shard_map/ppermute | solution.py:62
  334.7 14.6 %collective-permute-start.40 = (bf16[384,768]{1,0:T(8,128)(2,1)S(1)}, bf16[384,768]{1,0:T(8,128)(2,1)S(1)}, u32[]{:S(2)}, u32[]{:S(2)}) collective-permute-start(bf16[384,768]{1,0:T(8,128)(2,1)S(1)} %constant_dynamic-slice_fusion.2), channel_id=1, source_target_pairs={{0,4},{4,0},{8,12},{12,8},{16,20},{20,16},{24,28},{28,24},{1,5},{5... | collective-permute-start | bytes 1769480 | tf_op jit(solution)/shard_map/ppermute | solution.py:66
  336.0 15.8 %collective-permute-start.28 = (bf16[512,768]{1,0:T(8,128)(2,1)S(1)}, bf16[512,768]{1,0:T(8,128)(2,1)S(1)}, u32[]{:S(2)}, u32[]{:S(2)}) collective-permute-start(bf16[512,768]{1,0:T(8,128)(2,1)S(1)} %add.480), channel_id=1, source_target_pairs={{1,2},{2,1},{5,6},{6,5},{9,10},{10,9},{13,14},{14,13},{17,18},{18,... | collective-permute-start | bytes 2359304 | tf_op jit(solution)/shard_map/ppermute | solution.py:62
  336.9 13.1 %collective-permute-start.37 = (bf16[384,768]{1,0:T(8,128)(2,1)S(1)}, bf16[384,768]{1,0:T(8,128)(2,1)S(1)}, u32[]{:S(2)}, u32[]{:S(2)}) collective-permute-start(bf16[384,768]{1,0:T(8,128)(2,1)S(1)} %constant_dynamic-slice_fusion.5), channel_id=1, source_target_pairs={{0,4},{4,0},{8,12},{12,8},{16,20},{20,16},{24,28},{28,24},{1,5},{5... | collective-permute-start | bytes 1769480 | tf_op jit(solution)/shard_map/ppermute | solution.py:66
  337.6 60.4 %collective-permute-start.24 = (bf16[512,768]{1,0:T(8,128)(2,1)}, bf16[512,768]{1,0:T(8,128)(2,1)}, u32[]{:S(2)}, u32[]{:S(2)}) collective-permute-start(bf16[512,768]{1,0:T(8,128)(2,1)} %get-tuple-element.131), channel_id=1, source_target_pairs={{0,1},{3,2},{4,5},{7,6},{8,9},{11,10},{12,13},{15,14},{16,17},{19,... | collective-permute-start | bytes 2359304 | tf_op jit(solution)/shard_map/ppermute | solution.py:62
  347.7 50.3 %collective-permute-start.26 = (bf16[512,768]{1,0:T(8,128)(2,1)}, bf16[512,768]{1,0:T(8,128)(2,1)}, u32[]{:S(2)}, u32[]{:S(2)}) collective-permute-start(bf16[512,768]{1,0:T(8,128)(2,1)} %add.478), channel_id=1, source_target_pairs={{1,2},{2,1},{5,6},{6,5},{9,10},{10,9},{13,14},{14,13},{17,18},{18,... | collective-permute-start | bytes 2359304 | tf_op jit(solution)/shard_map/ppermute | solution.py:62
  349.5 15.8 %collective-permute-start.41 = (bf16[192,768]{1,0:T(8,128)(2,1)S(1)}, bf16[192,768]{1,0:T(8,128)(2,1)S(1)}, u32[]{:S(2)}, u32[]{:S(2)}) collective-permute-start(bf16[192,768]{1,0:T(8,128)(2,1)S(1)} %constant_dynamic-slice_fusion.1), channel_id=1, source_target_pairs={{0,8},{4,12},{8,0},{12,4},{16,24},{20,28},{24,16},{28,20},{1,9},{5... | collective-permute-start | bytes 884744 | tf_op jit(solution)/shard_map/ppermute | solution.py:66
  350.2 29.5 %collective-permute-start.38 = (bf16[192,768]{1,0:T(8,128)(2,1)S(1)}, bf16[192,768]{1,0:T(8,128)(2,1)S(1)}, u32[]{:S(2)}, u32[]{:S(2)}) collective-permute-start(bf16[192,768]{1,0:T(8,128)(2,1)S(1)} %constant_dynamic-slice_fusion.4), channel_id=1, source_target_pairs={{0,8},{4,12},{8,0},{12,4},{16,24},{20,28},{24,16},{28,20},{1,9},{5... | collective-permute-start | bytes 884744 | tf_op jit(solution)/shard_map/ppermute | solution.py:66
  354.0 35.2 %copy-start.61 = (f32[10,10]{1,0:T(8,128)S(1)}, f32[10,10]{1,0:T(8,128)}, u32[]{:S(2)}) copy-start(f32[10,10]{1,0:T(8,128)} %param.24) | copy-start | bytes 1204
  354.0 36.0 %copy-start.53 = (f32[768]{0:T(1024)S(1)}, f32[768]{0:T(1024)}, u32[]{:S(2)}) copy-start(f32[768]{0:T(1024)} %param.19) | copy-start | bytes 9220
  354.0 44.0 %copy-start.8 = (bf16[512,768]{1,0:T(8,128)(2,1)S(1)}, bf16[512,768]{1,0:T(8,128)(2,1)}, u32[]{:S(2)}) copy-start(bf16[512,768]{1,0:T(8,128)(2,1)} %copy-done.6) | copy-start | bytes 2359300
  354.0 44.0 %copy-start.25 = (f32[512,768]{1,0:T(8,128)S(1)}, f32[512,768]{1,0:T(8,128)}, u32[]{:S(2)}) copy-start(f32[512,768]{1,0:T(8,128)} %copy-done.22) | copy-start | bytes 4718596
  354.0 44.0 %copy-start.69 = (f32[512]{0:T(512)S(1)}, f32[512]{0:T(512)}, u32[]{:S(2)}) copy-start(f32[512]{0:T(512)} %copy-done.68) | copy-start | bytes 6148
  354.1 43.9 %collective-permute-start.29 = (bf16[512,768]{1,0:T(8,128)(2,1)}, bf16[512,768]{1,0:T(8,128)(2,1)}, u32[]{:S(2)}, u32[]{:S(2)}) collective-permute-start(bf16[512,768]{1,0:T(8,128)(2,1)} %add.481), channel_id=1, source_target_pairs={{1,0},{2,3},{5,4},{6,7},{9,8},{10,11},{13,12},{14,15},{17,16},{18,... | collective-permute-start | bytes 2359304 | tf_op jit(solution)/shard_map/ppermute | solution.py:62
  365.3 20.8 %collective-permute-start.42 = (bf16[96,768]{1,0:T(8,128)(2,1)S(1)}, bf16[96,768]{1,0:T(8,128)(2,1)S(1)}, u32[]{:S(2)}, u32[]{:S(2)}) collective-permute-start(bf16[96,768]{1,0:T(8,128)(2,1)S(1)} %constant_dynamic-slice_fusion), channel_id=1, source_target_pairs={{0,16},{4,20},{8,24},{12,28},{16,0},{20,4},{24,8},{28,12},{1,17},{... | collective-permute-start | bytes 442376 | tf_op jit(solution)/shard_map/ppermute | solution.py:66
  380.5 10.1 %collective-permute-start.39 = (bf16[96,768]{1,0:T(8,128)(2,1)S(1)}, bf16[96,768]{1,0:T(8,128)(2,1)S(1)}, u32[]{:S(2)}, u32[]{:S(2)}) collective-permute-start(bf16[96,768]{1,0:T(8,128)(2,1)S(1)} %constant_dynamic-slice_fusion.3), channel_id=1, source_target_pairs={{0,16},{4,20},{8,24},{12,28},{16,0},{20,4},{24,8},{28,12},{1,17},{... | collective-permute-start | bytes 442376 | tf_op jit(solution)/shard_map/ppermute | solution.py:66
  386.8 9.6 %collective-permute-start.43 = (bf16[96,768]{1,0:T(8,128)(2,1)}, bf16[96,768]{1,0:T(8,128)(2,1)}, u32[]{:S(2)}, u32[]{:S(2)}) collective-permute-start(bf16[96,768]{1,0:T(8,128)(2,1)} %dynamic-slice_add_fusion.4), channel_id=1, source_target_pairs={{0,2},{1,3},{2,0},{3,1},{4,6},{5,7},{6,4},{7,5},{8,10},{9,11},{10,... | collective-permute-start | bytes 442376 | tf_op jit(solution)/shard_map/ppermute | solution.py:62
  391.3 28.3 %collective-permute-start.31 = (bf16[512,768]{1,0:T(8,128)(2,1)}, bf16[512,768]{1,0:T(8,128)(2,1)S(1)}, u32[]{:S(2)}, u32[]{:S(2)}) collective-permute-start(bf16[512,768]{1,0:T(8,128)(2,1)} %get-tuple-element.140), channel_id=1, source_target_pairs={{0,1},{1,0},{2,3},{3,2},{4,5},{5,4},{6,7},{7,6},{8,9},{9,8},{10,11... | collective-permute-start | bytes 2359304 | tf_op jit(solution)/shard_map/ppermute | solution.py:62
  397.6 12.5 %collective-permute-start.44 = (bf16[96,768]{1,0:T(8,128)(2,1)S(1)}, bf16[96,768]{1,0:T(8,128)(2,1)}, u32[]{:S(2)}, u32[]{:S(2)}) collective-permute-start(bf16[96,768]{1,0:T(8,128)(2,1)S(1)} %add_add_fusion.1), channel_id=1, source_target_pairs={{0,16},{4,20},{8,24},{12,28},{16,0},{20,4},{24,8},{28,12},{1,17},{... | collective-permute-start | bytes 442376 | tf_op jit(solution)/shard_map/ppermute | solution.py:66
  410.0 9.4 %collective-permute-start.32 = (f32[29,768]{1,0:T(8,128)S(1)}, f32[29,768]{1,0:T(8,128)S(1)}, u32[]{:S(2)}, u32[]{:S(2)}) collective-permute-start(f32[29,768]{1,0:T(8,128)S(1)} %concatenate.83), channel_id=1, source_target_pairs={{0,4},{4,0},{8,12},{12,8},{16,20},{20,16},{24,28},{28,24},{1,5},{5... | collective-permute-start | bytes 267272 | tf_op jit(solution)/shard_map/ppermute | solution.py:66
  411.1 31.2 %collective-permute-start.45 = (bf16[192,768]{1,0:T(8,128)(2,1)S(1)}, bf16[192,768]{1,0:T(8,128)(2,1)S(1)}, u32[]{:S(2)}, u32[]{:S(2)}) collective-permute-start(bf16[192,768]{1,0:T(8,128)(2,1)S(1)} %maximum_select_fusion.5), channel_id=1, source_target_pairs={{0,8},{4,12},{8,0},{12,4},{16,24},{20,28},{24,16},{28,20},{1,9},{5... | collective-permute-start | bytes 884744 | tf_op jit(solution)/shard_map/ppermute | solution.py:66
  419.4 15.7 %collective-permute-start.33 = (f32[29,768]{1,0:T(8,128)S(1)}, f32[29,768]{1,0:T(8,128)S(1)}, u32[]{:S(2)}, u32[]{:S(2)}) collective-permute-start(f32[29,768]{1,0:T(8,128)S(1)} %add.488), channel_id=1, source_target_pairs={{0,8},{4,12},{8,0},{12,4},{16,24},{20,28},{24,16},{28,20},{1,9},{5... | collective-permute-start | bytes 267272 | tf_op jit(solution)/shard_map/ppermute | solution.py:66
  419.6 27.7 %copy-start.33 = (f32[512,768]{1,0:T(8,128)S(1)}, f32[512,768]{1,0:T(8,128)}, u32[]{:S(2)}) copy-start(f32[512,768]{1,0:T(8,128)} %get-tuple-element.180) | copy-start | bytes 4718596
  421.6 25.7 %copy-start.30 = (f32[512,768]{1,0:T(8,128)S(1)}, f32[512,768]{1,0:T(8,128)}, u32[]{:S(2)}) copy-start(f32[512,768]{1,0:T(8,128)} %param.17) | copy-start | bytes 4718596
  421.6 25.7 %copy-start.67 = (f32[512]{0:T(512)S(1)}, f32[512]{0:T(512)}, u32[]{:S(2)}) copy-start(f32[512]{0:T(512)} %copy-done.66) | copy-start | bytes 6148
  421.7 25.7 %copy-start.71 = (f32[512]{0:T(512)S(1)}, f32[512]{0:T(512)}, u32[]{:S(2)}) copy-start(f32[512]{0:T(512)} %get-tuple-element.212) | copy-start | bytes 6148
  435.1 7.1 %collective-permute-start.34 = (f32[29,768]{1,0:T(8,128)S(1)}, f32[29,768]{1,0:T(8,128)S(1)}, u32[]{:S(2)}, u32[]{:S(2)}) collective-permute-start(f32[29,768]{1,0:T(8,128)S(1)} %add.489), channel_id=1, source_target_pairs={{0,16},{4,20},{8,24},{12,28},{16,0},{20,4},{24,8},{28,12},{1,17},{... | collective-permute-start | bytes 267272 | tf_op jit(solution)/shard_map/ppermute | solution.py:66
  442.2 4.7 collective-permute-start.35
  442.5 15.3 %collective-permute-start.46 = (bf16[384,768]{1,0:T(8,128)(2,1)S(1)}, bf16[384,768]{1,0:T(8,128)(2,1)S(1)}, u32[]{:S(2)}, u32[]{:S(2)}) collective-permute-start(bf16[384,768]{1,0:T(8,128)(2,1)S(1)} %maximum_select_fusion.3), channel_id=1, source_target_pairs={{0,4},{4,0},{8,12},{12,8},{16,20},{20,16},{24,28},{28,24},{1,5},{5... | collective-permute-start | bytes 1769480 | tf_op jit(solution)/shard_map/ppermute | solution.py:66
  446.9 6.1 %collective-permute-start.36 = (f32[29,768]{1,0:T(8,128)S(1)}, f32[29,768]{1,0:T(8,128)S(1)}, u32[]{:S(2)}, u32[]{:S(2)}) collective-permute-start(f32[29,768]{1,0:T(8,128)S(1)} %add.491), channel_id=1, source_target_pairs={{0,2},{1,3},{2,0},{3,1},{4,6},{5,7},{6,4},{7,5},{8,10},{9,11},{10,... | collective-permute-start | bytes 267272 | tf_op jit(solution)/shard_map/ppermute | solution.py:62
  (61 other events, 324.9 us)
Sparse Core Ops, SparseCore 0:
  263.8 223.4 all-reduce.6
where the time goes:
time: 524 us; the launch traced here: 514 us
  Pallas kernels  163 us (31%)
  starting transfers between devices  100 us (19%)
  waiting for transfers between devices  99 us (19%)
  other arithmetic  62.4 us (12%)
  local copies, waits for them, and re-layouts  60.2 us (11%)
  between operations  17.9 us (3%)
  matrix products  10.5 us (2%)
    pallas_call x4, Pallas kernels, expert_chunk(): pl.pallas_call(functools.partial(expert_kernel, tiles, span, sources), gr...  76.7 us
    ppermute x32, starting transfers between devices, along_z(): return lax.ppermute(value, 'tensor', pairs)  63.5 us
    ppermute x32, waiting for transfers between devices, along_z(): return lax.ppermute(value, 'tensor', pairs)  40.1 us
    ppermute x15, starting transfers between devices, along_dp(): return lax.ppermute(value, 'dp', [(i, i ^ 1 << bit) for i in range(size)])  36.8 us
    pallas_call x1, Pallas kernels, attention_backward(): pl.pallas_call(attention_back_kernel, grid_spec=pltpu.PrefetchScalarGridS...  32 us
    ppermute x15, waiting for transfers between devices, along_dp(): return lax.ppermute(value, 'dp', [(i, i ^ 1 << bit) for i in range(size)])  31.9 us
    psum x1, waiting for transfers between devices, shards(): lax.psum((up_low, up_high, down_low, down_high), 'dp')  27 us
    pallas_call x1, Pallas kernels, attention_forward(): pl.pallas_call(attention_kernel, grid_spec=pltpu.PrefetchScalarGridSpec(n...  20.8 us
  transfers between devices with their start and end apart: 48, of which 15 were waited for; matrix products, arithmetic and copies ran while one was open for 21% of the time, Pallas kernels for 25%

commit v1 on v0

--- a/solution.py
+++ b/solution.py
@@ -97,18 +97,12 @@
     return value
 
 
-def sum_everywhere(value, bits, size):
-    for bit in bits:
+def sum_everywhere(value, bits, size, beside):
+    value = value + along_z(value, SIDE)
+    value = value + along_z(value, CROSS)
+    for bit in bits[1:]:
         value = value + along_dp(value, bit, size)
-    value = value + along_z(value, SIDE)
-    return value + along_z(value, CROSS)
-
-
-def piece_place(index, order):
-    place = 0
-    for bit in order:
-        place = 2 * place + ((index >> bit) & 1)
-    return place
+    return value + behind(along_dp(value, bits[0], size), beside)
 
 
 def rope_tables(offset):
@@ -593,10 +587,8 @@
     )(meta, chunk, place, carry, routes, w_router, w_up, w_down, *taken, *extra)
 
 
-def grad_walk(number, first, tiles, half):
-    experts, chunks = number.shape[0] // 2, number.shape[1]
-    number = lax.dynamic_slice_in_dim(number, half * experts, experts, 0)
-    first = lax.dynamic_slice_in_dim(first, half * experts, experts, 0)
+def grad_walk(number, first, tiles):
+    experts, chunks = number.shape
     flat = number.reshape(-1)
     groups = flat.shape[0]
     earlier = jnp.arange(groups)[:, None] > jnp.arange(groups)[None, :]
@@ -623,9 +615,31 @@
     return jnp.concatenate([owner, block, left, everything[None]]).astype(I32)
 
 
+def packing(width, hidden_width):
+    columns = 2 * hidden_width
+    spare = columns - width
+    height = hidden_width * width // columns
+    pieces = [(slice(width, width + height), slice(0, width), slice(0, height), slice(0, width))]
+    short = hidden_width - height
+    for at in range(width // spare):
+        pieces.append(
+            (
+                slice(width + at * short, width + (at + 1) * short),
+                slice(width, columns),
+                slice(height, hidden_width),
+                slice(at * spare, (at + 1) * spare),
+            )
+        )
+    return pieces
+
+
+def packed_height(width, hidden_width):
+    return width + width // 2
+
+
 def weight_grad_kernel(steps, walk, *refs):
-    kept, (grad_up, grad_down) = refs[:4], refs[4:6]
-    rows, (sum_up, sum_down, out_up, out_down, load_sems, save_sems) = refs[6:10], refs[10:]
+    kept, packed = refs[:4], refs[4]
+    rows, (sum_up, sum_down, out, load_sems, save_sems) = refs[5:9], refs[9:]
     number = walk[(2 + GROUP) * steps]
     width, hidden_width = sum_up.shape[0], sum_down.shape[0]
 
@@ -645,14 +659,15 @@
                 )
         return copies
 
-    def saves(expert):
-        slot = lax.rem(expert, 2)
-        up_rows = pl.ds(pl.multiple_of(expert * width, width), width)
-        down_rows = pl.ds(pl.multiple_of(expert * hidden_width, hidden_width), hidden_width)
-        return (
-            pltpu.make_async_copy(out_up.at[slot], grad_up.at[up_rows], save_sems.at[slot, 0]),
-            pltpu.make_async_copy(out_down.at[slot], grad_down.at[down_rows], save_sems.at[slot, 1]),
-        )
+    def save(expert):
+        slot, height = lax.rem(expert, 2), out.shape[1]
+        goal = pl.ds(pl.multiple_of(expert * height, height), height)
+        return pltpu.make_async_copy(out.at[slot], packed.at[goal], save_sems.at[slot])
+
+    def store(side, up, down):
+        out[side, :width] = up.astype(BF16)
+        for goal, columns, source, taken in packing(width, hidden_width):
+            out[side, goal, columns] = down[source, taken].astype(BF16)
 
     for copy in loads(0):
         copy.start()
@@ -685,13 +700,11 @@
 
         @pl.when(done & (expert >= 2))
         def _():
-            for copy in saves(expert - 2):
-                copy.wait()
+            save(expert - 2).wait()
 
         @pl.when(fresh & done)
         def _():
-            up, down = products()
-            out_up[side], out_down[side] = up.astype(BF16), down.astype(BF16)
+            store(side, *products())
 
         @pl.when(fresh & jnp.logical_not(done))
         def _():
@@ -706,23 +719,20 @@
         @pl.when(jnp.logical_not(fresh) & done)
         def _():
             up, down = products()
-            out_up[side] = (sum_up[...] + up).astype(BF16)
-            out_down[side] = (sum_down[...] + down).astype(BF16)
+            store(side, sum_up[...] + up, sum_down[...] + down)
 
         @pl.when(done)
         def _():
-            for copy in saves(expert):
-                copy.start()
-
-    for expert in (EXP_FFN // 2 - 2, EXP_FFN // 2 - 1):
-        for copy in saves(expert):
-            copy.wait()
+            save(expert).start()
+
+    for expert in (EXP_FFN - 2, EXP_FFN - 1):
+        save(expert).wait()
 
 
 def weight_grads(walk, saved):
     width, hidden_width = saved[0].shape[1], saved[1].shape[1]
-    experts = EXP_FFN // 2
-    steps = most_groups(saved[0].shape[0] // TILE, experts)
+    height = packed_height(width, hidden_width)
+    steps = most_groups(saved[0].shape[0] // TILE, EXP_FFN)
     shape = jax.ShapeDtypeStruct
     stay = pl.BlockSpec(memory_space=pl.ANY)
     return pl.pallas_call(
@@ -731,108 +741,53 @@
             num_scalar_prefetch=1,
             grid=(1,),
             in_specs=[stay] * 4,
-            out_specs=[stay] * 2,
+            out_specs=stay,
             scratch_shapes=[
                 *[pltpu.VMEM((2, GROUP * TILE, kept.shape[1]), BF16) for kept in saved],
                 pltpu.VMEM((width, 2 * hidden_width), F32),
                 pltpu.VMEM((hidden_width, width), F32),
-                pltpu.VMEM((2, width, 2 * hidden_width), BF16),
-                pltpu.VMEM((2, hidden_width, width), BF16),
+                pltpu.VMEM((2, height, 2 * hidden_width), BF16),
                 pltpu.SemaphoreType.DMA((2, GROUP, 4)),
-                pltpu.SemaphoreType.DMA((2, 2)),
+                pltpu.SemaphoreType.DMA((2,)),
             ],
         ),
-        out_shape=[
-            shape((experts * width, 2 * hidden_width), BF16),
-            shape((experts * hidden_width, width), BF16),
-        ],
+        out_shape=shape((EXP_FFN * height, 2 * hidden_width), BF16),
         compiler_params=pltpu.CompilerParams(vmem_limit_bytes=48 * 2**20),
         cost_estimate=lasting(COST_GRADS),
         name="weight_grads",
     )(walk, *saved)
 
 
-def combine_kernel(scalars, own_send, far_send, own_keep, far_keep, *refs):
-    send, keep = refs[-2:]
-    send[...] = own_send[...] + far_send[...]
-    keep[...] = own_keep[...] + far_keep[...]
-
-
-def combine(own, far, bit, start, rows, ready):
-    columns = own.shape[1]
-    half = rows // 2
-    block = min(half, 384)
-    number = half // block
-    place = lambda side: pl.BlockSpec(
-        (block, columns), lambda i, b: (start // block + (b[0] if side else 1 - b[0]) * number + i, 0)
-    )
-    out = pl.BlockSpec((block, columns), lambda i, b: (i, 0))
-    shape = jax.ShapeDtypeStruct((half, columns), own.dtype)
-    return pl.pallas_call(
-        combine_kernel,
-        grid_spec=pltpu.PrefetchScalarGridSpec(
-            num_scalar_prefetch=1,
-            grid=(number,),
-            in_specs=[place(False), place(False), place(True), place(True)]
-            + [pl.BlockSpec(memory_space=pl.ANY)] * len(ready),
-            out_specs=[out, out],
-        ),
-        out_shape=[shape, shape],
-        compiler_params=pltpu.CompilerParams(vmem_limit_bytes=32 * 2**20),
-        cost_estimate=lasting(COST_ADD),
-        name="combine",
-    )(bit, own, far, own, far, *ready)
-
-
-def widen_kernel(source, *refs):
-    refs[-1][...] = source[...].astype(F32)
-
-
-def widen(source, half, target):
-    rows, columns = source.shape
-    block = 768
-    number = rows // block
-    extra = () if target is None else (target,)
+def widen_kernel(source, up, down):
+    width = down.shape[1]
+    split = source.shape[1] // LANES
+    for row in range(split):
+        at = row % 2 * (source.shape[1] // 2) + row // 2 * LANES
+        up[pl.ds(row, width, stride=split), :] = source[:width, at : at + LANES].astype(F32)
+    for place, columns, goal, taken in packing(width, down.shape[0]):
+        down[goal, taken] = source[place, columns].astype(F32)
+
+
+def widen(packed, width, hidden_width):
+    height = packed_height(width, hidden_width)
+    rows = width * packed.shape[1] // LANES
+    shape = jax.ShapeDtypeStruct
     return pl.pallas_call(
         widen_kernel,
-        grid=(number,),
-        in_specs=[pl.BlockSpec((block, columns), lambda i: (i, 0))]
-        + [pl.BlockSpec(memory_space=pl.ANY)] * len(extra),
-        out_specs=pl.BlockSpec((block, columns), lambda i: (half * number + i, 0)),
-        out_shape=jax.ShapeDtypeStruct((2 * rows, columns), F32),
-        input_output_aliases={1: 0} if extra else {},
-        compiler_params=pltpu.CompilerParams(vmem_limit_bytes=48 * 2**20),
+        grid=(EXP_FFN,),
+        in_specs=[pl.BlockSpec((height, packed.shape[1]), lambda i: (i, 0))],
+        out_specs=[
+            pl.BlockSpec((rows, LANES), lambda i: (i, 0)),
+            pl.BlockSpec((hidden_width, width), lambda i: (i, 0)),
+        ],
+        out_shape=[
+            shape((EXP_FFN * rows, LANES), F32),
+            shape((EXP_FFN * hidden_width, width), F32),
+        ],
+        compiler_params=pltpu.CompilerParams(vmem_limit_bytes=60 * 2**20),
         cost_estimate=lasting(COST_WIDEN),
         name="widen",
-    )(source, *extra)
-
-
-def widen_pairs_kernel(source, *refs):
-    target = refs[-1]
-    rows, columns = source.shape
-    for row in range(columns // LANES):
-        at = row % 2 * (columns // 2) + row // 2 * LANES
-        target[pl.ds(row, rows, stride=columns // LANES), :] = source[:, at : at + LANES].astype(F32)
-
-
-def widen_pairs(source, half, target):
-    rows, columns = source.shape
-    block = 768
-    number = rows // block
-    extra = () if target is None else (target,)
-    split = columns // LANES
-    return pl.pallas_call(
-        widen_pairs_kernel,
-        grid=(number,),
-        in_specs=[pl.BlockSpec((block, columns), lambda i: (i, 0))]
-        + [pl.BlockSpec(memory_space=pl.ANY)] * len(extra),
-        out_specs=pl.BlockSpec((block * split, LANES), lambda i: (half * number + i, 0)),
-        out_shape=jax.ShapeDtypeStruct((2 * rows * split, LANES), F32),
-        input_output_aliases={1: 0} if extra else {},
-        compiler_params=pltpu.CompilerParams(vmem_limit_bytes=48 * 2**20),
-        cost_estimate=lasting(COST_WIDEN),
-        name="widen_pairs",
-    )(source, *extra)
+    )(packed)
 
 
 def shards(
@@ -885,7 +840,7 @@
             place, meta, number, first = expert_plan(*behind((routes, valid), piece), chunks)
         if level == 1:
             number, first = behind((number, first), piece)
-            walks = [grad_walk(number, first, most_tiles(rows), half) for half in range(2)]
+            walk = grad_walk(number, first, most_tiles(rows))
         other = along_dp(piece, bit, dp_size)
         piece = jnp.where(
             (index >> bit) & 1 == 0,
@@ -908,7 +863,7 @@
     cosine, sine = rope_tables(offset)
     valid_rows = jnp.concatenate([cut(valid, first_row), cut(valid, (here ^ 1) * rows)])[:, None]
     fixed = (both_in, both_out, cosine, sine, valid_rows)
-    ready = (place, meta, *walks, cot_side, cot_middle, carry_wide, routes_live, router_wide)
+    ready = (place, meta, walk, cot_side, cot_middle, carry_wide, routes_live, router_wide)
     part_own, part_other, *saved_attention = attention_forward(
         scalars, normed_low, normed_other, *fixed, ready
     )
@@ -950,7 +905,7 @@
     far, across = along_z(middle_rows, OUTWARD), along_z(side, MIDDLE)
     cot_last.append(along_z(behind(cot_pieces[1], part_0), OUTWARD))
     part_1, feed_1, *saved = chunk(1, [{"x": [side], "cot": [cot_side]}], saved)
-    near = along_z(part_1, INWARD)
+    near, feed_near = along_z(part_1, INWARD), along_z(feed_1, INWARD)
     far, across, cot_last[1] = behind((far, across, cot_last[1]), part_1)
     last = along_z(across, OUTWARD)
     cot_last.append(along_z(behind(cot_pieces[2], part_1), OUTWARD))
@@ -966,14 +921,14 @@
     )
 
     inward = along_z(part_3, INWARD)
-    up_low, down_low = weight_grads(walks[0], saved)
-    inward = part_3 + behind(inward, up_low)
-    inward = along_z(inward, MIDDLE)
+    packed = weight_grads(walk, saved)
+    inward, packed = lax.optimization_barrier((inward, packed))
+    packed = lax.psum_scatter(packed, "dp", scatter_dimension=0, tiled=True)
+    feed_outward = along_z(behind(feed_3, inward), INWARD)
+    inward = part_3 + inward
+    inward, feed_outward = lax.optimization_barrier((along_z(inward, MIDDLE), feed_outward))
     third = along_z(part_2 + third, MIDDLE)
-    up_high, down_high = weight_grads(walks[1], saved)
-    outward_sum = part_1 + behind(inward, up_high)
-    outward = along_z(outward_sum, OUTWARD)
-    up_low, up_high, down_low, down_high = lax.psum((up_low, up_high, down_low, down_high), "dp")
+    outward = along_z(part_1 + inward, OUTWARD)
     summed = part_0.astype(F32) + near.astype(F32) + third.astype(F32) + outward.astype(F32)
 
     logits = dot(second_low, w_router) + cut(carry, first_row)
@@ -1053,6 +1008,7 @@
 
     grad_low = grad_middle.astype(BF16)
     grad_other = along_z(grad_low, SIDE)
+    feed_outward = feed_3 + feed_outward
 
     part_own, part_other, grad_w, grad_o, gain_rows = attention_backward(
         scalars, normed_low, normed_other, *fixed, grad_low, grad_other, saved_attention, ()
@@ -1060,12 +1016,12 @@
     grad_normed = part_own.astype(F32) + along_z(part_other, SIDE).astype(F32)
     grad_stream = grad_middle + norm_backward(stream, inverse_one, gain_attention, grad_normed)
 
-    feed_1, feed_2, feed_3 = behind((feed_1, feed_2, feed_3), grad_low)
-    near = along_z(feed_1, INWARD)
-    third = along_z(feed_2 + along_z(feed_2, INWARD), MIDDLE)
-    outward = along_z(feed_3 + along_z(feed_3, INWARD), MIDDLE)
-    outward = along_z(feed_1 + outward, OUTWARD)
-    feed = feed_0.astype(F32) + near.astype(F32) + third.astype(F32) + outward.astype(F32)
+    feed_2, feed_outward = behind((feed_2, feed_outward), part_own)
+    feed_third, feed_outward = along_z(feed_2, INWARD), along_z(feed_outward, MIDDLE)
+    feed_third = along_z(feed_2 + feed_third, MIDDLE)
+    feed_outward = along_z(feed_1 + feed_outward, OUTWARD)
+    feed = feed_0.astype(F32) + feed_near.astype(F32)
+    feed = feed + feed_third.astype(F32) + feed_outward.astype(F32)
     experts = feed + extra
     block_out = middle + experts
     squares = [
@@ -1073,19 +1029,20 @@
     ]
     squares = jnp.stack([*squares, jnp.sum(valid_here)])
 
-    grad_down = widen(down_high, 1, widen(down_low, 0, None))
-    grad_down = grad_down.reshape(EXP_FFN, -1, width)
-    grad_gate_up = widen_pairs(up_high, 1, widen_pairs(up_low, 0, None))
-    tiles = up_low.shape[1] // (2 * LANES)
-    grad_gate_up = grad_gate_up.reshape(EXP_FFN, width, tiles, 2, LANES).transpose(0, 1, 3, 2, 4)
-    grad_gate_up = grad_gate_up.reshape(EXP_FFN, width, 2, -1)
-
     own_grads = jnp.concatenate([grad_w[:, :head_columns], grad_o[None, :head_columns]], axis=0)
     far_grads = jnp.concatenate([grad_w[:, head_columns:], grad_o[None, head_columns:]], axis=0)
     order = bits
-    own_piece = reduce_blocks(own_grads.reshape(-1, width), order, index, dp_size)
-    far_piece = reduce_blocks(far_grads.reshape(-1, width), order, index, dp_size)
+    own_piece = reduce_blocks(own_grads.reshape(-1, width), order[:1], index, dp_size)
+    far_piece = reduce_blocks(far_grads.reshape(-1, width), order[:1], index, dp_size)
+    packed = lax.all_gather(behind(packed, own_piece), "dp", axis=0, tiled=True)
+    own_piece = reduce_blocks(own_piece, order[1:], index, dp_size)
+    far_piece = reduce_blocks(far_piece, order[1:], index, dp_size)
     own_piece = own_piece + along_z(far_piece, CROSS)
+    grad_gate_up, grad_down = widen(packed, width, w_down.shape[1])
+    grad_gate_up = grad_gate_up.reshape(EXP_FFN, width, -1, 2, LANES).transpose(0, 1, 3, 2, 4)
+    grad_gate_up = grad_gate_up.reshape(EXP_FFN, width, 2, -1)
+    grad_down = grad_down.reshape(EXP_FFN, -1, width)
+
     attention_grads = spread_blocks(own_piece, order, index, dp_size).astype(F32)
     attention_grads = attention_grads.reshape(4, head_columns, width)
     grad_inputs = attention_grads[:3].transpose(0, 2, 1)
@@ -1104,7 +1061,7 @@
         ],
         axis=0,
     )
-    small = sum_everywhere(small, bits, dp_size)
+    small = sum_everywhere(small, bits, dp_size, grad_down)
     at = 1 + 2 * columns
     squares = small[at + 6, :3]
     counted = small[at + 6, 3]

time: 524 us -> 510 us (0.973)
  local copies, waits for them, and re-layouts: 60.2 us -> 52.1 us
    ppermute x32, waiting for transfers between devices: 40.1 us -> 71.2 us  [along_z(): return lax.ppermute(value, 'tensor', pairs)]
    psum x1 -> x0, waiting for transfers between devices: 27 us -> none  [shards(): lax.psum((up_low, up_high, down_low, down_high), 'dp')]
    ppermute x15, starting transfers between devices: 36.8 us -> 45.3 us  [along_dp(): return lax.ppermute(value, 'dp', [(i, i ^ 1 << bit) for i in range(size)])]
    ppermute x32, starting transfers between devices: 63.5 us -> 55.2 us  [along_z(): return lax.ppermute(value, 'tensor', pairs)]
    ppermute x15, waiting for transfers between devices: 31.9 us -> 24.8 us  [along_dp(): return lax.ppermute(value, 'dp', [(i, i ^ 1 << bit) for i in range(size)])]
    unnamed x158 -> x148, local copies, waits for them, and re-layouts: 18.9 us -> 14.1 us
    add x6 -> x7, other arithmetic: 6.79 us -> 10.9 us  [the longest x1 2.43 us: shards(): feed_outward = feed_3 + feed_outward]
    pallas_call x2 -> x1, Pallas kernels: 18.9 us -> 16.1 us  [weight_grads(): pl.pallas_call(functools.partial(weight_grad_kernel, steps), grid_spec=pl...]
  transfers between devices with their start and end apart: 48 -> 49, of which waited for: 15 -> 18; matrix products, arithmetic and copies ran while one was open for 21% -> 21% of each run, Pallas kernels for 25% -> 28%
where the time goes in v1:
time: 510 us; the launch traced here: 502 us
  Pallas kernels  162 us (32%)
  starting transfers between devices  101 us (20%)
  waiting for transfers between devices  97.5 us (19%)
  other arithmetic  62.6 us (12%)
  local copies, waits for them, and re-layouts  52.1 us (10%)
  between operations  17 us (3%)
  matrix products  10.5 us (2%)
    pallas_call x4, Pallas kernels, expert_chunk(): pl.pallas_call(functools.partial(expert_kernel, tiles, span, sources), gr...  76.4 us
    ppermute x32, waiting for transfers between devices, along_z(): return lax.ppermute(value, 'tensor', pairs)  71.2 us
    ppermute x32, starting transfers between devices, along_z(): return lax.ppermute(value, 'tensor', pairs)  55.2 us
    ppermute x15, starting transfers between devices, along_dp(): return lax.ppermute(value, 'dp', [(i, i ^ 1 << bit) for i in range(size)])  45.3 us
    pallas_call x1, Pallas kernels, attention_backward(): pl.pallas_call(attention_back_kernel, grid_spec=pltpu.PrefetchScalarGridS...  32 us
    ppermute x15, waiting for transfers between devices, along_dp(): return lax.ppermute(value, 'dp', [(i, i ^ 1 << bit) for i in range(size)])  24.8 us
    pallas_call x1, Pallas kernels, attention_forward(): pl.pallas_call(attention_kernel, grid_spec=pltpu.PrefetchScalarGridSpec(n...  20.8 us
    pallas_call x1, Pallas kernels, widen(): pl.pallas_call(widen_kernel, grid=(EXP_FFN,), in_specs=[pl.BlockSpec((hei...  16.5 us
  transfers between devices with their start and end apart: 49, of which 18 were waited for; matrix products, arithmetic and copies ran while one was open for 21% of the time, Pallas kernels for 28%

profile of v1, /device:TPU:0, one launch (start us, length us, event | category | flops | bytes accessed | tf_op | source)
XLA Modules:
  0.0 502.1 jit_solution(7396859300377418347)
XLA Ops:
  8.8 4.1 collective-permute-start.1
  13.9 1.6 collective-permute-start
  17.0 1.9 fusion.18
  20.4 2.4 convert_element_type.106.refs_1_
  26.6 1.6 collective-permute-start.2
  31.3 2.3 pad.16.clone
  34.5 1.6 collective-permute-start.3
  37.2 5.6 %collective-permute-done.3 = bf16[192,768]{1,0:T(8,128)(2,1)} collective-permute-done((bf16[192,768]{1,0:T(8,128)(2,1)S(1)}, bf16[192,768]{1,0:T(8,128)(2,1)}, u32[]{:S(2)}, u32[]{:S(2)}) %collective-permute-start.3) | collective-permute-done | bytes 294944 | tf_op jit(solution)/shard_map/ppermute | solution.py:66
  47.0 5.0 collective-permute-done.5.refs_3_.refs_1_
  52.8 1.6 maximum_select_fusion
  57.0 20.8 %attention_forward.1 = (bf16[512,768]{1,0:T(8,128)(2,1)S(1)}, bf16[512,768]{1,0:T(8,128)(2,1)}, bf16[1024,384]{1,0:T(8,128)(2,1)}, bf16[1024,384]{1,0:T(8,128)(2...) custom-call(s32[2]{0:T(128)S(1)} %pad_add_fusion.3.scalars, ...), custom_call_target="tpu_custom_call" | custom-call | bytes 60000000 | tf_op jit(solution)/shard_map/attention_forward/pallas_call | solution.py:210
  79.3 2.8 collective-permute-start.7
  83.9 16.0 %reshape.496.w_up_all = bf16[6,768,1024]{2,1,0:T(8,128)(2,1)} reshape(bf16[6,768,2,512]{3,2,1,0:T(2,128)(2,1)} %param.25) | data formatting | bytes 18874368 | tf_op jit(solution)/shard_map/reshape | solution.py:874
  99.9 2.1 multiply_reduce_fusion.6
  105.2 1.6 collective-permute-start.11
  111.9 18.8 %expert_chunk.4 = (bf16[528,768]{1,0:T(8,128)(2,1)}, bf16[512,768]{1,0:T(8,128)(2,1)}, bf16[6656,768]{1,0:T(8,128)(2,1)}, bf16[6656,512]{1,0:T(8,128)(2,1)}, bf1...) custom-call(s32[156]{0:T(256)S(1)} %reshape.492.refs_1_.meta, s32[2]{0:T(128)S(1)} %pad_add_fusion.2.chunk, ...), custom_call_target="tpu_custom_call" | custom-call | bytes 60000000 | tf_op jit(solution)/shard_map/expert_chunk/pallas_call | solution.py:549
  132.7 1.6 collective-permute-start.15
  136.2 18.8 %expert_chunk.5 = (bf16[528,768]{1,0:T(8,128)(2,1)}, bf16[512,768]{1,0:T(8,128)(2,1)}, bf16[6656,768]{1,0:T(8,128)(2,1)}, bf16[6656,512]{1,0:T(8,128)(2,1)}, bf1...) custom-call(s32[156]{0:T(256)S(1)} %reshape.492.refs_1_.meta, ...), custom_call_target="tpu_custom_call", output_to_operand_aliasing={{2}: (10, {}), {3}: (11, {}), {4}: (12, {}), {5}: (13, {})} | custom-call | bytes 60000000 | tf_op jit(solution)/shard_map/expert_chunk/pallas_call | solution.py:549
  155.0 2.0 collective-permute-done.16.refs_4_
  159.0 1.7 slice.135
  164.2 19.3 %expert_chunk.6 = (bf16[528,768]{1,0:T(8,128)(2,1)}, bf16[512,768]{1,0:T(8,128)(2,1)}, bf16[6656,768]{1,0:T(8,128)(2,1)}, bf16[6656,512]{1,0:T(8,128)(2,1)}, bf1...) custom-call(s32[156]{0:T(256)S(1)} %reshape.492.refs_1_.meta, ...), custom_call_target="tpu_custom_call", output_to_operand_aliasing={{2}: (12, {}), {3}: (13, {}), {4}: (14, {}), {5}: (15, {})} | custom-call | bytes 60000000 | tf_op jit(solution)/shard_map/expert_chunk/pallas_call | solution.py:549
  184.0 19.6 %expert_chunk.7 = (bf16[528,768]{1,0:T(8,128)(2,1)}, bf16[512,768]{1,0:T(8,128)(2,1)}, bf16[6656,768]{1,0:T(8,128)(2,1)}, bf16[6656,512]{1,0:T(8,128)(2,1)}, bf1...) custom-call(s32[156]{0:T(256)S(1)} %reshape.492.refs_1_.meta, ...), custom_call_target="tpu_custom_call", output_to_operand_aliasing={{2}: (14, {}), {3}: (15, {}), {4}: (16, {}), {5}: (17, {})} | custom-call | bytes 60000000 | tf_op jit(solution)/shard_map/expert_chunk/pallas_call | solution.py:549
  203.6 7.4 %collective-permute-start.19 = (bf16[528,768]{1,0:T(8,128)(2,1)}, bf16[528,768]{1,0:T(8,128)(2,1)}, u32[]{:S(2)}, u32[]{:S(2)}) collective-permute-start(bf16[528,768]{1,0:T(8,128)(2,1)} %get-tuple-element.124), channel_id=1, source_target_pairs={{0,1},{3,2},{4,5},{7,6},{8,9},{11,10},{12,13},{15,14},{16,17},{19,... | collective-permute-start | bytes 2433032 | tf_op jit(solution)/shard_map/ppermute | solution.py:62
  211.0 16.1 %weight_grads.1 = bf16[6912,1024]{1,0:T(8,128)(2,1)} custom-call(s32[103]{0:T(128)S(1)} %pad_add_fusion.4.refs_2_.walk, bf16[6656,768]{1,0:T(8,128)(2,1)} %get-tuple-element.125.refs_0_, bf16[6656,512]{1,0:T(8,128)(2,1)} %get-tuple-element.126.refs_1_, bf16[6656,768]{1,0:T(8,128)(2,1)} %get-tuple-element.127.refs_2_, ...), custom_call_target="tpu_custom_call" | custom-call | bytes 33000000 | tf_op jit(solution)/shard_map/weight_grads/pallas_call | solution.py:738
  229.1 2.8 fusion.11
  231.9 2.8 collective-permute-start.23
  234.7 2.3 add.361
  237.0 2.2 collective-permute-start.21
  239.2 1.6 collective-permute-start.20
  242.4 10.2 %collective-permute-done.23 = bf16[528,768]{1,0:T(8,128)(2,1)} collective-permute-done((bf16[528,768]{1,0:T(8,128)(2,1)}, bf16[528,768]{1,0:T(8,128)(2,1)}, u32[]{:S(2)}, u32[]{:S(2)}) %collective-permute-start.23) | collective-permute-done | bytes 811040 | tf_op jit(solution)/shard_map/ppermute | solution.py:62
  252.6 2.1 add.364
  255.6 13.9 %collective-permute-done.21 = bf16[512,768]{1,0:T(8,128)(2,1)} collective-permute-done((bf16[512,768]{1,0:T(8,128)(2,1)}, bf16[512,768]{1,0:T(8,128)(2,1)}, u32[]{:S(2)}, u32[]{:S(2)}) %collective-permute-start.21) | collective-permute-done | bytes 786464 | tf_op jit(solution)/shard_map/ppermute | solution.py:62
  272.4 3.9 fusion.2
  276.4 6.2 %collective-permute-done.22 = bf16[528,768]{1,0:T(8,128)(2,1)S(1)} collective-permute-done((bf16[528,768]{1,0:T(8,128)(2,1)}, bf16[528,768]{1,0:T(8,128)(2,1)S(1)}, u32[]{:S(2)}, u32[]{:S(2)}) %collective-permute-start.22) | collective-permute-done | bytes 811040 | tf_op jit(solution)/shard_map/ppermute | solution.py:62
  282.6 2.4 collective-permute-done.25
  286.8 2.4 multiply_reduce_fusion.2
  289.2 1.9 fusion.45
  291.3 13.8 %collective-permute-done.26.grad_other = bf16[512,768]{1,0:T(8,128)(2,1)} collective-permute-done((bf16[512,768]{1,0:T(8,128)(2,1)}, bf16[512,768]{1,0:T(8,128)(2,1)}, u32[]{:S(2)}, u32[]{:S(2)}) %collective-permute-start.26) | collective-permute-done | bytes 786464 | tf_op jit(solution)/shard_map/ppermute | solution.py:62
  306.1 32.0 %attention_backward.1 = (bf16[512,768]{1,0:T(8,128)(2,1)S(1)}, bf16[512,768]{1,0:T(8,128)(2,1)}, bf16[3,384,768]{2,1,0:T(8,128)(2,1)}, bf16[384,768]{1,0:T(8,128)(2,1)S(1)}, f32[8,768]{1,0:T(8,128)S(1)}) custom-call(s32[2]{0:T(128)S(1)} %pad_add_fusion.3.scalars, bf16[512,768]{1,0:T(8,128)(2,1)S(1)} %multiply_convert_fusion.own, ...), custom_call_target="tpu_custom_call" | custom-call | bytes 96000000 | tf_op jit(solution)/shard_map/attention_backward/pallas_call | solution.py:309
  338.2 2.7 fusion.50
  341.2 2.1 collective-permute-done.37
  349.0 2.4 add.362
  351.5 4.3 collective-permute-start.27
  355.8 1.8 collective-permute-start.29
  359.1 3.1 collective-permute-start.13
  367.2 5.8 %collective-permute-done.27 = bf16[512,768]{1,0:T(8,128)(2,1)} collective-permute-done((bf16[512,768]{1,0:T(8,128)(2,1)}, bf16[512,768]{1,0:T(8,128)(2,1)}, u32[]{:S(2)}, u32[]{:S(2)}) %collective-permute-start.27) | collective-permute-done | bytes 786464 | tf_op jit(solution)/shard_map/ppermute | solution.py:62
  373.0 2.4 add.375
  375.5 1.5 collective-permute-start.28
  377.0 2.4 add.377
  380.9 23.7 %collective-permute-start.42 = (bf16[96,768]{1,0:T(8,128)(2,1)S(1)}, bf16[96,768]{1,0:T(8,128)(2,1)S(1)}, u32[]{:S(2)}, u32[]{:S(2)}) collective-permute-start(bf16[96,768]{1,0:T(8,128)(2,1)S(1)} %constant_dynamic-slice_fusion), channel_id=1, source_target_pairs={{0,16},{4,20},{8,24},{12,28},{16,0},{20,4},{24,8},{28,12},{1,17},{... | collective-permute-start | bytes 442376 | tf_op jit(solution)/shard_map/ppermute | solution.py:66
  404.8 10.0 %collective-permute-start.39 = (bf16[96,768]{1,0:T(8,128)(2,1)S(1)}, bf16[96,768]{1,0:T(8,128)(2,1)S(1)}, u32[]{:S(2)}, u32[]{:S(2)}) collective-permute-start(bf16[96,768]{1,0:T(8,128)(2,1)S(1)} %constant_dynamic-slice_fusion.3), channel_id=1, source_target_pairs={{0,16},{4,20},{8,24},{12,28},{16,0},{20,4},{24,8},{28,12},{1,17},{... | collective-permute-start | bytes 442376 | tf_op jit(solution)/shard_map/ppermute | solution.py:66
  416.3 2.4 collective-permute-done.39
  418.7 5.6 %collective-permute-done.43 = bf16[96,768]{1,0:T(8,128)(2,1)S(1)} collective-permute-done((bf16[96,768]{1,0:T(8,128)(2,1)S(1)}, bf16[96,768]{1,0:T(8,128)(2,1)S(1)}, u32[]{:S(2)}, u32[]{:S(2)}) %collective-permute-start.43) | collective-permute-done | bytes 147488 | tf_op jit(solution)/shard_map/ppermute | solution.py:62
  425.7 8.0 %collective-permute-done.44 = bf16[96,768]{1,0:T(8,128)(2,1)S(1)} collective-permute-done((bf16[96,768]{1,0:T(8,128)(2,1)S(1)}, bf16[96,768]{1,0:T(8,128)(2,1)S(1)}, u32[]{:S(2)}, u32[]{:S(2)}) %collective-permute-start.44) | collective-permute-done | bytes 147488 | tf_op jit(solution)/shard_map/ppermute | solution.py:66
  434.5 3.6 collective-permute-start.45
  439.0 6.5 %fusion.5 = (f32[]{:T(128)}, f32[]{:T(128)}, f32[]{:T(128)}, f32[512,768]{1,0:T(8,128)}) fusion(f32[512]{0:T(512)S(1)} %convert_element_type.116, bf16[512,768]{1,0:T(8,128)(2,1)} %collective-permute-done.7, bf16[512,768]{1,0:T(8,128)(2,1)S(1)} %copy-done.7, f32[512,768]{1,0:T(8,128)} %copy-done.26, f32[512,768]{1,0:T(8,128)} %get-tuple-element.154, ...), kind=kLoop, calls=%fused_computation.17 | loop fusion | flops 9043965 | bytes 11014156 | tf_op jit(solution)/shard_map/reduce_sum | solution.py:1028
  445.5 2.7 maximum_bitcast_fusion
  450.3 3.0 collective-permute-done.32
  453.3 1.9 collective-permute-start.33
  456.7 3.0 collective-permute-done.33
  459.7 6.7 %collective-permute-done.34 = f32[29,768]{1,0:T(8,128)S(1)} collective-permute-done((f32[29,768]{1,0:T(8,128)S(1)}, f32[29,768]{1,0:T(8,128)S(1)}, u32[]{:S(2)}, u32[]{:S(2)}) %collective-permute-start.34) | collective-permute-done | bytes 89120 | tf_op jit(solution)/shard_map/ppermute | solution.py:66
  466.4 1.9 collective-permute-start.35
  468.3 2.8 subtract_add_fusion
  473.7 16.5 %widen.1 = (f32[36864,128]{1,0:T(8,128)}, f32[3072,768]{1,0:T(8,128)}) custom-call(bf16[6912,1024]{1,0:T(8,128)(2,1)} %all-gather.2.cloned.1.call-done.source), custom_call_target="tpu_custom_call" | custom-call | bytes 9000000 | tf_op jit(solution)/shard_map/widen/pallas_call | solution.py:775
  (373 shorter events, 81.8 us)
Async XLA Ops:
  7.2 21.0 %copy-start = (f32[2048,10]{0,1:T(8,128)S(1)}, f32[2048,10]{0,1:T(8,128)}, u32[]{:S(2)}) copy-start(f32[2048,10]{0,1:T(8,128)} %param.29) | copy-start | bytes 245764
  7.2 338.7 %reduce-scatter.2.cloned.1.call-start = ((), (), s32[]{:S(2)}) async-start(), calls=%async_computation.1 | async-start | bytes 15925248 | tf_op jit(solution)/shard_map/reduce_scatter | solution.py:926
  8.8 11.6 %collective-permute-start.1 = (bf16[96,768]{1,0:T(8,128)(2,1)S(1)}, bf16[96,768]{1,0:T(8,128)(2,1)S(1)}, u32[]{:S(2)}, u32[]{:S(2)}) collective-permute-start(bf16[96,768]{1,0:T(8,128)(2,1)S(1)} %constant_dynamic-slice_fusion.8), channel_id=1, source_target_pairs={{0,2},{1,3},{2,0},{3,1},{4,6},{5,7},{6,4},{7,5},{8,10},{9,11},{10,... | collective-permute-start | bytes 442376 | tf_op jit(solution)/shard_map/ppermute | solution.py:62
  13.9 43.1 %collective-permute-start = (bf16[512,768]{1,0:T(8,128)(2,1)S(1)}, bf16[512,768]{1,0:T(8,128)(2,1)}, u32[]{:S(2)}, u32[]{:S(2)}) collective-permute-start(bf16[512,768]{1,0:T(8,128)(2,1)S(1)} %multiply_convert_fusion.own), channel_id=1, source_target_pairs={{0,1},{1,0},{2,3},{3,2},{4,5},{5,4},{6,7},{7,6},{8,9},{9,8},{10,11... | collective-permute-start | bytes 2359304 | tf_op jit(solution)/shard_map/ppermute | solution.py:62
  20.1 36.9 %copy-start.1 = (s32[1024,1]{1,0:T(8,128)}, s32[1024,1]{1,0:T(8,128)S(1)}, u32[]{:S(2)}) copy-start(s32[1024,1]{1,0:T(8,128)S(1)} %copy.85.valid) | copy-start | bytes 12292
  22.8 29.1 %collective-permute-start.5 = (bf16[512,768]{1,0:T(8,128)(2,1)}, bf16[512,768]{1,0:T(8,128)(2,1)}, u32[]{:S(2)}, u32[]{:S(2)}) collective-permute-start(bf16[512,768]{1,0:T(8,128)(2,1)} %convert_element_type.106.refs_1_), channel_id=1, source_target_pairs={{0,1},{1,0},{2,3},{3,2},{4,5},{5,4},{6,7},{7,6},{8,9},{9,8},{10,11... | collective-permute-start | bytes 2359304 | tf_op jit(solution)/shard_map/ppermute | solution.py:62
  23.2 22.4 %collective-permute-start.6 = (bf16[512,768]{1,0:T(8,128)(2,1)}, bf16[512,768]{1,0:T(8,128)(2,1)}, u32[]{:S(2)}, u32[]{:S(2)}) collective-permute-start(bf16[512,768]{1,0:T(8,128)(2,1)} %convert_element_type.106.refs_1_), channel_id=1, source_target_pairs={{1,2},{2,1},{5,6},{6,5},{9,10},{10,9},{13,14},{14,13},{17,18},{18,... | collective-permute-start | bytes 2359304 | tf_op jit(solution)/shard_map/ppermute | solution.py:62
  26.6 30.4 %copy-start.8 = (s32[8,4,512]{2,0,1:T(8,128)}, s32[8,4,512]{2,0,1:T(8,128)S(1)}, u32[]{:S(2)}) copy-start(s32[8,4,512]{2,0,1:T(8,128)S(1)} %copy.94) | copy-start | bytes 196612
  26.6 6.9 %collective-permute-start.2 = (bf16[96,768]{1,0:T(8,128)(2,1)S(1)}, bf16[96,768]{1,0:T(8,128)(2,1)S(1)}, u32[]{:S(2)}, u32[]{:S(2)}) collective-permute-start(bf16[96,768]{1,0:T(8,128)(2,1)S(1)} %collective-permute-done.1), channel_id=1, source_target_pairs={{0,8},{4,12},{8,0},{12,4},{16,24},{20,28},{24,16},{28,20},{1,9},{5... | collective-permute-start | bytes 442376 | tf_op jit(solution)/shard_map/ppermute | solution.py:66
  34.5 8.3 %collective-permute-start.3 = (bf16[192,768]{1,0:T(8,128)(2,1)S(1)}, bf16[192,768]{1,0:T(8,128)(2,1)}, u32[]{:S(2)}, u32[]{:S(2)}) collective-permute-start(bf16[192,768]{1,0:T(8,128)(2,1)S(1)} %maximum_select_fusion.4), channel_id=1, source_target_pairs={{0,16},{4,20},{8,24},{12,28},{16,0},{20,4},{24,8},{28,12},{1,17},{... | collective-permute-start | bytes 884744 | tf_op jit(solution)/shard_map/ppermute | solution.py:66
  44.4 8.4 %collective-permute-start.4 = (bf16[384,768]{1,0:T(8,128)(2,1)S(1)}, bf16[384,768]{1,0:T(8,128)(2,1)}, u32[]{:S(2)}, u32[]{:S(2)}) collective-permute-start(bf16[384,768]{1,0:T(8,128)(2,1)S(1)} %maximum_select_fusion.2), channel_id=1, source_target_pairs={{0,4},{4,0},{8,12},{12,8},{16,20},{20,16},{24,28},{28,24},{1,5},{5... | collective-permute-start | bytes 1769480 | tf_op jit(solution)/shard_map/ppermute | solution.py:66
  45.7 36.5 %collective-permute-start.8 = (bf16[512,768]{1,0:T(8,128)(2,1)}, bf16[512,768]{1,0:T(8,128)(2,1)S(1)}, u32[]{:S(2)}, u32[]{:S(2)}) collective-permute-start(bf16[512,768]{1,0:T(8,128)(2,1)} %collective-permute-done.6.refs_4_.refs_1_), channel_id=1, source_target_pairs={{1,0},{2,3},{5,4},{6,7},{9,8},{10,11},{13,12},{14,15},{17,16},{18,... | collective-permute-start | bytes 2359304 | tf_op jit(solution)/shard_map/ppermute | solution.py:62
  51.9 30.2 %collective-permute-start.9 = (bf16[512,768]{1,0:T(8,128)(2,1)}, bf16[512,768]{1,0:T(8,128)(2,1)S(1)}, u32[]{:S(2)}, u32[]{:S(2)}) collective-permute-start(bf16[512,768]{1,0:T(8,128)(2,1)} %collective-permute-done.5.refs_3_.refs_1_), channel_id=1, source_target_pairs={{1,2},{2,1},{5,6},{6,5},{9,10},{10,9},{13,14},{14,13},{17,18},{18,... | collective-permute-start | bytes 2359304 | tf_op jit(solution)/shard_map/ppermute | solution.py:62
  79.3 20.6 %collective-permute-start.7 = (bf16[512,768]{1,0:T(8,128)(2,1)}, bf16[512,768]{1,0:T(8,128)(2,1)}, u32[]{:S(2)}, u32[]{:S(2)}) collective-permute-start(bf16[512,768]{1,0:T(8,128)(2,1)} %get-tuple-element.89), channel_id=1, source_target_pairs={{0,1},{1,0},{2,3},{3,2},{4,5},{5,4},{6,7},{7,6},{8,9},{9,8},{10,11... | collective-permute-start | bytes 2359304 | tf_op jit(solution)/shard_map/ppermute | solution.py:62
  104.8 26.6 %collective-permute-start.10 = (bf16[512,768]{1,0:T(8,128)(2,1)S(1)}, bf16[512,768]{1,0:T(8,128)(2,1)}, u32[]{:S(2)}, u32[]{:S(2)}) collective-permute-start(bf16[512,768]{1,0:T(8,128)(2,1)S(1)} %convert_element_type.109.refs_0_), channel_id=1, source_target_pairs={{0,1},{1,0},{2,3},{3,2},{4,5},{5,4},{6,7},{7,6},{8,9},{9,8},{10,11... | collective-permute-start | bytes 2359304 | tf_op jit(solution)/shard_map/ppermute | solution.py:62
  105.2 26.3 %collective-permute-start.11 = (bf16[512,768]{1,0:T(8,128)(2,1)S(1)}, bf16[512,768]{1,0:T(8,128)(2,1)}, u32[]{:S(2)}, u32[]{:S(2)}) collective-permute-start(bf16[512,768]{1,0:T(8,128)(2,1)S(1)} %convert_element_type.109.refs_0_), channel_id=1, source_target_pairs={{1,2},{2,1},{5,6},{6,5},{9,10},{10,9},{13,14},{14,13},{17,18},{18,... | collective-permute-start | bytes 2359304 | tf_op jit(solution)/shard_map/ppermute | solution.py:62
  107.8 22.9 %collective-permute-start.12 = (bf16[160,768]{1,0:T(8,128)(2,1)S(1)}, bf16[160,768]{1,0:T(8,128)(2,1)S(1)}, u32[]{:S(2)}, u32[]{:S(2)}) collective-permute-start(bf16[160,768]{1,0:T(8,128)(2,1)S(1)} %get-tuple-element.95), channel_id=1, source_target_pairs={{1,0},{2,3},{5,4},{6,7},{9,8},{10,11},{13,12},{14,15},{17,16},{18,... | collective-permute-start | bytes 737288 | tf_op jit(solution)/shard_map/ppermute | solution.py:62
  131.4 26.3 %collective-permute-start.14 = (bf16[512,768]{1,0:T(8,128)(2,1)}, bf16[512,768]{1,0:T(8,128)(2,1)}, u32[]{:S(2)}, u32[]{:S(2)}) collective-permute-start(bf16[512,768]{1,0:T(8,128)(2,1)} %collective-permute-done.11.refs_0_), channel_id=1, source_target_pairs={{1,0},{2,3},{5,4},{6,7},{9,8},{10,11},{13,12},{14,15},{17,16},{18,... | collective-permute-start | bytes 2359304 | tf_op jit(solution)/shard_map/ppermute | solution.py:62
  132.7 25.0 %collective-permute-start.15 = (bf16[512,768]{1,0:T(8,128)(2,1)}, bf16[512,768]{1,0:T(8,128)(2,1)}, u32[]{:S(2)}, u32[]{:S(2)}) collective-permute-start(bf16[512,768]{1,0:T(8,128)(2,1)} %collective-permute-done.10.refs_0_), channel_id=1, source_target_pairs={{1,2},{2,1},{5,6},{6,5},{9,10},{10,9},{13,14},{14,13},{17,18},{18,... | collective-permute-start | bytes 2359304 | tf_op jit(solution)/shard_map/ppermute | solution.py:62
  134.3 22.7 %collective-permute-start.16 = (bf16[160,768]{1,0:T(8,128)(2,1)S(1)}, bf16[160,768]{1,0:T(8,128)(2,1)S(1)}, u32[]{:S(2)}, u32[]{:S(2)}) collective-permute-start(bf16[160,768]{1,0:T(8,128)(2,1)S(1)} %get-tuple-element.104), channel_id=1, source_target_pairs={{1,0},{2,3},{5,4},{6,7},{9,8},{10,11},{13,12},{14,15},{17,16},{18,... | collective-permute-start | bytes 737288 | tf_op jit(solution)/shard_map/ppermute | solution.py:62
  157.7 26.3 %collective-permute-start.17 = (bf16[512,768]{1,0:T(8,128)(2,1)}, bf16[512,768]{1,0:T(8,128)(2,1)}, u32[]{:S(2)}, u32[]{:S(2)}) collective-permute-start(bf16[512,768]{1,0:T(8,128)(2,1)} %collective-permute-done.15.refs_0_), channel_id=1, source_target_pairs={{1,0},{2,3},{5,4},{6,7},{9,8},{10,11},{13,12},{14,15},{17,16},{18,... | collective-permute-start | bytes 2359304 | tf_op jit(solution)/shard_map/ppermute | solution.py:62
  160.7 23.4 %collective-permute-start.18 = (bf16[192,768]{1,0:T(8,128)(2,1)}, bf16[192,768]{1,0:T(8,128)(2,1)}, u32[]{:S(2)}, u32[]{:S(2)}) collective-permute-start(bf16[192,768]{1,0:T(8,128)(2,1)} %slice.135), channel_id=1, source_target_pairs={{1,0},{2,3},{5,4},{6,7},{9,8},{10,11},{13,12},{14,15},{17,16},{18,... | collective-permute-start | bytes 884744 | tf_op jit(solution)/shard_map/ppermute | solution.py:62
  164.2 19.8 %copy-start.12 = (bf16[160,768]{1,0:T(8,128)(2,1)S(1)}, bf16[160,768]{1,0:T(8,128)(2,1)}, u32[]{:S(2)}) copy-start(bf16[160,768]{1,0:T(8,128)(2,1)} %copy-done.11) | copy-start | bytes 737284
  164.2 19.8 %copy-start.14 = (bf16[160,768]{1,0:T(8,128)(2,1)S(1)}, bf16[160,768]{1,0:T(8,128)(2,1)}, u32[]{:S(2)}) copy-start(bf16[160,768]{1,0:T(8,128)(2,1)} %copy-done.13) | copy-start | bytes 737284
  203.6 23.6 %collective-permute-start.19 = (bf16[528,768]{1,0:T(8,128)(2,1)}, bf16[528,768]{1,0:T(8,128)(2,1)}, u32[]{:S(2)}, u32[]{:S(2)}) collective-permute-start(bf16[528,768]{1,0:T(8,128)(2,1)} %get-tuple-element.124), channel_id=1, source_target_pairs={{0,1},{3,2},{4,5},{7,6},{8,9},{11,10},{12,13},{15,14},{16,17},{19,... | collective-permute-start | bytes 2433032 | tf_op jit(solution)/shard_map/ppermute | solution.py:62
  227.3 246.4 %all-gather.2.cloned.1.call-start = ((), (), s32[]{:S(2)}) async-start(), calls=%async_computation.2 | async-start | bytes 15925248 | tf_op jit(solution)/shard_map/all_gather | solution.py:1037
  231.9 20.7 %collective-permute-start.23 = (bf16[528,768]{1,0:T(8,128)(2,1)}, bf16[528,768]{1,0:T(8,128)(2,1)}, u32[]{:S(2)}, u32[]{:S(2)}) collective-permute-start(bf16[528,768]{1,0:T(8,128)(2,1)} %get-tuple-element.114), channel_id=1, source_target_pairs={{0,1},{3,2},{4,5},{7,6},{8,9},{11,10},{12,13},{15,14},{16,17},{19,... | collective-permute-start | bytes 2433032 | tf_op jit(solution)/shard_map/ppermute | solution.py:62
  237.0 32.5 %collective-permute-start.21 = (bf16[512,768]{1,0:T(8,128)(2,1)}, bf16[512,768]{1,0:T(8,128)(2,1)}, u32[]{:S(2)}, u32[]{:S(2)}) collective-permute-start(bf16[512,768]{1,0:T(8,128)(2,1)} %get-tuple-element.130), channel_id=1, source_target_pairs={{0,1},{3,2},{4,5},{7,6},{8,9},{11,10},{12,13},{15,14},{16,17},{19,... | collective-permute-start | bytes 2359304 | tf_op jit(solution)/shard_map/ppermute | solution.py:62
  239.2 30.3 %collective-permute-start.20 = (bf16[528,768]{1,0:T(8,128)(2,1)}, bf16[528,768]{1,0:T(8,128)(2,1)}, u32[]{:S(2)}, u32[]{:S(2)}) collective-permute-start(bf16[528,768]{1,0:T(8,128)(2,1)} %add.361), channel_id=1, source_target_pairs={{1,2},{2,1},{5,6},{6,5},{9,10},{10,9},{13,14},{14,13},{17,18},{18,... | collective-permute-start | bytes 2433032 | tf_op jit(solution)/shard_map/ppermute | solution.py:62
  240.9 28.6 %copy-start.37 = (bf16[528,768]{1,0:T(8,128)(2,1)S(1)}, bf16[528,768]{1,0:T(8,128)(2,1)}, u32[]{:S(2)}) copy-start(bf16[528,768]{1,0:T(8,128)(2,1)} %get-tuple-element.105) | copy-start | bytes 2433028
  241.0 41.6 %collective-permute-start.22 = (bf16[528,768]{1,0:T(8,128)(2,1)}, bf16[528,768]{1,0:T(8,128)(2,1)S(1)}, u32[]{:S(2)}, u32[]{:S(2)}) collective-permute-start(bf16[528,768]{1,0:T(8,128)(2,1)} %get-tuple-element.105), channel_id=1, source_target_pairs={{0,1},{3,2},{4,5},{7,6},{8,9},{11,10},{12,13},{15,14},{16,17},{19,... | collective-permute-start | bytes 2433032 | tf_op jit(solution)/shard_map/ppermute | solution.py:62
  252.6 19.8 %copy-start.23 = (f32[512,768]{1,0:T(8,128)S(1)}, f32[512,768]{1,0:T(8,128)}, u32[]{:S(2)}) copy-start(f32[512,768]{1,0:T(8,128)} %param.18) | copy-start | bytes 4718596
  254.7 27.9 %collective-permute-start.24 = (bf16[528,768]{1,0:T(8,128)(2,1)S(1)}, bf16[528,768]{1,0:T(8,128)(2,1)S(1)}, u32[]{:S(2)}, u32[]{:S(2)}) collective-permute-start(bf16[528,768]{1,0:T(8,128)(2,1)S(1)} %add.364), channel_id=1, source_target_pairs={{1,2},{2,1},{5,6},{6,5},{9,10},{10,9},{13,14},{14,13},{17,18},{18,... | collective-permute-start | bytes 2433032 | tf_op jit(solution)/shard_map/ppermute | solution.py:62
  270.8 14.1 %collective-permute-start.25 = (bf16[528,768]{1,0:T(8,128)(2,1)S(1)}, bf16[528,768]{1,0:T(8,128)(2,1)S(1)}, u32[]{:S(2)}, u32[]{:S(2)}) collective-permute-start(bf16[528,768]{1,0:T(8,128)(2,1)S(1)} %add.366), channel_id=1, source_target_pairs={{1,0},{2,3},{5,4},{6,7},{9,8},{10,11},{13,12},{14,15},{17,16},{18,... | collective-permute-start | bytes 2433032 | tf_op jit(solution)/shard_map/ppermute | solution.py:62
  285.6 79.9 %copy-start.34 = (f32[512,10]{0,1:T(8,128)}, f32[512,10]{0,1:T(8,128)S(1)}, u32[]{:S(2)}) copy-start(f32[512,10]{0,1:T(8,128)S(1)} %select_reduce_fusion) | copy-start | bytes 61444
  291.1 14.0 %collective-permute-start.26 = (bf16[512,768]{1,0:T(8,128)(2,1)}, bf16[512,768]{1,0:T(8,128)(2,1)}, u32[]{:S(2)}, u32[]{:S(2)}) collective-permute-start(bf16[512,768]{1,0:T(8,128)(2,1)} %get-tuple-element.174.grad_own), channel_id=1, source_target_pairs={{0,1},{1,0},{2,3},{3,2},{4,5},{5,4},{6,7},{7,6},{8,9},{9,8},{10,11... | collective-permute-start | bytes 2359304 | tf_op jit(solution)/shard_map/ppermute | solution.py:62
  341.1 2.2 collective-permute-start.37
  349.0 13.7 %collective-permute-start.40 = (bf16[384,768]{1,0:T(8,128)(2,1)}, bf16[384,768]{1,0:T(8,128)(2,1)}, u32[]{:S(2)}, u32[]{:S(2)}) collective-permute-start(bf16[384,768]{1,0:T(8,128)(2,1)} %constant_dynamic-slice_fusion.2), channel_id=1, source_target_pairs={{0,4},{4,0},{8,12},{12,8},{16,20},{20,16},{24,28},{28,24},{1,5},{5... | collective-permute-start | bytes 1769480 | tf_op jit(solution)/shard_map/ppermute | solution.py:66
  351.5 21.6 %collective-permute-start.27 = (bf16[512,768]{1,0:T(8,128)(2,1)}, bf16[512,768]{1,0:T(8,128)(2,1)}, u32[]{:S(2)}, u32[]{:S(2)}) collective-permute-start(bf16[512,768]{1,0:T(8,128)(2,1)} %get-tuple-element.139), channel_id=1, source_target_pairs={{0,1},{3,2},{4,5},{7,6},{8,9},{11,10},{12,13},{15,14},{16,17},{19,... | collective-permute-start | bytes 2359304 | tf_op jit(solution)/shard_map/ppermute | solution.py:62
  355.8 21.2 %collective-permute-start.29 = (bf16[512,768]{1,0:T(8,128)(2,1)}, bf16[512,768]{1,0:T(8,128)(2,1)}, u32[]{:S(2)}, u32[]{:S(2)}) collective-permute-start(bf16[512,768]{1,0:T(8,128)(2,1)} %add.362), channel_id=1, source_target_pairs={{1,2},{2,1},{5,6},{6,5},{9,10},{10,9},{13,14},{14,13},{17,18},{18,... | collective-permute-start | bytes 2359304 | tf_op jit(solution)/shard_map/ppermute | solution.py:62
  359.1 79.0 %collective-permute-start.13 = (bf16[512,768]{1,0:T(8,128)(2,1)}, bf16[512,768]{1,0:T(8,128)(2,1)}, u32[]{:S(2)}, u32[]{:S(2)}) collective-permute-start(bf16[512,768]{1,0:T(8,128)(2,1)} %get-tuple-element.102), channel_id=1, source_target_pairs={{0,1},{3,2},{4,5},{7,6},{8,9},{11,10},{12,13},{15,14},{16,17},{19,... | collective-permute-start | bytes 2359304 | tf_op jit(solution)/shard_map/ppermute | solution.py:62
  364.2 16.6 %collective-permute-start.41 = (bf16[192,768]{1,0:T(8,128)(2,1)S(1)}, bf16[192,768]{1,0:T(8,128)(2,1)S(1)}, u32[]{:S(2)}, u32[]{:S(2)}) collective-permute-start(bf16[192,768]{1,0:T(8,128)(2,1)S(1)} %constant_dynamic-slice_fusion.1), channel_id=1, source_target_pairs={{0,8},{4,12},{8,0},{12,4},{16,24},{20,28},{24,16},{28,20},{1,9},{5... | collective-permute-start | bytes 884744 | tf_op jit(solution)/shard_map/ppermute | solution.py:66
  366.4 38.3 %collective-permute-start.38 = (bf16[192,768]{1,0:T(8,128)(2,1)S(1)}, bf16[192,768]{1,0:T(8,128)(2,1)S(1)}, u32[]{:S(2)}, u32[]{:S(2)}) collective-permute-start(bf16[192,768]{1,0:T(8,128)(2,1)S(1)} %constant_dynamic-slice_fusion.4), channel_id=1, source_target_pairs={{0,8},{4,12},{8,0},{12,4},{16,24},{20,28},{24,16},{28,20},{1,9},{5... | collective-permute-start | bytes 884744 | tf_op jit(solution)/shard_map/ppermute | solution.py:66
  375.5 62.6 %collective-permute-start.28 = (bf16[512,768]{1,0:T(8,128)(2,1)}, bf16[512,768]{1,0:T(8,128)(2,1)}, u32[]{:S(2)}, u32[]{:S(2)}) collective-permute-start(bf16[512,768]{1,0:T(8,128)(2,1)} %add.375), channel_id=1, source_target_pairs={{1,2},{2,1},{5,6},{6,5},{9,10},{10,9},{13,14},{14,13},{17,18},{18,... | collective-permute-start | bytes 2359304 | tf_op jit(solution)/shard_map/ppermute | solution.py:62
  379.4 35.9 %copy-start.35 = (f32[512,10]{0,1:T(8,128)S(1)}, f32[512,10]{0,1:T(8,128)}, u32[]{:S(2)}) copy-start(f32[512,10]{0,1:T(8,128)} %copy-done.34) | copy-start | bytes 61444
  379.4 58.7 %collective-permute-start.30 = (bf16[512,768]{1,0:T(8,128)(2,1)}, bf16[512,768]{1,0:T(8,128)(2,1)S(1)}, u32[]{:S(2)}, u32[]{:S(2)}) collective-permute-start(bf16[512,768]{1,0:T(8,128)(2,1)} %add.377), channel_id=1, source_target_pairs={{1,0},{2,3},{5,4},{6,7},{9,8},{10,11},{13,12},{14,15},{17,16},{18,... | collective-permute-start | bytes 2359304 | tf_op jit(solution)/shard_map/ppermute | solution.py:62
  380.9 43.8 %copy-start.55 = (f32[10,10]{1,0:T(8,128)S(1)}, f32[10,10]{1,0:T(8,128)}, u32[]{:S(2)}) copy-start(f32[10,10]{1,0:T(8,128)} %param.24) | copy-start | bytes 1204
  380.9 44.6 %copy-start.18 = (f32[8,768]{1,0:T(8,128)S(1)}, f32[8,768]{1,0:T(8,128)}, u32[]{:S(2)}) copy-start(f32[8,768]{1,0:T(8,128)} %copy-done.17) | copy-start | bytes 73732
  380.9 33.9 %collective-permute-start.42 = (bf16[96,768]{1,0:T(8,128)(2,1)S(1)}, bf16[96,768]{1,0:T(8,128)(2,1)S(1)}, u32[]{:S(2)}, u32[]{:S(2)}) collective-permute-start(bf16[96,768]{1,0:T(8,128)(2,1)S(1)} %constant_dynamic-slice_fusion), channel_id=1, source_target_pairs={{0,16},{4,20},{8,24},{12,28},{16,0},{20,4},{24,8},{28,12},{1,17},{... | collective-permute-start | bytes 442376 | tf_op jit(solution)/shard_map/ppermute | solution.py:66
  404.8 34.1 %copy-start.7 = (bf16[512,768]{1,0:T(8,128)(2,1)S(1)}, bf16[512,768]{1,0:T(8,128)(2,1)}, u32[]{:S(2)}) copy-start(bf16[512,768]{1,0:T(8,128)(2,1)} %copy-done.5) | copy-start | bytes 2359300
  404.8 34.1 %copy-start.65 = (f32[512]{0:T(512)S(1)}, f32[512]{0:T(512)}, u32[]{:S(2)}) copy-start(f32[512]{0:T(512)} %copy-done.64) | copy-start | bytes 6148
  404.8 13.9 %collective-permute-start.39 = (bf16[96,768]{1,0:T(8,128)(2,1)S(1)}, bf16[96,768]{1,0:T(8,128)(2,1)S(1)}, u32[]{:S(2)}, u32[]{:S(2)}) collective-permute-start(bf16[96,768]{1,0:T(8,128)(2,1)S(1)} %constant_dynamic-slice_fusion.3), channel_id=1, source_target_pairs={{0,16},{4,20},{8,24},{12,28},{16,0},{20,4},{24,8},{28,12},{1,17},{... | collective-permute-start | bytes 442376 | tf_op jit(solution)/shard_map/ppermute | solution.py:66
  414.9 9.4 %collective-permute-start.43 = (bf16[96,768]{1,0:T(8,128)(2,1)S(1)}, bf16[96,768]{1,0:T(8,128)(2,1)S(1)}, u32[]{:S(2)}, u32[]{:S(2)}) collective-permute-start(bf16[96,768]{1,0:T(8,128)(2,1)S(1)} %dynamic-slice_add_fusion.4), channel_id=1, source_target_pairs={{0,2},{1,3},{2,0},{3,1},{4,6},{5,7},{6,4},{7,5},{8,10},{9,11},{10,... | collective-permute-start | bytes 442376 | tf_op jit(solution)/shard_map/ppermute | solution.py:62
  424.4 9.3 %collective-permute-start.44 = (bf16[96,768]{1,0:T(8,128)(2,1)S(1)}, bf16[96,768]{1,0:T(8,128)(2,1)S(1)}, u32[]{:S(2)}, u32[]{:S(2)}) collective-permute-start(bf16[96,768]{1,0:T(8,128)(2,1)S(1)} %add_add_fusion.1), channel_id=1, source_target_pairs={{0,16},{4,20},{8,24},{12,28},{16,0},{20,4},{24,8},{28,12},{1,17},{... | collective-permute-start | bytes 442376 | tf_op jit(solution)/shard_map/ppermute | solution.py:66
  425.6 23.1 %collective-permute-start.31 = (bf16[512,768]{1,0:T(8,128)(2,1)}, bf16[512,768]{1,0:T(8,128)(2,1)}, u32[]{:S(2)}, u32[]{:S(2)}) collective-permute-start(bf16[512,768]{1,0:T(8,128)(2,1)} %get-tuple-element.141), channel_id=1, source_target_pairs={{0,1},{1,0},{2,3},{3,2},{4,5},{5,4},{6,7},{7,6},{8,9},{9,8},{10,11... | collective-permute-start | bytes 2359304 | tf_op jit(solution)/shard_map/ppermute | solution.py:62
  434.5 20.7 %collective-permute-start.45 = (bf16[192,768]{1,0:T(8,128)(2,1)}, bf16[192,768]{1,0:T(8,128)(2,1)}, u32[]{:S(2)}, u32[]{:S(2)}) collective-permute-start(bf16[192,768]{1,0:T(8,128)(2,1)} %maximum_select_fusion.5), channel_id=1, source_target_pairs={{0,8},{4,12},{8,0},{12,4},{16,24},{20,28},{24,16},{28,20},{1,9},{5... | collective-permute-start | bytes 884744 | tf_op jit(solution)/shard_map/ppermute | solution.py:66
  448.6 4.7 collective-permute-start.32
  450.3 18.1 %copy-start.28 = (f32[512,768]{1,0:T(8,128)S(1)}, f32[512,768]{1,0:T(8,128)}, u32[]{:S(2)}) copy-start(f32[512,768]{1,0:T(8,128)} %get-tuple-element.175) | copy-start | bytes 4718596
  450.3 18.1 %copy-start.63 = (f32[512]{0:T(512)S(1)}, f32[512]{0:T(512)}, u32[]{:S(2)}) copy-start(f32[512]{0:T(512)} %copy-done.62) | copy-start | bytes 6148
  453.3 6.3 %collective-permute-start.33 = (f32[29,768]{1,0:T(8,128)S(1)}, f32[29,768]{1,0:T(8,128)S(1)}, u32[]{:S(2)}, u32[]{:S(2)}) collective-permute-start(f32[29,768]{1,0:T(8,128)S(1)} %add.384), channel_id=1, source_target_pairs={{0,2},{1,3},{2,0},{3,1},{4,6},{5,7},{6,4},{7,5},{8,10},{9,11},{10,... | collective-permute-start | bytes 267272 | tf_op jit(solution)/shard_map/ppermute | solution.py:62
  456.6 14.7 %collective-permute-start.46 = (bf16[384,768]{1,0:T(8,128)(2,1)S(1)}, bf16[384,768]{1,0:T(8,128)(2,1)S(1)}, u32[]{:S(2)}, u32[]{:S(2)}) collective-permute-start(bf16[384,768]{1,0:T(8,128)(2,1)S(1)} %maximum_select_fusion.3), channel_id=1, source_target_pairs={{0,4},{4,0},{8,12},{12,8},{16,20},{20,16},{24,28},{28,24},{1,5},{5... | collective-permute-start | bytes 1769480 | tf_op jit(solution)/shard_map/ppermute | solution.py:66
  459.6 6.8 %collective-permute-start.34 = (f32[29,768]{1,0:T(8,128)S(1)}, f32[29,768]{1,0:T(8,128)S(1)}, u32[]{:S(2)}, u32[]{:S(2)}) collective-permute-start(f32[29,768]{1,0:T(8,128)S(1)} %add.385), channel_id=1, source_target_pairs={{0,8},{4,12},{8,0},{12,4},{16,24},{20,28},{24,16},{28,20},{1,9},{5... | collective-permute-start | bytes 267272 | tf_op jit(solution)/shard_map/ppermute | solution.py:66
  466.4 4.7 collective-permute-start.35
  471.2 19.0 %collective-permute-start.36 = (f32[29,768]{1,0:T(8,128)S(1)}, f32[29,768]{1,0:T(8,128)S(1)}, u32[]{:S(2)}, u32[]{:S(2)}) collective-permute-start(f32[29,768]{1,0:T(8,128)S(1)} %add.387), channel_id=1, source_target_pairs={{0,4},{4,0},{8,12},{12,8},{16,20},{20,16},{24,28},{28,24},{1,5},{5... | collective-permute-start | bytes 267272 | tf_op jit(solution)/shard_map/ppermute | solution.py:66
  (57 other events, 304.3 us)
Sparse Core Ops, SparseCore 0:
  227.4 118.4 reduce-scatter.1
  347.8 121.1 all-gather.1

commit v2 on v1

--- a/solution.py
+++ b/solution.py
@@ -1034,7 +1034,7 @@
     order = bits
     own_piece = reduce_blocks(own_grads.reshape(-1, width), order[:1], index, dp_size)
     far_piece = reduce_blocks(far_grads.reshape(-1, width), order[:1], index, dp_size)
-    packed = lax.all_gather(behind(packed, own_piece), "dp", axis=0, tiled=True)
+    packed = lax.all_gather(behind(packed, part_own), "dp", axis=0, tiled=True)
     own_piece = reduce_blocks(own_piece, order[1:], index, dp_size)
     far_piece = reduce_blocks(far_piece, order[1:], index, dp_size)
     own_piece = own_piece + along_z(far_piece, CROSS)

time: 510 us -> 515 us (level)
  waiting for transfers between devices: 97.5 us -> 124 us
  starting transfers between devices: 101 us -> 86.7 us
  other arithmetic: 62.6 us -> 56.7 us
    ppermute x32, waiting for transfers between devices: 71.2 us -> 96.4 us  [along_z(): return lax.ppermute(value, 'tensor', pairs)]
    ppermute x15, starting transfers between devices: 45.3 us -> 34.2 us  [along_dp(): return lax.ppermute(value, 'dp', [(i, i ^ 1 << bit) for i in range(size)])]
    reduce_scatter x1, waiting for transfers between devices: 1.37 us -> 10.3 us  [shards(): packed = lax.psum_scatter(packed, 'dp', scatter_dimension=0, tiled=True)]
    ppermute x15, waiting for transfers between devices: 24.8 us -> 16.9 us  [along_dp(): return lax.ppermute(value, 'dp', [(i, i ^ 1 << bit) for i in range(size)])]
    unnamed x148 -> x168, local copies, waits for them, and re-layouts: 14.1 us -> 16.9 us
  transfers between devices with their start and end apart: 49 -> 49, of which waited for: 18 -> 17; matrix products, arithmetic and copies ran while one was open for 21% -> 19% of each run, Pallas kernels for 28% -> 28%
where the time goes in v2:
time: 515 us; the launch traced here: 511 us
  Pallas kernels  162 us (31%)
  waiting for transfers between devices  124 us (24%)
  starting transfers between devices  86.7 us (17%)
  other arithmetic  56.7 us (11%)
  local copies, waits for them, and re-layouts  53.7 us (10%)
  between operations  17.1 us (3%)
  matrix products  11 us (2%)
    ppermute x32, waiting for transfers between devices, along_z(): return lax.ppermute(value, 'tensor', pairs)  96.4 us
    pallas_call x4, Pallas kernels, expert_chunk(): pl.pallas_call(functools.partial(expert_kernel, tiles, span, sources), gr...  76.5 us
    ppermute x32, starting transfers between devices, along_z(): return lax.ppermute(value, 'tensor', pairs)  52.5 us
    ppermute x15, starting transfers between devices, along_dp(): return lax.ppermute(value, 'dp', [(i, i ^ 1 << bit) for i in range(size)])  34.2 us
    pallas_call x1, Pallas kernels, attention_backward(): pl.pallas_call(attention_back_kernel, grid_spec=pltpu.PrefetchScalarGridS...  32.2 us
    pallas_call x1, Pallas kernels, attention_forward(): pl.pallas_call(attention_kernel, grid_spec=pltpu.PrefetchScalarGridSpec(n...  20.8 us
    ppermute x15, waiting for transfers between devices, along_dp(): return lax.ppermute(value, 'dp', [(i, i ^ 1 << bit) for i in range(size)])  16.9 us
    unnamed x168, local copies, waits for them, and re-layouts  16.9 us
  transfers between devices with their start and end apart: 49, of which 17 were waited for; matrix products, arithmetic and copies ran while one was open for 19% of the time, Pallas kernels for 28%

profile of v2, /device:TPU:0, one launch (start us, length us, event | category | flops | bytes accessed | tf_op | source)
XLA Modules:
  0.0 511.0 jit_solution(8602951034173287061)
XLA Ops:
  7.3 1.5 pad_maximum_fusion.1
  8.8 4.1 collective-permute-start.1
  13.9 1.6 collective-permute-start
  17.4 1.9 fusion.18
  20.9 2.4 convert_element_type.106.refs_1_
  23.7 1.5 collective-permute-start.6
  27.1 1.6 collective-permute-start.2
  31.8 2.3 pad.16.clone
  35.0 1.6 collective-permute-start.3
  37.7 5.1 %collective-permute-done.3 = bf16[192,768]{1,0:T(8,128)(2,1)} collective-permute-done((bf16[192,768]{1,0:T(8,128)(2,1)S(1)}, bf16[192,768]{1,0:T(8,128)(2,1)}, u32[]{:S(2)}, u32[]{:S(2)}) %collective-permute-start.3) | collective-permute-done | bytes 294944 | tf_op jit(solution)/shard_map/ppermute | solution.py:66
  42.9 1.4 maximum_select_fusion.2
  46.9 5.0 collective-permute-done.5.refs_3_.refs_1_
  52.8 1.6 maximum_select_fusion
  57.0 20.8 %attention_forward.1 = (bf16[512,768]{1,0:T(8,128)(2,1)S(1)}, bf16[512,768]{1,0:T(8,128)(2,1)}, bf16[1024,384]{1,0:T(8,128)(2,1)}, bf16[1024,384]{1,0:T(8,128)(2...) custom-call(s32[2]{0:T(128)S(1)} %pad_add_fusion.3.scalars, ...), custom_call_target="tpu_custom_call" | custom-call | bytes 60000000 | tf_op jit(solution)/shard_map/attention_forward/pallas_call | solution.py:210
  79.4 2.8 collective-permute-start.7
  84.0 16.0 %reshape.496.w_up_all = bf16[6,768,1024]{2,1,0:T(8,128)(2,1)} reshape(bf16[6,768,2,512]{3,2,1,0:T(2,128)(2,1)} %param.25) | data formatting | bytes 18874368 | tf_op jit(solution)/shard_map/reshape | solution.py:874
  100.0 2.1 multiply_reduce_fusion.6
  105.0 1.5 collective-permute-start.11
  111.8 19.0 %expert_chunk.4 = (bf16[528,768]{1,0:T(8,128)(2,1)}, bf16[512,768]{1,0:T(8,128)(2,1)}, bf16[6656,768]{1,0:T(8,128)(2,1)}, bf16[6656,512]{1,0:T(8,128)(2,1)}, bf1...) custom-call(s32[156]{0:T(256)S(1)} %reshape.492.refs_1_.meta, s32[2]{0:T(128)S(1)} %pad_add_fusion.2.chunk, ...), custom_call_target="tpu_custom_call" | custom-call | bytes 60000000 | tf_op jit(solution)/shard_map/expert_chunk/pallas_call | solution.py:549
  132.9 1.6 collective-permute-start.15
  136.4 18.8 %expert_chunk.5 = (bf16[528,768]{1,0:T(8,128)(2,1)}, bf16[512,768]{1,0:T(8,128)(2,1)}, bf16[6656,768]{1,0:T(8,128)(2,1)}, bf16[6656,512]{1,0:T(8,128)(2,1)}, bf1...) custom-call(s32[156]{0:T(256)S(1)} %reshape.492.refs_1_.meta, ...), custom_call_target="tpu_custom_call", output_to_operand_aliasing={{2}: (10, {}), {3}: (11, {}), {4}: (12, {}), {5}: (13, {})} | custom-call | bytes 60000000 | tf_op jit(solution)/shard_map/expert_chunk/pallas_call | solution.py:549
  155.3 2.0 collective-permute-done.16.refs_4_
  159.3 1.7 slice.135
  164.6 19.3 %expert_chunk.6 = (bf16[528,768]{1,0:T(8,128)(2,1)}, bf16[512,768]{1,0:T(8,128)(2,1)}, bf16[6656,768]{1,0:T(8,128)(2,1)}, bf16[6656,512]{1,0:T(8,128)(2,1)}, bf1...) custom-call(s32[156]{0:T(256)S(1)} %reshape.492.refs_1_.meta, ...), custom_call_target="tpu_custom_call", output_to_operand_aliasing={{2}: (12, {}), {3}: (13, {}), {4}: (14, {}), {5}: (15, {})} | custom-call | bytes 60000000 | tf_op jit(solution)/shard_map/expert_chunk/pallas_call | solution.py:549
  184.5 19.4 %expert_chunk.7 = (bf16[528,768]{1,0:T(8,128)(2,1)}, bf16[512,768]{1,0:T(8,128)(2,1)}, bf16[6656,768]{1,0:T(8,128)(2,1)}, bf16[6656,512]{1,0:T(8,128)(2,1)}, bf1...) custom-call(s32[156]{0:T(256)S(1)} %reshape.492.refs_1_.meta, ...), custom_call_target="tpu_custom_call", output_to_operand_aliasing={{2}: (14, {}), {3}: (15, {}), {4}: (16, {}), {5}: (17, {})} | custom-call | bytes 60000000 | tf_op jit(solution)/shard_map/expert_chunk/pallas_call | solution.py:549
  203.8 7.5 %collective-permute-start.19 = (bf16[528,768]{1,0:T(8,128)(2,1)}, bf16[528,768]{1,0:T(8,128)(2,1)}, u32[]{:S(2)}, u32[]{:S(2)}) collective-permute-start(bf16[528,768]{1,0:T(8,128)(2,1)} %get-tuple-element.124), channel_id=1, source_target_pairs={{0,1},{3,2},{4,5},{7,6},{8,9},{11,10},{12,13},{15,14},{16,17},{19,... | collective-permute-start | bytes 2433032 | tf_op jit(solution)/shard_map/ppermute | solution.py:62
  211.3 16.1 %weight_grads.1 = bf16[6912,1024]{1,0:T(8,128)(2,1)} custom-call(s32[103]{0:T(128)S(1)} %pad_add_fusion.4.refs_2_.walk, bf16[6656,768]{1,0:T(8,128)(2,1)} %get-tuple-element.125.refs_0_, bf16[6656,512]{1,0:T(8,128)(2,1)} %get-tuple-element.126.refs_1_, bf16[6656,768]{1,0:T(8,128)(2,1)} %get-tuple-element.127.refs_2_, ...), custom_call_target="tpu_custom_call" | custom-call | bytes 33000000 | tf_op jit(solution)/shard_map/weight_grads/pallas_call | solution.py:738
  229.3 2.8 fusion.11
  232.1 2.8 collective-permute-start.23
  234.9 2.3 add.361
  237.2 2.2 collective-permute-start.21
  239.4 1.6 collective-permute-start.20
  241.1 1.5 collective-permute-start.22
  242.6 10.2 %collective-permute-done.23 = bf16[528,768]{1,0:T(8,128)(2,1)} collective-permute-done((bf16[528,768]{1,0:T(8,128)(2,1)}, bf16[528,768]{1,0:T(8,128)(2,1)}, u32[]{:S(2)}, u32[]{:S(2)}) %collective-permute-start.23) | collective-permute-done | bytes 811040 | tf_op jit(solution)/shard_map/ppermute | solution.py:62
  252.8 1.7 add.364
  255.4 14.3 %collective-permute-done.21 = bf16[512,768]{1,0:T(8,128)(2,1)} collective-permute-done((bf16[512,768]{1,0:T(8,128)(2,1)}, bf16[512,768]{1,0:T(8,128)(2,1)}, u32[]{:S(2)}, u32[]{:S(2)}) %collective-permute-start.21) | collective-permute-done | bytes 786464 | tf_op jit(solution)/shard_map/ppermute | solution.py:62
  272.5 3.9 fusion.2
  276.5 6.3 %collective-permute-done.22 = bf16[528,768]{1,0:T(8,128)(2,1)S(1)} collective-permute-done((bf16[528,768]{1,0:T(8,128)(2,1)}, bf16[528,768]{1,0:T(8,128)(2,1)S(1)}, u32[]{:S(2)}, u32[]{:S(2)}) %collective-permute-start.22) | collective-permute-done | bytes 811040 | tf_op jit(solution)/shard_map/ppermute | solution.py:62
  282.7 2.5 collective-permute-done.25
  287.0 2.9 multiply_reduce_fusion.2
  289.9 1.7 fusion.45
  291.6 13.5 %collective-permute-done.26.grad_other = bf16[512,768]{1,0:T(8,128)(2,1)S(1)} collective-permute-done((bf16[512,768]{1,0:T(8,128)(2,1)S(1)}, bf16[512,768]{1,0:T(8,128)(2,1)S(1)}, u32[]{:S(2)}, u32[]{:S(2)}) %collective-permute-start.26) | collective-permute-done | bytes 786464 | tf_op jit(solution)/shard_map/ppermute | solution.py:62
  306.1 32.2 %attention_backward.1 = (bf16[512,768]{1,0:T(8,128)(2,1)S(1)}, bf16[512,768]{1,0:T(8,128)(2,1)}, bf16[3,384,768]{2,1,0:T(8,128)(2,1)}, bf16[384,768]{1,0:T(8,128)(2,1)S(1)}, f32[8,768]{1,0:T(8,128)S(1)}) custom-call(s32[2]{0:T(128)S(1)} %pad_add_fusion.3.scalars, bf16[512,768]{1,0:T(8,128)(2,1)S(1)} %multiply_convert_fusion.own, ...), custom_call_target="tpu_custom_call" | custom-call | bytes 96000000 | tf_op jit(solution)/shard_map/attention_backward/pallas_call | solution.py:309
  340.5 10.3 %reduce-scatter.2.cloned.1.call-done = bf16[864,1024]{1,0:T(8,128)(2,1)} async-done(((bf16[6912,1024]{1,0:T(8,128)(2,1)}), bf16[864,1024]{1,0:T(8,128)(2,1)}) %reduce-scatter.2.cloned.1.call-update) | async-done | bytes 1769488 | tf_op jit(solution)/shard_map/reduce_scatter | solution.py:926
  352.0 2.5 fusion.50
  357.4 4.4 collective-permute-start.13
  361.8 1.6 add.362
  363.4 1.5 collective-permute-start.27
  371.1 23.6 %collective-permute-done.27 = bf16[512,768]{1,0:T(8,128)(2,1)S(1)} collective-permute-done((bf16[512,768]{1,0:T(8,128)(2,1)S(1)}, bf16[512,768]{1,0:T(8,128)(2,1)S(1)}, u32[]{:S(2)}, u32[]{:S(2)}) %collective-permute-start.27) | collective-permute-done | bytes 786464 | tf_op jit(solution)/shard_map/ppermute | solution.py:62
  395.8 1.6 collective-permute-start.28
  401.6 9.0 %collective-permute-start.39 = (bf16[96,768]{1,0:T(8,128)(2,1)S(1)}, bf16[96,768]{1,0:T(8,128)(2,1)S(1)}, u32[]{:S(2)}, u32[]{:S(2)}) collective-permute-start(bf16[96,768]{1,0:T(8,128)(2,1)S(1)} %constant_dynamic-slice_fusion.3), channel_id=1, source_target_pairs={{0,16},{4,20},{8,24},{12,28},{16,0},{20,4},{24,8},{28,12},{1,17},{... | collective-permute-start | bytes 442376 | tf_op jit(solution)/shard_map/ppermute | solution.py:66
  410.6 2.5 collective-permute-start.43
  414.7 10.0 %collective-permute-done.43 = bf16[96,768]{1,0:T(8,128)(2,1)S(1)} collective-permute-done((bf16[96,768]{1,0:T(8,128)(2,1)S(1)}, bf16[96,768]{1,0:T(8,128)(2,1)S(1)}, u32[]{:S(2)}, u32[]{:S(2)}) %collective-permute-start.43) | collective-permute-done | bytes 147488 | tf_op jit(solution)/shard_map/ppermute | solution.py:62
  427.0 6.6 %collective-permute-done.44 = bf16[96,768]{1,0:T(8,128)(2,1)S(1)} collective-permute-done((bf16[96,768]{1,0:T(8,128)(2,1)S(1)}, bf16[96,768]{1,0:T(8,128)(2,1)S(1)}, u32[]{:S(2)}, u32[]{:S(2)}) %collective-permute-start.44) | collective-permute-done | bytes 147488 | tf_op jit(solution)/shard_map/ppermute | solution.py:66
  434.4 14.9 %collective-permute-start.45 = (bf16[192,768]{1,0:T(8,128)(2,1)}, bf16[192,768]{1,0:T(8,128)(2,1)}, u32[]{:S(2)}, u32[]{:S(2)}) collective-permute-start(bf16[192,768]{1,0:T(8,128)(2,1)} %maximum_select_fusion.5), channel_id=1, source_target_pairs={{0,8},{4,12},{8,0},{12,4},{16,24},{20,28},{24,16},{28,20},{1,9},{5... | collective-permute-start | bytes 884744 | tf_op jit(solution)/shard_map/ppermute | solution.py:66
  449.4 6.5 %fusion.5 = (f32[]{:T(128)}, f32[]{:T(128)}, f32[]{:T(128)}, f32[512,768]{1,0:T(8,128)}) fusion(f32[512]{0:T(512)S(1)} %copy-done.57, bf16[512,768]{1,0:T(8,128)(2,1)} %collective-permute-done.7, bf16[512,768]{1,0:T(8,128)(2,1)S(1)} %copy-done.7, f32[512,768]{1,0:T(8,128)} %copy-done.28, f32[512,768]{1,0:T(8,128)} %get-tuple-element.154, ...), kind=kLoop, calls=%fused_computation.17 | loop fusion | flops 9043965 | bytes 11014156 | tf_op jit(solution)/shard_map/reduce_sum | solution.py:1028
  455.9 2.7 maximum_bitcast_fusion
  459.1 1.5 multiply_reduce_fusion.3
  460.7 3.4 collective-permute-done.32
  465.7 5.0 collective-permute-done.33
  470.8 4.6 collective-permute-done.34
  475.4 1.8 collective-permute-start.35
  477.2 2.8 subtract_add_fusion
  482.6 16.5 %widen.1 = (f32[36864,128]{1,0:T(8,128)}, f32[3072,768]{1,0:T(8,128)}) custom-call(bf16[6912,1024]{1,0:T(8,128)(2,1)} %all-gather.2.cloned.1.call-done.source), custom_call_target="tpu_custom_call" | custom-call | bytes 9000000 | tf_op jit(solution)/shard_map/widen/pallas_call | solution.py:775
  (393 shorter events, 78.2 us)
Async XLA Ops:
  7.2 21.5 %copy-start = (f32[2048,10]{0,1:T(8,128)S(1)}, f32[2048,10]{0,1:T(8,128)}, u32[]{:S(2)}) copy-start(f32[2048,10]{0,1:T(8,128)} %param.29) | copy-start | bytes 245764
  7.2 343.7 %reduce-scatter.2.cloned.1.call-start = ((), (), s32[]{:S(2)}) async-start(), calls=%async_computation.1 | async-start | bytes 15925248 | tf_op jit(solution)/shard_map/reduce_scatter | solution.py:926
  8.8 12.1 %collective-permute-start.1 = (bf16[96,768]{1,0:T(8,128)(2,1)S(1)}, bf16[96,768]{1,0:T(8,128)(2,1)S(1)}, u32[]{:S(2)}, u32[]{:S(2)}) collective-permute-start(bf16[96,768]{1,0:T(8,128)(2,1)S(1)} %constant_dynamic-slice_fusion.8), channel_id=1, source_target_pairs={{0,2},{1,3},{2,0},{3,1},{4,6},{5,7},{6,4},{7,5},{8,10},{9,11},{10,... | collective-permute-start | bytes 442376 | tf_op jit(solution)/shard_map/ppermute | solution.py:62
  13.9 43.1 %collective-permute-start = (bf16[512,768]{1,0:T(8,128)(2,1)S(1)}, bf16[512,768]{1,0:T(8,128)(2,1)}, u32[]{:S(2)}, u32[]{:S(2)}) collective-permute-start(bf16[512,768]{1,0:T(8,128)(2,1)S(1)} %multiply_convert_fusion.own), channel_id=1, source_target_pairs={{0,1},{1,0},{2,3},{3,2},{4,5},{5,4},{6,7},{7,6},{8,9},{9,8},{10,11... | collective-permute-start | bytes 2359304 | tf_op jit(solution)/shard_map/ppermute | solution.py:62
  20.6 36.5 %copy-start.1 = (s32[1024,1]{1,0:T(8,128)}, s32[1024,1]{1,0:T(8,128)S(1)}, u32[]{:S(2)}) copy-start(s32[1024,1]{1,0:T(8,128)S(1)} %copy.85.valid) | copy-start | bytes 12292
  23.3 28.6 %collective-permute-start.5 = (bf16[512,768]{1,0:T(8,128)(2,1)}, bf16[512,768]{1,0:T(8,128)(2,1)}, u32[]{:S(2)}, u32[]{:S(2)}) collective-permute-start(bf16[512,768]{1,0:T(8,128)(2,1)} %convert_element_type.106.refs_1_), channel_id=1, source_target_pairs={{0,1},{1,0},{2,3},{3,2},{4,5},{5,4},{6,7},{7,6},{8,9},{9,8},{10,11... | collective-permute-start | bytes 2359304 | tf_op jit(solution)/shard_map/ppermute | solution.py:62
  23.7 21.9 %collective-permute-start.6 = (bf16[512,768]{1,0:T(8,128)(2,1)}, bf16[512,768]{1,0:T(8,128)(2,1)}, u32[]{:S(2)}, u32[]{:S(2)}) collective-permute-start(bf16[512,768]{1,0:T(8,128)(2,1)} %convert_element_type.106.refs_1_), channel_id=1, source_target_pairs={{1,2},{2,1},{5,6},{6,5},{9,10},{10,9},{13,14},{14,13},{17,18},{18,... | collective-permute-start | bytes 2359304 | tf_op jit(solution)/shard_map/ppermute | solution.py:62
  27.1 29.9 %copy-start.8 = (s32[8,4,512]{2,0,1:T(8,128)}, s32[8,4,512]{2,0,1:T(8,128)S(1)}, u32[]{:S(2)}) copy-start(s32[8,4,512]{2,0,1:T(8,128)S(1)} %copy.94) | copy-start | bytes 196612
  27.1 6.9 %collective-permute-start.2 = (bf16[96,768]{1,0:T(8,128)(2,1)S(1)}, bf16[96,768]{1,0:T(8,128)(2,1)S(1)}, u32[]{:S(2)}, u32[]{:S(2)}) collective-permute-start(bf16[96,768]{1,0:T(8,128)(2,1)S(1)} %collective-permute-done.1), channel_id=1, source_target_pairs={{0,8},{4,12},{8,0},{12,4},{16,24},{20,28},{24,16},{28,20},{1,9},{5... | collective-permute-start | bytes 442376 | tf_op jit(solution)/shard_map/ppermute | solution.py:66
  35.0 7.9 %collective-permute-start.3 = (bf16[192,768]{1,0:T(8,128)(2,1)S(1)}, bf16[192,768]{1,0:T(8,128)(2,1)}, u32[]{:S(2)}, u32[]{:S(2)}) collective-permute-start(bf16[192,768]{1,0:T(8,128)(2,1)S(1)} %maximum_select_fusion.4), channel_id=1, source_target_pairs={{0,16},{4,20},{8,24},{12,28},{16,0},{20,4},{24,8},{28,12},{1,17},{... | collective-permute-start | bytes 884744 | tf_op jit(solution)/shard_map/ppermute | solution.py:66
  44.3 8.5 %collective-permute-start.4 = (bf16[384,768]{1,0:T(8,128)(2,1)S(1)}, bf16[384,768]{1,0:T(8,128)(2,1)}, u32[]{:S(2)}, u32[]{:S(2)}) collective-permute-start(bf16[384,768]{1,0:T(8,128)(2,1)S(1)} %maximum_select_fusion.2), channel_id=1, source_target_pairs={{0,4},{4,0},{8,12},{12,8},{16,20},{20,16},{24,28},{28,24},{1,5},{5... | collective-permute-start | bytes 1769480 | tf_op jit(solution)/shard_map/ppermute | solution.py:66
  45.6 36.6 %collective-permute-start.8 = (bf16[512,768]{1,0:T(8,128)(2,1)}, bf16[512,768]{1,0:T(8,128)(2,1)S(1)}, u32[]{:S(2)}, u32[]{:S(2)}) collective-permute-start(bf16[512,768]{1,0:T(8,128)(2,1)} %collective-permute-done.6.refs_4_.refs_1_), channel_id=1, source_target_pairs={{1,0},{2,3},{5,4},{6,7},{9,8},{10,11},{13,12},{14,15},{17,16},{18,... | collective-permute-start | bytes 2359304 | tf_op jit(solution)/shard_map/ppermute | solution.py:62
  51.9 30.3 %collective-permute-start.9 = (bf16[512,768]{1,0:T(8,128)(2,1)}, bf16[512,768]{1,0:T(8,128)(2,1)S(1)}, u32[]{:S(2)}, u32[]{:S(2)}) collective-permute-start(bf16[512,768]{1,0:T(8,128)(2,1)} %collective-permute-done.5.refs_3_.refs_1_), channel_id=1, source_target_pairs={{1,2},{2,1},{5,6},{6,5},{9,10},{10,9},{13,14},{14,13},{17,18},{18,... | collective-permute-start | bytes 2359304 | tf_op jit(solution)/shard_map/ppermute | solution.py:62
  79.4 20.6 %collective-permute-start.7 = (bf16[512,768]{1,0:T(8,128)(2,1)}, bf16[512,768]{1,0:T(8,128)(2,1)}, u32[]{:S(2)}, u32[]{:S(2)}) collective-permute-start(bf16[512,768]{1,0:T(8,128)(2,1)} %get-tuple-element.89), channel_id=1, source_target_pairs={{0,1},{1,0},{2,3},{3,2},{4,5},{5,4},{6,7},{7,6},{8,9},{9,8},{10,11... | collective-permute-start | bytes 2359304 | tf_op jit(solution)/shard_map/ppermute | solution.py:62
  104.9 26.6 %collective-permute-start.10 = (bf16[512,768]{1,0:T(8,128)(2,1)S(1)}, bf16[512,768]{1,0:T(8,128)(2,1)}, u32[]{:S(2)}, u32[]{:S(2)}) collective-permute-start(bf16[512,768]{1,0:T(8,128)(2,1)S(1)} %convert_element_type.109.refs_0_), channel_id=1, source_target_pairs={{0,1},{1,0},{2,3},{3,2},{4,5},{5,4},{6,7},{7,6},{8,9},{9,8},{10,11... | collective-permute-start | bytes 2359304 | tf_op jit(solution)/shard_map/ppermute | solution.py:62
  105.0 26.5 %collective-permute-start.11 = (bf16[512,768]{1,0:T(8,128)(2,1)S(1)}, bf16[512,768]{1,0:T(8,128)(2,1)}, u32[]{:S(2)}, u32[]{:S(2)}) collective-permute-start(bf16[512,768]{1,0:T(8,128)(2,1)S(1)} %convert_element_type.109.refs_0_), channel_id=1, source_target_pairs={{1,2},{2,1},{5,6},{6,5},{9,10},{10,9},{13,14},{14,13},{17,18},{18,... | collective-permute-start | bytes 2359304 | tf_op jit(solution)/shard_map/ppermute | solution.py:62
  107.7 23.2 %collective-permute-start.12 = (bf16[160,768]{1,0:T(8,128)(2,1)S(1)}, bf16[160,768]{1,0:T(8,128)(2,1)S(1)}, u32[]{:S(2)}, u32[]{:S(2)}) collective-permute-start(bf16[160,768]{1,0:T(8,128)(2,1)S(1)} %get-tuple-element.95), channel_id=1, source_target_pairs={{1,0},{2,3},{5,4},{6,7},{9,8},{10,11},{13,12},{14,15},{17,16},{18,... | collective-permute-start | bytes 737288 | tf_op jit(solution)/shard_map/ppermute | solution.py:62
  131.6 26.4 %collective-permute-start.14 = (bf16[512,768]{1,0:T(8,128)(2,1)}, bf16[512,768]{1,0:T(8,128)(2,1)}, u32[]{:S(2)}, u32[]{:S(2)}) collective-permute-start(bf16[512,768]{1,0:T(8,128)(2,1)} %collective-permute-done.11.refs_0_), channel_id=1, source_target_pairs={{1,0},{2,3},{5,4},{6,7},{9,8},{10,11},{13,12},{14,15},{17,16},{18,... | collective-permute-start | bytes 2359304 | tf_op jit(solution)/shard_map/ppermute | solution.py:62
  132.9 25.2 %collective-permute-start.15 = (bf16[512,768]{1,0:T(8,128)(2,1)}, bf16[512,768]{1,0:T(8,128)(2,1)}, u32[]{:S(2)}, u32[]{:S(2)}) collective-permute-start(bf16[512,768]{1,0:T(8,128)(2,1)} %collective-permute-done.10.refs_0_), channel_id=1, source_target_pairs={{1,2},{2,1},{5,6},{6,5},{9,10},{10,9},{13,14},{14,13},{17,18},{18,... | collective-permute-start | bytes 2359304 | tf_op jit(solution)/shard_map/ppermute | solution.py:62
  134.4 22.9 %collective-permute-start.16 = (bf16[160,768]{1,0:T(8,128)(2,1)S(1)}, bf16[160,768]{1,0:T(8,128)(2,1)S(1)}, u32[]{:S(2)}, u32[]{:S(2)}) collective-permute-start(bf16[160,768]{1,0:T(8,128)(2,1)S(1)} %get-tuple-element.104), channel_id=1, source_target_pairs={{1,0},{2,3},{5,4},{6,7},{9,8},{10,11},{13,12},{14,15},{17,16},{18,... | collective-permute-start | bytes 737288 | tf_op jit(solution)/shard_map/ppermute | solution.py:62
  158.0 26.5 %collective-permute-start.17 = (bf16[512,768]{1,0:T(8,128)(2,1)}, bf16[512,768]{1,0:T(8,128)(2,1)}, u32[]{:S(2)}, u32[]{:S(2)}) collective-permute-start(bf16[512,768]{1,0:T(8,128)(2,1)} %collective-permute-done.15.refs_0_), channel_id=1, source_target_pairs={{1,0},{2,3},{5,4},{6,7},{9,8},{10,11},{13,12},{14,15},{17,16},{18,... | collective-permute-start | bytes 2359304 | tf_op jit(solution)/shard_map/ppermute | solution.py:62
  161.0 23.5 %collective-permute-start.18 = (bf16[192,768]{1,0:T(8,128)(2,1)}, bf16[192,768]{1,0:T(8,128)(2,1)}, u32[]{:S(2)}, u32[]{:S(2)}) collective-permute-start(bf16[192,768]{1,0:T(8,128)(2,1)} %slice.135), channel_id=1, source_target_pairs={{1,0},{2,3},{5,4},{6,7},{9,8},{10,11},{13,12},{14,15},{17,16},{18,... | collective-permute-start | bytes 884744 | tf_op jit(solution)/shard_map/ppermute | solution.py:62
  164.6 19.9 %copy-start.14 = (bf16[160,768]{1,0:T(8,128)(2,1)S(1)}, bf16[160,768]{1,0:T(8,128)(2,1)}, u32[]{:S(2)}) copy-start(bf16[160,768]{1,0:T(8,128)(2,1)} %copy-done.13) | copy-start | bytes 737284
  164.6 19.9 %copy-start.16 = (bf16[160,768]{1,0:T(8,128)(2,1)S(1)}, bf16[160,768]{1,0:T(8,128)(2,1)}, u32[]{:S(2)}) copy-start(bf16[160,768]{1,0:T(8,128)(2,1)} %copy-done.15) | copy-start | bytes 737284
  203.8 23.7 %collective-permute-start.19 = (bf16[528,768]{1,0:T(8,128)(2,1)}, bf16[528,768]{1,0:T(8,128)(2,1)}, u32[]{:S(2)}, u32[]{:S(2)}) collective-permute-start(bf16[528,768]{1,0:T(8,128)(2,1)} %get-tuple-element.124), channel_id=1, source_target_pairs={{0,1},{3,2},{4,5},{7,6},{8,9},{11,10},{12,13},{15,14},{16,17},{19,... | collective-permute-start | bytes 2433032 | tf_op jit(solution)/shard_map/ppermute | solution.py:62
  227.5 255.0 %all-gather.2.cloned.1.call-start = ((), (), s32[]{:S(2)}) async-start(), calls=%async_computation.2 | async-start | bytes 15925248 | tf_op jit(solution)/shard_map/all_gather | solution.py:1037
  227.6 58.2 %copy-start.56 = (f32[512]{0:T(512)}, f32[512]{0:T(512)S(1)}, u32[]{:S(2)}) copy-start(f32[512]{0:T(512)S(1)} %convert_element_type.116) | copy-start | bytes 6148
  232.1 20.7 %collective-permute-start.23 = (bf16[528,768]{1,0:T(8,128)(2,1)}, bf16[528,768]{1,0:T(8,128)(2,1)}, u32[]{:S(2)}, u32[]{:S(2)}) collective-permute-start(bf16[528,768]{1,0:T(8,128)(2,1)} %get-tuple-element.114), channel_id=1, source_target_pairs={{0,1},{3,2},{4,5},{7,6},{8,9},{11,10},{12,13},{15,14},{16,17},{19,... | collective-permute-start | bytes 2433032 | tf_op jit(solution)/shard_map/ppermute | solution.py:62
  237.2 32.5 %collective-permute-start.21 = (bf16[512,768]{1,0:T(8,128)(2,1)}, bf16[512,768]{1,0:T(8,128)(2,1)}, u32[]{:S(2)}, u32[]{:S(2)}) collective-permute-start(bf16[512,768]{1,0:T(8,128)(2,1)} %get-tuple-element.130), channel_id=1, source_target_pairs={{0,1},{3,2},{4,5},{7,6},{8,9},{11,10},{12,13},{15,14},{16,17},{19,... | collective-permute-start | bytes 2359304 | tf_op jit(solution)/shard_map/ppermute | solution.py:62
  239.4 30.3 %collective-permute-start.20 = (bf16[528,768]{1,0:T(8,128)(2,1)}, bf16[528,768]{1,0:T(8,128)(2,1)}, u32[]{:S(2)}, u32[]{:S(2)}) collective-permute-start(bf16[528,768]{1,0:T(8,128)(2,1)} %add.361), channel_id=1, source_target_pairs={{1,2},{2,1},{5,6},{6,5},{9,10},{10,9},{13,14},{14,13},{17,18},{18,... | collective-permute-start | bytes 2433032 | tf_op jit(solution)/shard_map/ppermute | solution.py:62
  241.0 28.6 %copy-start.39 = (bf16[528,768]{1,0:T(8,128)(2,1)S(1)}, bf16[528,768]{1,0:T(8,128)(2,1)}, u32[]{:S(2)}) copy-start(bf16[528,768]{1,0:T(8,128)(2,1)} %get-tuple-element.105) | copy-start | bytes 2433028
  241.1 41.6 %collective-permute-start.22 = (bf16[528,768]{1,0:T(8,128)(2,1)}, bf16[528,768]{1,0:T(8,128)(2,1)S(1)}, u32[]{:S(2)}, u32[]{:S(2)}) collective-permute-start(bf16[528,768]{1,0:T(8,128)(2,1)} %get-tuple-element.105), channel_id=1, source_target_pairs={{0,1},{3,2},{4,5},{7,6},{8,9},{11,10},{12,13},{15,14},{16,17},{19,... | collective-permute-start | bytes 2433032 | tf_op jit(solution)/shard_map/ppermute | solution.py:62
  254.5 28.2 %collective-permute-start.24 = (bf16[528,768]{1,0:T(8,128)(2,1)S(1)}, bf16[528,768]{1,0:T(8,128)(2,1)S(1)}, u32[]{:S(2)}, u32[]{:S(2)}) collective-permute-start(bf16[528,768]{1,0:T(8,128)(2,1)S(1)} %add.364), channel_id=1, source_target_pairs={{1,2},{2,1},{5,6},{6,5},{9,10},{10,9},{13,14},{14,13},{17,18},{18,... | collective-permute-start | bytes 2433032 | tf_op jit(solution)/shard_map/ppermute | solution.py:62
  271.0 14.1 %collective-permute-start.25 = (bf16[528,768]{1,0:T(8,128)(2,1)S(1)}, bf16[528,768]{1,0:T(8,128)(2,1)S(1)}, u32[]{:S(2)}, u32[]{:S(2)}) collective-permute-start(bf16[528,768]{1,0:T(8,128)(2,1)S(1)} %add.366), channel_id=1, source_target_pairs={{1,0},{2,3},{5,4},{6,7},{9,8},{10,11},{13,12},{14,15},{17,16},{18,... | collective-permute-start | bytes 2433032 | tf_op jit(solution)/shard_map/ppermute | solution.py:62
  285.9 80.0 %copy-start.36 = (f32[512,10]{0,1:T(8,128)}, f32[512,10]{0,1:T(8,128)S(1)}, u32[]{:S(2)}) copy-start(f32[512,10]{0,1:T(8,128)S(1)} %select_reduce_fusion) | copy-start | bytes 61444
  291.6 13.5 %collective-permute-start.26 = (bf16[512,768]{1,0:T(8,128)(2,1)S(1)}, bf16[512,768]{1,0:T(8,128)(2,1)S(1)}, u32[]{:S(2)}, u32[]{:S(2)}) collective-permute-start(bf16[512,768]{1,0:T(8,128)(2,1)S(1)} %get-tuple-element.174.grad_own), channel_id=1, source_target_pairs={{0,1},{1,0},{2,3},{3,2},{4,5},{5,4},{6,7},{7,6},{8,9},{9,8},{10,11... | collective-permute-start | bytes 2359304 | tf_op jit(solution)/shard_map/ppermute | solution.py:62
  354.6 12.9 %collective-permute-start.40 = (bf16[384,768]{1,0:T(8,128)(2,1)S(1)}, bf16[384,768]{1,0:T(8,128)(2,1)}, u32[]{:S(2)}, u32[]{:S(2)}) collective-permute-start(bf16[384,768]{1,0:T(8,128)(2,1)S(1)} %constant_dynamic-slice_fusion.2), channel_id=1, source_target_pairs={{0,4},{4,0},{8,12},{12,8},{16,20},{20,16},{24,28},{28,24},{1,5},{5... | collective-permute-start | bytes 1769480 | tf_op jit(solution)/shard_map/ppermute | solution.py:66
  357.4 91.9 %collective-permute-start.13 = (bf16[512,768]{1,0:T(8,128)(2,1)}, bf16[512,768]{1,0:T(8,128)(2,1)}, u32[]{:S(2)}, u32[]{:S(2)}) collective-permute-start(bf16[512,768]{1,0:T(8,128)(2,1)} %get-tuple-element.102), channel_id=1, source_target_pairs={{0,1},{3,2},{4,5},{7,6},{8,9},{11,10},{12,13},{15,14},{16,17},{19,... | collective-permute-start | bytes 2359304 | tf_op jit(solution)/shard_map/ppermute | solution.py:62
  363.4 31.4 %collective-permute-start.27 = (bf16[512,768]{1,0:T(8,128)(2,1)S(1)}, bf16[512,768]{1,0:T(8,128)(2,1)S(1)}, u32[]{:S(2)}, u32[]{:S(2)}) collective-permute-start(bf16[512,768]{1,0:T(8,128)(2,1)S(1)} %copy-done.43), channel_id=1, source_target_pairs={{0,1},{3,2},{4,5},{7,6},{8,9},{11,10},{12,13},{15,14},{16,17},{19,... | collective-permute-start | bytes 2359304 | tf_op jit(solution)/shard_map/ppermute | solution.py:62
  364.9 32.5 %collective-permute-start.29 = (bf16[512,768]{1,0:T(8,128)(2,1)S(1)}, bf16[512,768]{1,0:T(8,128)(2,1)S(1)}, u32[]{:S(2)}, u32[]{:S(2)}) collective-permute-start(bf16[512,768]{1,0:T(8,128)(2,1)S(1)} %add.362), channel_id=1, source_target_pairs={{1,2},{2,1},{5,6},{6,5},{9,10},{10,9},{13,14},{14,13},{17,18},{18,... | collective-permute-start | bytes 2359304 | tf_op jit(solution)/shard_map/ppermute | solution.py:62
  365.8 4.3 collective-permute-start.37
  368.7 31.1 %collective-permute-start.41 = (bf16[192,768]{1,0:T(8,128)(2,1)S(1)}, bf16[192,768]{1,0:T(8,128)(2,1)S(1)}, u32[]{:S(2)}, u32[]{:S(2)}) collective-permute-start(bf16[192,768]{1,0:T(8,128)(2,1)S(1)} %constant_dynamic-slice_fusion.1), channel_id=1, source_target_pairs={{0,8},{4,12},{8,0},{12,4},{16,24},{20,28},{24,16},{28,20},{1,9},{5... | collective-permute-start | bytes 884744 | tf_op jit(solution)/shard_map/ppermute | solution.py:66
  370.3 27.1 %copy-start.42 = (bf16[512,768]{1,0:T(8,128)(2,1)S(1)}, bf16[512,768]{1,0:T(8,128)(2,1)}, u32[]{:S(2)}) copy-start(bf16[512,768]{1,0:T(8,128)(2,1)} %get-tuple-element.102) | copy-start | bytes 2359300
  370.3 31.1 %collective-permute-start.38 = (bf16[192,768]{1,0:T(8,128)(2,1)S(1)}, bf16[192,768]{1,0:T(8,128)(2,1)S(1)}, u32[]{:S(2)}, u32[]{:S(2)}) collective-permute-start(bf16[192,768]{1,0:T(8,128)(2,1)S(1)} %constant_dynamic-slice_fusion.4), channel_id=1, source_target_pairs={{0,8},{4,12},{8,0},{12,4},{16,24},{20,28},{24,16},{28,20},{1,9},{5... | collective-permute-start | bytes 884744 | tf_op jit(solution)/shard_map/ppermute | solution.py:66
  395.8 53.4 %collective-permute-start.28 = (bf16[512,768]{1,0:T(8,128)(2,1)}, bf16[512,768]{1,0:T(8,128)(2,1)}, u32[]{:S(2)}, u32[]{:S(2)}) collective-permute-start(bf16[512,768]{1,0:T(8,128)(2,1)} %add.375), channel_id=1, source_target_pairs={{1,2},{2,1},{5,6},{6,5},{9,10},{10,9},{13,14},{14,13},{17,18},{18,... | collective-permute-start | bytes 2359304 | tf_op jit(solution)/shard_map/ppermute | solution.py:62
  398.5 50.8 %collective-permute-start.30 = (bf16[512,768]{1,0:T(8,128)(2,1)}, bf16[512,768]{1,0:T(8,128)(2,1)}, u32[]{:S(2)}, u32[]{:S(2)}) collective-permute-start(bf16[512,768]{1,0:T(8,128)(2,1)} %add.377), channel_id=1, source_target_pairs={{1,0},{2,3},{5,4},{6,7},{9,8},{10,11},{13,12},{14,15},{17,16},{18,... | collective-permute-start | bytes 2359304 | tf_op jit(solution)/shard_map/ppermute | solution.py:62
  400.0 26.1 %copy-start.65 = (f32[10,10]{1,0:T(8,128)S(1)}, f32[10,10]{1,0:T(8,128)}, u32[]{:S(2)}) copy-start(f32[10,10]{1,0:T(8,128)} %param.24) | copy-start | bytes 1204
  400.0 26.9 %copy-start.20 = (f32[8,768]{1,0:T(8,128)S(1)}, f32[8,768]{1,0:T(8,128)}, u32[]{:S(2)}) copy-start(f32[8,768]{1,0:T(8,128)} %copy-done.19) | copy-start | bytes 73732
  400.0 26.9 %copy-start.55 = (f32[768]{0:T(1024)S(1)}, f32[768]{0:T(1024)}, u32[]{:S(2)}) copy-start(f32[768]{0:T(1024)} %param.19) | copy-start | bytes 9220
  400.0 10.5 %collective-permute-start.42 = (bf16[96,768]{1,0:T(8,128)(2,1)S(1)}, bf16[96,768]{1,0:T(8,128)(2,1)S(1)}, u32[]{:S(2)}, u32[]{:S(2)}) collective-permute-start(bf16[96,768]{1,0:T(8,128)(2,1)S(1)} %constant_dynamic-slice_fusion), channel_id=1, source_target_pairs={{0,16},{4,20},{8,24},{12,28},{16,0},{20,4},{24,8},{28,12},{1,17},{... | collective-permute-start | bytes 442376 | tf_op jit(solution)/shard_map/ppermute | solution.py:66
  401.5 47.7 %copy-start.7 = (bf16[512,768]{1,0:T(8,128)(2,1)S(1)}, bf16[512,768]{1,0:T(8,128)(2,1)}, u32[]{:S(2)}) copy-start(bf16[512,768]{1,0:T(8,128)(2,1)} %copy-done.5) | copy-start | bytes 2359300
  401.5 47.7 %copy-start.57 = (f32[512]{0:T(512)S(1)}, f32[512]{0:T(512)}, u32[]{:S(2)}) copy-start(f32[512]{0:T(512)} %copy-done.56) | copy-start | bytes 6148
  401.5 47.7 %copy-start.73 = (f32[512]{0:T(512)S(1)}, f32[512]{0:T(512)}, u32[]{:S(2)}) copy-start(f32[512]{0:T(512)} %copy-done.72) | copy-start | bytes 6148
  401.6 13.1 %collective-permute-start.39 = (bf16[96,768]{1,0:T(8,128)(2,1)S(1)}, bf16[96,768]{1,0:T(8,128)(2,1)S(1)}, u32[]{:S(2)}, u32[]{:S(2)}) collective-permute-start(bf16[96,768]{1,0:T(8,128)(2,1)S(1)} %constant_dynamic-slice_fusion.3), channel_id=1, source_target_pairs={{0,16},{4,20},{8,24},{12,28},{16,0},{20,4},{24,8},{28,12},{1,17},{... | collective-permute-start | bytes 442376 | tf_op jit(solution)/shard_map/ppermute | solution.py:66
  410.6 14.0 %collective-permute-start.43 = (bf16[96,768]{1,0:T(8,128)(2,1)S(1)}, bf16[96,768]{1,0:T(8,128)(2,1)S(1)}, u32[]{:S(2)}, u32[]{:S(2)}) collective-permute-start(bf16[96,768]{1,0:T(8,128)(2,1)S(1)} %dynamic-slice_add_fusion.4), channel_id=1, source_target_pairs={{0,2},{1,3},{2,0},{3,1},{4,6},{5,7},{6,4},{7,5},{8,10},{9,11},{10,... | collective-permute-start | bytes 442376 | tf_op jit(solution)/shard_map/ppermute | solution.py:62
  424.7 8.9 %collective-permute-start.44 = (bf16[96,768]{1,0:T(8,128)(2,1)S(1)}, bf16[96,768]{1,0:T(8,128)(2,1)S(1)}, u32[]{:S(2)}, u32[]{:S(2)}) collective-permute-start(bf16[96,768]{1,0:T(8,128)(2,1)S(1)} %add_add_fusion.1), channel_id=1, source_target_pairs={{0,16},{4,20},{8,24},{12,28},{16,0},{20,4},{24,8},{28,12},{1,17},{... | collective-permute-start | bytes 442376 | tf_op jit(solution)/shard_map/ppermute | solution.py:66
  426.9 32.1 %collective-permute-start.31 = (bf16[512,768]{1,0:T(8,128)(2,1)}, bf16[512,768]{1,0:T(8,128)(2,1)}, u32[]{:S(2)}, u32[]{:S(2)}) collective-permute-start(bf16[512,768]{1,0:T(8,128)(2,1)} %get-tuple-element.141), channel_id=1, source_target_pairs={{0,1},{1,0},{2,3},{3,2},{4,5},{5,4},{6,7},{7,6},{8,9},{9,8},{10,11... | collective-permute-start | bytes 2359304 | tf_op jit(solution)/shard_map/ppermute | solution.py:62
  434.4 29.9 %collective-permute-start.45 = (bf16[192,768]{1,0:T(8,128)(2,1)}, bf16[192,768]{1,0:T(8,128)(2,1)}, u32[]{:S(2)}, u32[]{:S(2)}) collective-permute-start(bf16[192,768]{1,0:T(8,128)(2,1)} %maximum_select_fusion.5), channel_id=1, source_target_pairs={{0,8},{4,12},{8,0},{12,4},{16,24},{20,28},{24,16},{28,20},{1,9},{5... | collective-permute-start | bytes 884744 | tf_op jit(solution)/shard_map/ppermute | solution.py:66
  459.0 5.0 collective-permute-start.32
  464.1 6.6 %collective-permute-start.33 = (f32[29,768]{1,0:T(8,128)S(1)}, f32[29,768]{1,0:T(8,128)S(1)}, u32[]{:S(2)}, u32[]{:S(2)}) collective-permute-start(f32[29,768]{1,0:T(8,128)S(1)} %add.384), channel_id=1, source_target_pairs={{0,2},{1,3},{2,0},{3,1},{4,6},{5,7},{6,4},{7,5},{8,10},{9,11},{10,... | collective-permute-start | bytes 267272 | tf_op jit(solution)/shard_map/ppermute | solution.py:62
  465.6 14.6 %collective-permute-start.46 = (bf16[384,768]{1,0:T(8,128)(2,1)S(1)}, bf16[384,768]{1,0:T(8,128)(2,1)S(1)}, u32[]{:S(2)}, u32[]{:S(2)}) collective-permute-start(bf16[384,768]{1,0:T(8,128)(2,1)S(1)} %maximum_select_fusion.3), channel_id=1, source_target_pairs={{0,4},{4,0},{8,12},{12,8},{16,20},{20,16},{24,28},{28,24},{1,5},{5... | collective-permute-start | bytes 1769480 | tf_op jit(solution)/shard_map/ppermute | solution.py:66
  470.7 4.7 collective-permute-start.34
  475.4 4.7 collective-permute-start.35
  480.1 19.0 %collective-permute-start.36 = (f32[29,768]{1,0:T(8,128)S(1)}, f32[29,768]{1,0:T(8,128)S(1)}, u32[]{:S(2)}, u32[]{:S(2)}) collective-permute-start(f32[29,768]{1,0:T(8,128)S(1)} %add.387), channel_id=1, source_target_pairs={{0,4},{4,0},{8,12},{12,8},{16,20},{20,16},{24,28},{28,24},{1,5},{5... | collective-permute-start | bytes 267272 | tf_op jit(solution)/shard_map/ppermute | solution.py:66
  (67 other events, 408.7 us)
Sparse Core Ops, SparseCore 0:
  227.7 123.1 reduce-scatter.1
  352.8 109.1 all-gather.1

commit v3 on v1

--- a/solution.py
+++ b/solution.py
@@ -20,7 +20,7 @@
 TILE = 128
 QUERY_BLOCK = 1024
 GROUP = 4
-GATHER = 3
+GATHER = 2
 COST_FORWARD, COST_BACKWARD, COST_EXPERT, COST_GRADS, COST_WIDEN, COST_ADD = 20, 32, 20, 11, 3, 3
 
 

time: 510 us -> 511 us (level)
  transfers between devices with their start and end apart: 49 -> 49, of which waited for: 18 -> 18; matrix products, arithmetic and copies ran while one was open for 21% -> 20% of each run, Pallas kernels for 28% -> 28%
where the time goes in v3:
time: 511 us; the launch traced here: 505 us
  Pallas kernels  162 us (32%)
  starting transfers between devices  105 us (21%)
  waiting for transfers between devices  96.2 us (19%)
  other arithmetic  62.6 us (12%)
  local copies, waits for them, and re-layouts  52.1 us (10%)
  between operations  17.2 us (3%)
  matrix products  10.5 us (2%)
    pallas_call x4, Pallas kernels, expert_chunk(): pl.pallas_call(functools.partial(expert_kernel, tiles, span, sources), gr...  76.2 us
    ppermute x32, waiting for transfers between devices, along_z(): return lax.ppermute(value, 'tensor', pairs)  71.3 us
    ppermute x32, starting transfers between devices, along_z(): return lax.ppermute(value, 'tensor', pairs)  55.4 us
    ppermute x15, starting transfers between devices, along_dp(): return lax.ppermute(value, 'dp', [(i, i ^ 1 << bit) for i in range(size)])  49.3 us
    pallas_call x1, Pallas kernels, attention_backward(): pl.pallas_call(attention_back_kernel, grid_spec=pltpu.PrefetchScalarGridS...  32.1 us
    ppermute x15, waiting for transfers between devices, along_dp(): return lax.ppermute(value, 'dp', [(i, i ^ 1 << bit) for i in range(size)])  24.7 us
    pallas_call x1, Pallas kernels, attention_forward(): pl.pallas_call(attention_kernel, grid_spec=pltpu.PrefetchScalarGridSpec(n...  20.8 us
    pallas_call x1, Pallas kernels, widen(): pl.pallas_call(widen_kernel, grid=(EXP_FFN,), in_specs=[pl.BlockSpec((hei...  16.5 us
  transfers between devices with their start and end apart: 49, of which 18 were waited for; matrix products, arithmetic and copies ran while one was open for 20% of the time, Pallas kernels for 28%

profile of v3, /device:TPU:0, one launch (start us, length us, event | category | flops | bytes accessed | tf_op | source)
XLA Modules:
  0.0 505.1 jit_solution(13858053944865406289)
XLA Ops:
  8.8 4.1 collective-permute-start.1
  13.9 1.6 collective-permute-start
  17.0 1.9 fusion.18
  20.4 2.4 convert_element_type.106.refs_1_
  26.6 1.6 collective-permute-start.2
  31.3 2.3 pad.16.clone
  34.5 1.6 collective-permute-start.3
  37.2 5.6 %collective-permute-done.3 = bf16[192,768]{1,0:T(8,128)(2,1)} collective-permute-done((bf16[192,768]{1,0:T(8,128)(2,1)S(1)}, bf16[192,768]{1,0:T(8,128)(2,1)}, u32[]{:S(2)}, u32[]{:S(2)}) %collective-permute-start.3) | collective-permute-done | bytes 294944 | tf_op jit(solution)/shard_map/ppermute | solution.py:66
  47.0 5.0 collective-permute-done.5.refs_3_.refs_1_
  52.8 1.6 maximum_select_fusion
  57.0 20.8 %attention_forward.1 = (bf16[512,768]{1,0:T(8,128)(2,1)S(1)}, bf16[512,768]{1,0:T(8,128)(2,1)}, bf16[1024,384]{1,0:T(8,128)(2,1)}, bf16[1024,384]{1,0:T(8,128)(2...) custom-call(s32[2]{0:T(128)S(1)} %pad_add_fusion.3.scalars, ...), custom_call_target="tpu_custom_call" | custom-call | bytes 60000000 | tf_op jit(solution)/shard_map/attention_forward/pallas_call | solution.py:210
  79.4 2.8 collective-permute-start.7
  84.0 16.0 %reshape.496.w_up_all = bf16[6,768,1024]{2,1,0:T(8,128)(2,1)} reshape(bf16[6,768,2,512]{3,2,1,0:T(2,128)(2,1)} %param.25) | data formatting | bytes 18874368 | tf_op jit(solution)/shard_map/reshape | solution.py:874
  100.0 2.1 multiply_reduce_fusion.6
  105.2 1.6 collective-permute-start.11
  111.9 19.0 %expert_chunk.4 = (bf16[528,768]{1,0:T(8,128)(2,1)}, bf16[512,768]{1,0:T(8,128)(2,1)}, bf16[6656,768]{1,0:T(8,128)(2,1)}, bf16[6656,512]{1,0:T(8,128)(2,1)}, bf1...) custom-call(s32[156]{0:T(256)S(1)} %reshape.492.refs_1_.meta, s32[2]{0:T(128)S(1)} %pad_add_fusion.2.chunk, ...), custom_call_target="tpu_custom_call" | custom-call | bytes 60000000 | tf_op jit(solution)/shard_map/expert_chunk/pallas_call | solution.py:549
  132.9 1.6 collective-permute-start.15
  136.4 18.8 %expert_chunk.5 = (bf16[528,768]{1,0:T(8,128)(2,1)}, bf16[512,768]{1,0:T(8,128)(2,1)}, bf16[6656,768]{1,0:T(8,128)(2,1)}, bf16[6656,512]{1,0:T(8,128)(2,1)}, bf1...) custom-call(s32[156]{0:T(256)S(1)} %reshape.492.refs_1_.meta, ...), custom_call_target="tpu_custom_call", output_to_operand_aliasing={{2}: (10, {}), {3}: (11, {}), {4}: (12, {}), {5}: (13, {})} | custom-call | bytes 60000000 | tf_op jit(solution)/shard_map/expert_chunk/pallas_call | solution.py:549
  155.2 2.0 collective-permute-done.16.refs_4_
  159.2 1.7 slice.135
  164.5 19.2 %expert_chunk.6 = (bf16[528,768]{1,0:T(8,128)(2,1)}, bf16[512,768]{1,0:T(8,128)(2,1)}, bf16[6656,768]{1,0:T(8,128)(2,1)}, bf16[6656,512]{1,0:T(8,128)(2,1)}, bf1...) custom-call(s32[156]{0:T(256)S(1)} %reshape.492.refs_1_.meta, ...), custom_call_target="tpu_custom_call", output_to_operand_aliasing={{2}: (12, {}), {3}: (13, {}), {4}: (14, {}), {5}: (15, {})} | custom-call | bytes 60000000 | tf_op jit(solution)/shard_map/expert_chunk/pallas_call | solution.py:549
  184.2 19.2 %expert_chunk.7 = (bf16[528,768]{1,0:T(8,128)(2,1)}, bf16[512,768]{1,0:T(8,128)(2,1)}, bf16[6656,768]{1,0:T(8,128)(2,1)}, bf16[6656,512]{1,0:T(8,128)(2,1)}, bf1...) custom-call(s32[156]{0:T(256)S(1)} %reshape.492.refs_1_.meta, ...), custom_call_target="tpu_custom_call", output_to_operand_aliasing={{2}: (14, {}), {3}: (15, {}), {4}: (16, {}), {5}: (17, {})} | custom-call | bytes 60000000 | tf_op jit(solution)/shard_map/expert_chunk/pallas_call | solution.py:549
  203.5 7.4 %collective-permute-start.19 = (bf16[528,768]{1,0:T(8,128)(2,1)}, bf16[528,768]{1,0:T(8,128)(2,1)}, u32[]{:S(2)}, u32[]{:S(2)}) collective-permute-start(bf16[528,768]{1,0:T(8,128)(2,1)} %get-tuple-element.124), channel_id=1, source_target_pairs={{0,1},{3,2},{4,5},{7,6},{8,9},{11,10},{12,13},{15,14},{16,17},{19,... | collective-permute-start | bytes 2433032 | tf_op jit(solution)/shard_map/ppermute | solution.py:62
  210.8 16.1 %weight_grads.1 = bf16[6912,1024]{1,0:T(8,128)(2,1)} custom-call(s32[103]{0:T(128)S(1)} %pad_add_fusion.4.refs_2_.walk, bf16[6656,768]{1,0:T(8,128)(2,1)} %get-tuple-element.125.refs_0_, bf16[6656,512]{1,0:T(8,128)(2,1)} %get-tuple-element.126.refs_1_, bf16[6656,768]{1,0:T(8,128)(2,1)} %get-tuple-element.127.refs_2_, ...), custom_call_target="tpu_custom_call" | custom-call | bytes 33000000 | tf_op jit(solution)/shard_map/weight_grads/pallas_call | solution.py:738
  228.9 2.8 fusion.11
  231.7 2.8 collective-permute-start.23
  234.5 2.3 add.361
  236.7 2.2 collective-permute-start.21
  238.9 1.6 collective-permute-start.20
  242.2 10.2 %collective-permute-done.23 = bf16[528,768]{1,0:T(8,128)(2,1)} collective-permute-done((bf16[528,768]{1,0:T(8,128)(2,1)}, bf16[528,768]{1,0:T(8,128)(2,1)}, u32[]{:S(2)}, u32[]{:S(2)}) %collective-permute-start.23) | collective-permute-done | bytes 811040 | tf_op jit(solution)/shard_map/ppermute | solution.py:62
  252.4 2.2 add.364
  255.5 13.7 %collective-permute-done.21 = bf16[512,768]{1,0:T(8,128)(2,1)} collective-permute-done((bf16[512,768]{1,0:T(8,128)(2,1)}, bf16[512,768]{1,0:T(8,128)(2,1)}, u32[]{:S(2)}, u32[]{:S(2)}) %collective-permute-start.21) | collective-permute-done | bytes 786464 | tf_op jit(solution)/shard_map/ppermute | solution.py:62
  272.0 3.9 fusion.2
  276.0 6.4 %collective-permute-done.22 = bf16[528,768]{1,0:T(8,128)(2,1)S(1)} collective-permute-done((bf16[528,768]{1,0:T(8,128)(2,1)}, bf16[528,768]{1,0:T(8,128)(2,1)S(1)}, u32[]{:S(2)}, u32[]{:S(2)}) %collective-permute-start.22) | collective-permute-done | bytes 811040 | tf_op jit(solution)/shard_map/ppermute | solution.py:62
  282.4 2.4 collective-permute-done.25
  286.6 2.4 multiply_reduce_fusion.2
  288.9 1.9 fusion.45
  290.9 14.0 %collective-permute-done.26.grad_other = bf16[512,768]{1,0:T(8,128)(2,1)} collective-permute-done((bf16[512,768]{1,0:T(8,128)(2,1)}, bf16[512,768]{1,0:T(8,128)(2,1)}, u32[]{:S(2)}, u32[]{:S(2)}) %collective-permute-start.26) | collective-permute-done | bytes 786464 | tf_op jit(solution)/shard_map/ppermute | solution.py:62
  305.9 32.1 %attention_backward.1 = (bf16[512,768]{1,0:T(8,128)(2,1)S(1)}, bf16[512,768]{1,0:T(8,128)(2,1)}, bf16[3,384,768]{2,1,0:T(8,128)(2,1)}, bf16[384,768]{1,0:T(8,128)(2,1)S(1)}, f32[8,768]{1,0:T(8,128)S(1)}) custom-call(s32[2]{0:T(128)S(1)} %pad_add_fusion.3.scalars, bf16[512,768]{1,0:T(8,128)(2,1)S(1)} %multiply_convert_fusion.own, ...), custom_call_target="tpu_custom_call" | custom-call | bytes 96000000 | tf_op jit(solution)/shard_map/attention_backward/pallas_call | solution.py:309
  338.0 2.7 fusion.50
  341.0 2.1 collective-permute-done.37
  347.7 2.4 add.362
  350.2 4.6 collective-permute-start.27
  354.8 1.8 collective-permute-start.29
  358.1 3.4 collective-permute-start.13
  366.5 5.6 %collective-permute-done.27 = bf16[512,768]{1,0:T(8,128)(2,1)} collective-permute-done((bf16[512,768]{1,0:T(8,128)(2,1)}, bf16[512,768]{1,0:T(8,128)(2,1)}, u32[]{:S(2)}, u32[]{:S(2)}) %collective-permute-start.27) | collective-permute-done | bytes 786464 | tf_op jit(solution)/shard_map/ppermute | solution.py:62
  372.1 2.4 add.375
  374.5 1.5 collective-permute-start.28
  376.0 2.2 add.377
  379.8 27.7 %collective-permute-start.42 = (bf16[96,768]{1,0:T(8,128)(2,1)S(1)}, bf16[96,768]{1,0:T(8,128)(2,1)S(1)}, u32[]{:S(2)}, u32[]{:S(2)}) collective-permute-start(bf16[96,768]{1,0:T(8,128)(2,1)S(1)} %constant_dynamic-slice_fusion), channel_id=1, source_target_pairs={{0,16},{4,20},{8,24},{12,28},{16,0},{20,4},{24,8},{28,12},{1,17},{... | collective-permute-start | bytes 442376 | tf_op jit(solution)/shard_map/ppermute | solution.py:66
  407.7 10.0 %collective-permute-start.39 = (bf16[96,768]{1,0:T(8,128)(2,1)S(1)}, bf16[96,768]{1,0:T(8,128)(2,1)S(1)}, u32[]{:S(2)}, u32[]{:S(2)}) collective-permute-start(bf16[96,768]{1,0:T(8,128)(2,1)S(1)} %constant_dynamic-slice_fusion.3), channel_id=1, source_target_pairs={{0,16},{4,20},{8,24},{12,28},{16,0},{20,4},{24,8},{28,12},{1,17},{... | collective-permute-start | bytes 442376 | tf_op jit(solution)/shard_map/ppermute | solution.py:66
  419.2 2.3 collective-permute-done.39
  421.5 5.6 %collective-permute-done.43 = bf16[96,768]{1,0:T(8,128)(2,1)S(1)} collective-permute-done((bf16[96,768]{1,0:T(8,128)(2,1)S(1)}, bf16[96,768]{1,0:T(8,128)(2,1)S(1)}, u32[]{:S(2)}, u32[]{:S(2)}) %collective-permute-start.43) | collective-permute-done | bytes 147488 | tf_op jit(solution)/shard_map/ppermute | solution.py:62
  428.5 8.0 %collective-permute-done.44 = bf16[96,768]{1,0:T(8,128)(2,1)S(1)} collective-permute-done((bf16[96,768]{1,0:T(8,128)(2,1)S(1)}, bf16[96,768]{1,0:T(8,128)(2,1)S(1)}, u32[]{:S(2)}, u32[]{:S(2)}) %collective-permute-start.44) | collective-permute-done | bytes 147488 | tf_op jit(solution)/shard_map/ppermute | solution.py:66
  437.3 3.6 collective-permute-start.45
  441.8 6.5 %fusion.5 = (f32[]{:T(128)}, f32[]{:T(128)}, f32[]{:T(128)}, f32[512,768]{1,0:T(8,128)}) fusion(f32[512]{0:T(512)S(1)} %convert_element_type.116, bf16[512,768]{1,0:T(8,128)(2,1)} %collective-permute-done.7, bf16[512,768]{1,0:T(8,128)(2,1)S(1)} %copy-done.7, f32[512,768]{1,0:T(8,128)} %copy-done.26, f32[512,768]{1,0:T(8,128)} %get-tuple-element.154, ...), kind=kLoop, calls=%fused_computation.17 | loop fusion | flops 9043965 | bytes 11014156 | tf_op jit(solution)/shard_map/reduce_sum | solution.py:1028
  448.3 2.7 maximum_bitcast_fusion
  453.1 3.0 collective-permute-done.32
  456.2 1.9 collective-permute-start.33
  459.5 2.9 collective-permute-done.33
  462.6 6.7 %collective-permute-done.34 = f32[29,768]{1,0:T(8,128)S(1)} collective-permute-done((f32[29,768]{1,0:T(8,128)S(1)}, f32[29,768]{1,0:T(8,128)S(1)}, u32[]{:S(2)}, u32[]{:S(2)}) %collective-permute-start.34) | collective-permute-done | bytes 89120 | tf_op jit(solution)/shard_map/ppermute | solution.py:66
  469.2 1.9 collective-permute-start.35
  471.2 2.8 subtract_add_fusion
  476.5 16.5 %widen.1 = (f32[36864,128]{1,0:T(8,128)}, f32[3072,768]{1,0:T(8,128)}) custom-call(bf16[6912,1024]{1,0:T(8,128)(2,1)} %all-gather.2.cloned.1.call-done.source), custom_call_target="tpu_custom_call" | custom-call | bytes 9000000 | tf_op jit(solution)/shard_map/widen/pallas_call | solution.py:775
  (373 shorter events, 80.3 us)
Async XLA Ops:
  7.2 21.0 %copy-start = (f32[2048,10]{0,1:T(8,128)S(1)}, f32[2048,10]{0,1:T(8,128)}, u32[]{:S(2)}) copy-start(f32[2048,10]{0,1:T(8,128)} %param.29) | copy-start | bytes 245764
  7.2 337.2 %reduce-scatter.2.cloned.1.call-start = ((), (), s32[]{:S(2)}) async-start(), calls=%async_computation.1 | async-start | bytes 15925248 | tf_op jit(solution)/shard_map/reduce_scatter | solution.py:926
  8.8 11.6 %collective-permute-start.1 = (bf16[96,768]{1,0:T(8,128)(2,1)S(1)}, bf16[96,768]{1,0:T(8,128)(2,1)S(1)}, u32[]{:S(2)}, u32[]{:S(2)}) collective-permute-start(bf16[96,768]{1,0:T(8,128)(2,1)S(1)} %constant_dynamic-slice_fusion.8), channel_id=1, source_target_pairs={{0,2},{1,3},{2,0},{3,1},{4,6},{5,7},{6,4},{7,5},{8,10},{9,11},{10,... | collective-permute-start | bytes 442376 | tf_op jit(solution)/shard_map/ppermute | solution.py:62
  13.9 43.1 %collective-permute-start = (bf16[512,768]{1,0:T(8,128)(2,1)S(1)}, bf16[512,768]{1,0:T(8,128)(2,1)}, u32[]{:S(2)}, u32[]{:S(2)}) collective-permute-start(bf16[512,768]{1,0:T(8,128)(2,1)S(1)} %multiply_convert_fusion.own), channel_id=1, source_target_pairs={{0,1},{1,0},{2,3},{3,2},{4,5},{5,4},{6,7},{7,6},{8,9},{9,8},{10,11... | collective-permute-start | bytes 2359304 | tf_op jit(solution)/shard_map/ppermute | solution.py:62
  20.1 36.9 %copy-start.1 = (s32[1024,1]{1,0:T(8,128)}, s32[1024,1]{1,0:T(8,128)S(1)}, u32[]{:S(2)}) copy-start(s32[1024,1]{1,0:T(8,128)S(1)} %copy.85.valid) | copy-start | bytes 12292
  22.8 29.1 %collective-permute-start.5 = (bf16[512,768]{1,0:T(8,128)(2,1)}, bf16[512,768]{1,0:T(8,128)(2,1)}, u32[]{:S(2)}, u32[]{:S(2)}) collective-permute-start(bf16[512,768]{1,0:T(8,128)(2,1)} %convert_element_type.106.refs_1_), channel_id=1, source_target_pairs={{0,1},{1,0},{2,3},{3,2},{4,5},{5,4},{6,7},{7,6},{8,9},{9,8},{10,11... | collective-permute-start | bytes 2359304 | tf_op jit(solution)/shard_map/ppermute | solution.py:62
  23.2 22.4 %collective-permute-start.6 = (bf16[512,768]{1,0:T(8,128)(2,1)}, bf16[512,768]{1,0:T(8,128)(2,1)}, u32[]{:S(2)}, u32[]{:S(2)}) collective-permute-start(bf16[512,768]{1,0:T(8,128)(2,1)} %convert_element_type.106.refs_1_), channel_id=1, source_target_pairs={{1,2},{2,1},{5,6},{6,5},{9,10},{10,9},{13,14},{14,13},{17,18},{18,... | collective-permute-start | bytes 2359304 | tf_op jit(solution)/shard_map/ppermute | solution.py:62
  26.6 30.4 %copy-start.8 = (s32[8,4,512]{2,0,1:T(8,128)}, s32[8,4,512]{2,0,1:T(8,128)S(1)}, u32[]{:S(2)}) copy-start(s32[8,4,512]{2,0,1:T(8,128)S(1)} %copy.94) | copy-start | bytes 196612
  26.6 6.9 %collective-permute-start.2 = (bf16[96,768]{1,0:T(8,128)(2,1)S(1)}, bf16[96,768]{1,0:T(8,128)(2,1)S(1)}, u32[]{:S(2)}, u32[]{:S(2)}) collective-permute-start(bf16[96,768]{1,0:T(8,128)(2,1)S(1)} %collective-permute-done.1), channel_id=1, source_target_pairs={{0,8},{4,12},{8,0},{12,4},{16,24},{20,28},{24,16},{28,20},{1,9},{5... | collective-permute-start | bytes 442376 | tf_op jit(solution)/shard_map/ppermute | solution.py:66
  34.5 8.3 %collective-permute-start.3 = (bf16[192,768]{1,0:T(8,128)(2,1)S(1)}, bf16[192,768]{1,0:T(8,128)(2,1)}, u32[]{:S(2)}, u32[]{:S(2)}) collective-permute-start(bf16[192,768]{1,0:T(8,128)(2,1)S(1)} %maximum_select_fusion.4), channel_id=1, source_target_pairs={{0,16},{4,20},{8,24},{12,28},{16,0},{20,4},{24,8},{28,12},{1,17},{... | collective-permute-start | bytes 884744 | tf_op jit(solution)/shard_map/ppermute | solution.py:66
  44.4 8.5 %collective-permute-start.4 = (bf16[384,768]{1,0:T(8,128)(2,1)S(1)}, bf16[384,768]{1,0:T(8,128)(2,1)}, u32[]{:S(2)}, u32[]{:S(2)}) collective-permute-start(bf16[384,768]{1,0:T(8,128)(2,1)S(1)} %maximum_select_fusion.2), channel_id=1, source_target_pairs={{0,4},{4,0},{8,12},{12,8},{16,20},{20,16},{24,28},{28,24},{1,5},{5... | collective-permute-start | bytes 1769480 | tf_op jit(solution)/shard_map/ppermute | solution.py:66
  45.7 36.5 %collective-permute-start.8 = (bf16[512,768]{1,0:T(8,128)(2,1)}, bf16[512,768]{1,0:T(8,128)(2,1)S(1)}, u32[]{:S(2)}, u32[]{:S(2)}) collective-permute-start(bf16[512,768]{1,0:T(8,128)(2,1)} %collective-permute-done.6.refs_4_.refs_1_), channel_id=1, source_target_pairs={{1,0},{2,3},{5,4},{6,7},{9,8},{10,11},{13,12},{14,15},{17,16},{18,... | collective-permute-start | bytes 2359304 | tf_op jit(solution)/shard_map/ppermute | solution.py:62
  51.9 30.3 %collective-permute-start.9 = (bf16[512,768]{1,0:T(8,128)(2,1)}, bf16[512,768]{1,0:T(8,128)(2,1)S(1)}, u32[]{:S(2)}, u32[]{:S(2)}) collective-permute-start(bf16[512,768]{1,0:T(8,128)(2,1)} %collective-permute-done.5.refs_3_.refs_1_), channel_id=1, source_target_pairs={{1,2},{2,1},{5,6},{6,5},{9,10},{10,9},{13,14},{14,13},{17,18},{18,... | collective-permute-start | bytes 2359304 | tf_op jit(solution)/shard_map/ppermute | solution.py:62
  79.4 20.6 %collective-permute-start.7 = (bf16[512,768]{1,0:T(8,128)(2,1)}, bf16[512,768]{1,0:T(8,128)(2,1)}, u32[]{:S(2)}, u32[]{:S(2)}) collective-permute-start(bf16[512,768]{1,0:T(8,128)(2,1)} %get-tuple-element.89), channel_id=1, source_target_pairs={{0,1},{1,0},{2,3},{3,2},{4,5},{5,4},{6,7},{7,6},{8,9},{9,8},{10,11... | collective-permute-start | bytes 2359304 | tf_op jit(solution)/shard_map/ppermute | solution.py:62
  104.9 26.7 %collective-permute-start.10 = (bf16[512,768]{1,0:T(8,128)(2,1)S(1)}, bf16[512,768]{1,0:T(8,128)(2,1)}, u32[]{:S(2)}, u32[]{:S(2)}) collective-permute-start(bf16[512,768]{1,0:T(8,128)(2,1)S(1)} %convert_element_type.109.refs_0_), channel_id=1, source_target_pairs={{0,1},{1,0},{2,3},{3,2},{4,5},{5,4},{6,7},{7,6},{8,9},{9,8},{10,11... | collective-permute-start | bytes 2359304 | tf_op jit(solution)/shard_map/ppermute | solution.py:62
  105.2 26.5 %collective-permute-start.11 = (bf16[512,768]{1,0:T(8,128)(2,1)S(1)}, bf16[512,768]{1,0:T(8,128)(2,1)}, u32[]{:S(2)}, u32[]{:S(2)}) collective-permute-start(bf16[512,768]{1,0:T(8,128)(2,1)S(1)} %convert_element_type.109.refs_0_), channel_id=1, source_target_pairs={{1,2},{2,1},{5,6},{6,5},{9,10},{10,9},{13,14},{14,13},{17,18},{18,... | collective-permute-start | bytes 2359304 | tf_op jit(solution)/shard_map/ppermute | solution.py:62
  107.8 23.1 %collective-permute-start.12 = (bf16[160,768]{1,0:T(8,128)(2,1)S(1)}, bf16[160,768]{1,0:T(8,128)(2,1)S(1)}, u32[]{:S(2)}, u32[]{:S(2)}) collective-permute-start(bf16[160,768]{1,0:T(8,128)(2,1)S(1)} %get-tuple-element.95), channel_id=1, source_target_pairs={{1,0},{2,3},{5,4},{6,7},{9,8},{10,11},{13,12},{14,15},{17,16},{18,... | collective-permute-start | bytes 737288 | tf_op jit(solution)/shard_map/ppermute | solution.py:62
  131.6 26.3 %collective-permute-start.14 = (bf16[512,768]{1,0:T(8,128)(2,1)}, bf16[512,768]{1,0:T(8,128)(2,1)}, u32[]{:S(2)}, u32[]{:S(2)}) collective-permute-start(bf16[512,768]{1,0:T(8,128)(2,1)} %collective-permute-done.11.refs_0_), channel_id=1, source_target_pairs={{1,0},{2,3},{5,4},{6,7},{9,8},{10,11},{13,12},{14,15},{17,16},{18,... | collective-permute-start | bytes 2359304 | tf_op jit(solution)/shard_map/ppermute | solution.py:62
  132.9 25.0 %collective-permute-start.15 = (bf16[512,768]{1,0:T(8,128)(2,1)}, bf16[512,768]{1,0:T(8,128)(2,1)}, u32[]{:S(2)}, u32[]{:S(2)}) collective-permute-start(bf16[512,768]{1,0:T(8,128)(2,1)} %collective-permute-done.10.refs_0_), channel_id=1, source_target_pairs={{1,2},{2,1},{5,6},{6,5},{9,10},{10,9},{13,14},{14,13},{17,18},{18,... | collective-permute-start | bytes 2359304 | tf_op jit(solution)/shard_map/ppermute | solution.py:62
  134.5 22.7 %collective-permute-start.16 = (bf16[160,768]{1,0:T(8,128)(2,1)S(1)}, bf16[160,768]{1,0:T(8,128)(2,1)S(1)}, u32[]{:S(2)}, u32[]{:S(2)}) collective-permute-start(bf16[160,768]{1,0:T(8,128)(2,1)S(1)} %get-tuple-element.104), channel_id=1, source_target_pairs={{1,0},{2,3},{5,4},{6,7},{9,8},{10,11},{13,12},{14,15},{17,16},{18,... | collective-permute-start | bytes 737288 | tf_op jit(solution)/shard_map/ppermute | solution.py:62
  157.9 26.3 %collective-permute-start.17 = (bf16[512,768]{1,0:T(8,128)(2,1)}, bf16[512,768]{1,0:T(8,128)(2,1)}, u32[]{:S(2)}, u32[]{:S(2)}) collective-permute-start(bf16[512,768]{1,0:T(8,128)(2,1)} %collective-permute-done.15.refs_0_), channel_id=1, source_target_pairs={{1,0},{2,3},{5,4},{6,7},{9,8},{10,11},{13,12},{14,15},{17,16},{18,... | collective-permute-start | bytes 2359304 | tf_op jit(solution)/shard_map/ppermute | solution.py:62
  160.9 23.3 %collective-permute-start.18 = (bf16[192,768]{1,0:T(8,128)(2,1)}, bf16[192,768]{1,0:T(8,128)(2,1)}, u32[]{:S(2)}, u32[]{:S(2)}) collective-permute-start(bf16[192,768]{1,0:T(8,128)(2,1)} %slice.135), channel_id=1, source_target_pairs={{1,0},{2,3},{5,4},{6,7},{9,8},{10,11},{13,12},{14,15},{17,16},{18,... | collective-permute-start | bytes 884744 | tf_op jit(solution)/shard_map/ppermute | solution.py:62
  164.5 19.7 %copy-start.12 = (bf16[160,768]{1,0:T(8,128)(2,1)S(1)}, bf16[160,768]{1,0:T(8,128)(2,1)}, u32[]{:S(2)}) copy-start(bf16[160,768]{1,0:T(8,128)(2,1)} %copy-done.11) | copy-start | bytes 737284
  164.5 19.7 %copy-start.14 = (bf16[160,768]{1,0:T(8,128)(2,1)S(1)}, bf16[160,768]{1,0:T(8,128)(2,1)}, u32[]{:S(2)}) copy-start(bf16[160,768]{1,0:T(8,128)(2,1)} %copy-done.13) | copy-start | bytes 737284
  203.5 23.6 %collective-permute-start.19 = (bf16[528,768]{1,0:T(8,128)(2,1)}, bf16[528,768]{1,0:T(8,128)(2,1)}, u32[]{:S(2)}, u32[]{:S(2)}) collective-permute-start(bf16[528,768]{1,0:T(8,128)(2,1)} %get-tuple-element.124), channel_id=1, source_target_pairs={{0,1},{3,2},{4,5},{7,6},{8,9},{11,10},{12,13},{15,14},{16,17},{19,... | collective-permute-start | bytes 2433032 | tf_op jit(solution)/shard_map/ppermute | solution.py:62
  227.1 249.4 %all-gather.2.cloned.1.call-start = ((), (), s32[]{:S(2)}) async-start(), calls=%async_computation.2 | async-start | bytes 15925248 | tf_op jit(solution)/shard_map/all_gather | solution.py:1037
  231.7 20.7 %collective-permute-start.23 = (bf16[528,768]{1,0:T(8,128)(2,1)}, bf16[528,768]{1,0:T(8,128)(2,1)}, u32[]{:S(2)}, u32[]{:S(2)}) collective-permute-start(bf16[528,768]{1,0:T(8,128)(2,1)} %get-tuple-element.114), channel_id=1, source_target_pairs={{0,1},{3,2},{4,5},{7,6},{8,9},{11,10},{12,13},{15,14},{16,17},{19,... | collective-permute-start | bytes 2433032 | tf_op jit(solution)/shard_map/ppermute | solution.py:62
  236.7 32.5 %collective-permute-start.21 = (bf16[512,768]{1,0:T(8,128)(2,1)}, bf16[512,768]{1,0:T(8,128)(2,1)}, u32[]{:S(2)}, u32[]{:S(2)}) collective-permute-start(bf16[512,768]{1,0:T(8,128)(2,1)} %get-tuple-element.130), channel_id=1, source_target_pairs={{0,1},{3,2},{4,5},{7,6},{8,9},{11,10},{12,13},{15,14},{16,17},{19,... | collective-permute-start | bytes 2359304 | tf_op jit(solution)/shard_map/ppermute | solution.py:62
  238.9 30.3 %collective-permute-start.20 = (bf16[528,768]{1,0:T(8,128)(2,1)}, bf16[528,768]{1,0:T(8,128)(2,1)}, u32[]{:S(2)}, u32[]{:S(2)}) collective-permute-start(bf16[528,768]{1,0:T(8,128)(2,1)} %add.361), channel_id=1, source_target_pairs={{1,2},{2,1},{5,6},{6,5},{9,10},{10,9},{13,14},{14,13},{17,18},{18,... | collective-permute-start | bytes 2433032 | tf_op jit(solution)/shard_map/ppermute | solution.py:62
  240.6 28.6 %copy-start.37 = (bf16[528,768]{1,0:T(8,128)(2,1)S(1)}, bf16[528,768]{1,0:T(8,128)(2,1)}, u32[]{:S(2)}) copy-start(bf16[528,768]{1,0:T(8,128)(2,1)} %get-tuple-element.105) | copy-start | bytes 2433028
  240.7 41.6 %collective-permute-start.22 = (bf16[528,768]{1,0:T(8,128)(2,1)}, bf16[528,768]{1,0:T(8,128)(2,1)S(1)}, u32[]{:S(2)}, u32[]{:S(2)}) collective-permute-start(bf16[528,768]{1,0:T(8,128)(2,1)} %get-tuple-element.105), channel_id=1, source_target_pairs={{0,1},{3,2},{4,5},{7,6},{8,9},{11,10},{12,13},{15,14},{16,17},{19,... | collective-permute-start | bytes 2433032 | tf_op jit(solution)/shard_map/ppermute | solution.py:62
  252.4 19.6 %copy-start.23 = (f32[512,768]{1,0:T(8,128)S(1)}, f32[512,768]{1,0:T(8,128)}, u32[]{:S(2)}) copy-start(f32[512,768]{1,0:T(8,128)} %param.18) | copy-start | bytes 4718596
  254.6 27.7 %collective-permute-start.24 = (bf16[528,768]{1,0:T(8,128)(2,1)S(1)}, bf16[528,768]{1,0:T(8,128)(2,1)S(1)}, u32[]{:S(2)}, u32[]{:S(2)}) collective-permute-start(bf16[528,768]{1,0:T(8,128)(2,1)S(1)} %add.364), channel_id=1, source_target_pairs={{1,2},{2,1},{5,6},{6,5},{9,10},{10,9},{13,14},{14,13},{17,18},{18,... | collective-permute-start | bytes 2433032 | tf_op jit(solution)/shard_map/ppermute | solution.py:62
  270.6 14.1 %collective-permute-start.25 = (bf16[528,768]{1,0:T(8,128)(2,1)S(1)}, bf16[528,768]{1,0:T(8,128)(2,1)S(1)}, u32[]{:S(2)}, u32[]{:S(2)}) collective-permute-start(bf16[528,768]{1,0:T(8,128)(2,1)S(1)} %add.366), channel_id=1, source_target_pairs={{1,0},{2,3},{5,4},{6,7},{9,8},{10,11},{13,12},{14,15},{17,16},{18,... | collective-permute-start | bytes 2433032 | tf_op jit(solution)/shard_map/ppermute | solution.py:62
  285.4 79.4 %copy-start.34 = (f32[512,10]{0,1:T(8,128)}, f32[512,10]{0,1:T(8,128)S(1)}, u32[]{:S(2)}) copy-start(f32[512,10]{0,1:T(8,128)S(1)} %select_reduce_fusion) | copy-start | bytes 61444
  290.8 14.0 %collective-permute-start.26 = (bf16[512,768]{1,0:T(8,128)(2,1)}, bf16[512,768]{1,0:T(8,128)(2,1)}, u32[]{:S(2)}, u32[]{:S(2)}) collective-permute-start(bf16[512,768]{1,0:T(8,128)(2,1)} %get-tuple-element.174.grad_own), channel_id=1, source_target_pairs={{0,1},{1,0},{2,3},{3,2},{4,5},{5,4},{6,7},{7,6},{8,9},{9,8},{10,11... | collective-permute-start | bytes 2359304 | tf_op jit(solution)/shard_map/ppermute | solution.py:62
  340.9 2.2 collective-permute-start.37
  347.6 14.5 %collective-permute-start.40 = (bf16[384,768]{1,0:T(8,128)(2,1)}, bf16[384,768]{1,0:T(8,128)(2,1)}, u32[]{:S(2)}, u32[]{:S(2)}) collective-permute-start(bf16[384,768]{1,0:T(8,128)(2,1)} %constant_dynamic-slice_fusion.2), channel_id=1, source_target_pairs={{0,4},{4,0},{8,12},{12,8},{16,20},{20,16},{24,28},{28,24},{1,5},{5... | collective-permute-start | bytes 1769480 | tf_op jit(solution)/shard_map/ppermute | solution.py:66
  350.2 21.9 %collective-permute-start.27 = (bf16[512,768]{1,0:T(8,128)(2,1)}, bf16[512,768]{1,0:T(8,128)(2,1)}, u32[]{:S(2)}, u32[]{:S(2)}) collective-permute-start(bf16[512,768]{1,0:T(8,128)(2,1)} %get-tuple-element.139), channel_id=1, source_target_pairs={{0,1},{3,2},{4,5},{7,6},{8,9},{11,10},{12,13},{15,14},{16,17},{19,... | collective-permute-start | bytes 2359304 | tf_op jit(solution)/shard_map/ppermute | solution.py:62
  354.8 21.3 %collective-permute-start.29 = (bf16[512,768]{1,0:T(8,128)(2,1)}, bf16[512,768]{1,0:T(8,128)(2,1)}, u32[]{:S(2)}, u32[]{:S(2)}) collective-permute-start(bf16[512,768]{1,0:T(8,128)(2,1)} %add.362), channel_id=1, source_target_pairs={{1,2},{2,1},{5,6},{6,5},{9,10},{10,9},{13,14},{14,13},{17,18},{18,... | collective-permute-start | bytes 2359304 | tf_op jit(solution)/shard_map/ppermute | solution.py:62
  358.1 82.8 %collective-permute-start.13 = (bf16[512,768]{1,0:T(8,128)(2,1)}, bf16[512,768]{1,0:T(8,128)(2,1)}, u32[]{:S(2)}, u32[]{:S(2)}) collective-permute-start(bf16[512,768]{1,0:T(8,128)(2,1)} %get-tuple-element.102), channel_id=1, source_target_pairs={{0,1},{3,2},{4,5},{7,6},{8,9},{11,10},{12,13},{15,14},{16,17},{19,... | collective-permute-start | bytes 2359304 | tf_op jit(solution)/shard_map/ppermute | solution.py:62
  363.5 16.2 %collective-permute-start.41 = (bf16[192,768]{1,0:T(8,128)(2,1)S(1)}, bf16[192,768]{1,0:T(8,128)(2,1)S(1)}, u32[]{:S(2)}, u32[]{:S(2)}) collective-permute-start(bf16[192,768]{1,0:T(8,128)(2,1)S(1)} %constant_dynamic-slice_fusion.1), channel_id=1, source_target_pairs={{0,8},{4,12},{8,0},{12,4},{16,24},{20,28},{24,16},{28,20},{1,9},{5... | collective-permute-start | bytes 884744 | tf_op jit(solution)/shard_map/ppermute | solution.py:66
  365.6 42.0 %collective-permute-start.38 = (bf16[192,768]{1,0:T(8,128)(2,1)S(1)}, bf16[192,768]{1,0:T(8,128)(2,1)S(1)}, u32[]{:S(2)}, u32[]{:S(2)}) collective-permute-start(bf16[192,768]{1,0:T(8,128)(2,1)S(1)} %constant_dynamic-slice_fusion.4), channel_id=1, source_target_pairs={{0,8},{4,12},{8,0},{12,4},{16,24},{20,28},{24,16},{28,20},{1,9},{5... | collective-permute-start | bytes 884744 | tf_op jit(solution)/shard_map/ppermute | solution.py:66
  374.5 66.4 %collective-permute-start.28 = (bf16[512,768]{1,0:T(8,128)(2,1)}, bf16[512,768]{1,0:T(8,128)(2,1)}, u32[]{:S(2)}, u32[]{:S(2)}) collective-permute-start(bf16[512,768]{1,0:T(8,128)(2,1)} %add.375), channel_id=1, source_target_pairs={{1,2},{2,1},{5,6},{6,5},{9,10},{10,9},{13,14},{14,13},{17,18},{18,... | collective-permute-start | bytes 2359304 | tf_op jit(solution)/shard_map/ppermute | solution.py:62
  378.3 39.9 %copy-start.35 = (f32[512,10]{0,1:T(8,128)S(1)}, f32[512,10]{0,1:T(8,128)}, u32[]{:S(2)}) copy-start(f32[512,10]{0,1:T(8,128)} %copy-done.34) | copy-start | bytes 61444
  378.3 62.6 %collective-permute-start.30 = (bf16[512,768]{1,0:T(8,128)(2,1)}, bf16[512,768]{1,0:T(8,128)(2,1)S(1)}, u32[]{:S(2)}, u32[]{:S(2)}) collective-permute-start(bf16[512,768]{1,0:T(8,128)(2,1)} %add.377), channel_id=1, source_target_pairs={{1,0},{2,3},{5,4},{6,7},{9,8},{10,11},{13,12},{14,15},{17,16},{18,... | collective-permute-start | bytes 2359304 | tf_op jit(solution)/shard_map/ppermute | solution.py:62
  379.8 47.8 %copy-start.55 = (f32[10,10]{1,0:T(8,128)S(1)}, f32[10,10]{1,0:T(8,128)}, u32[]{:S(2)}) copy-start(f32[10,10]{1,0:T(8,128)} %param.24) | copy-start | bytes 1204
  379.8 48.5 %copy-start.18 = (f32[8,768]{1,0:T(8,128)S(1)}, f32[8,768]{1,0:T(8,128)}, u32[]{:S(2)}) copy-start(f32[8,768]{1,0:T(8,128)} %copy-done.17) | copy-start | bytes 73732
  379.8 37.8 %collective-permute-start.42 = (bf16[96,768]{1,0:T(8,128)(2,1)S(1)}, bf16[96,768]{1,0:T(8,128)(2,1)S(1)}, u32[]{:S(2)}, u32[]{:S(2)}) collective-permute-start(bf16[96,768]{1,0:T(8,128)(2,1)S(1)} %constant_dynamic-slice_fusion), channel_id=1, source_target_pairs={{0,16},{4,20},{8,24},{12,28},{16,0},{20,4},{24,8},{28,12},{1,17},{... | collective-permute-start | bytes 442376 | tf_op jit(solution)/shard_map/ppermute | solution.py:66
  407.7 34.1 %copy-start.7 = (bf16[512,768]{1,0:T(8,128)(2,1)S(1)}, bf16[512,768]{1,0:T(8,128)(2,1)}, u32[]{:S(2)}) copy-start(bf16[512,768]{1,0:T(8,128)(2,1)} %copy-done.5) | copy-start | bytes 2359300
  407.7 34.1 %copy-start.65 = (f32[512]{0:T(512)S(1)}, f32[512]{0:T(512)}, u32[]{:S(2)}) copy-start(f32[512]{0:T(512)} %copy-done.64) | copy-start | bytes 6148
  407.7 13.8 %collective-permute-start.39 = (bf16[96,768]{1,0:T(8,128)(2,1)S(1)}, bf16[96,768]{1,0:T(8,128)(2,1)S(1)}, u32[]{:S(2)}, u32[]{:S(2)}) collective-permute-start(bf16[96,768]{1,0:T(8,128)(2,1)S(1)} %constant_dynamic-slice_fusion.3), channel_id=1, source_target_pairs={{0,16},{4,20},{8,24},{12,28},{16,0},{20,4},{24,8},{28,12},{1,17},{... | collective-permute-start | bytes 442376 | tf_op jit(solution)/shard_map/ppermute | solution.py:66
  417.7 9.4 %collective-permute-start.43 = (bf16[96,768]{1,0:T(8,128)(2,1)S(1)}, bf16[96,768]{1,0:T(8,128)(2,1)S(1)}, u32[]{:S(2)}, u32[]{:S(2)}) collective-permute-start(bf16[96,768]{1,0:T(8,128)(2,1)S(1)} %dynamic-slice_add_fusion.4), channel_id=1, source_target_pairs={{0,2},{1,3},{2,0},{3,1},{4,6},{5,7},{6,4},{7,5},{8,10},{9,11},{10,... | collective-permute-start | bytes 442376 | tf_op jit(solution)/shard_map/ppermute | solution.py:62
  427.2 9.3 %collective-permute-start.44 = (bf16[96,768]{1,0:T(8,128)(2,1)S(1)}, bf16[96,768]{1,0:T(8,128)(2,1)S(1)}, u32[]{:S(2)}, u32[]{:S(2)}) collective-permute-start(bf16[96,768]{1,0:T(8,128)(2,1)S(1)} %add_add_fusion.1), channel_id=1, source_target_pairs={{0,16},{4,20},{8,24},{12,28},{16,0},{20,4},{24,8},{28,12},{1,17},{... | collective-permute-start | bytes 442376 | tf_op jit(solution)/shard_map/ppermute | solution.py:66
  428.4 23.2 %collective-permute-start.31 = (bf16[512,768]{1,0:T(8,128)(2,1)}, bf16[512,768]{1,0:T(8,128)(2,1)}, u32[]{:S(2)}, u32[]{:S(2)}) collective-permute-start(bf16[512,768]{1,0:T(8,128)(2,1)} %get-tuple-element.141), channel_id=1, source_target_pairs={{0,1},{1,0},{2,3},{3,2},{4,5},{5,4},{6,7},{7,6},{8,9},{9,8},{10,11... | collective-permute-start | bytes 2359304 | tf_op jit(solution)/shard_map/ppermute | solution.py:62
  437.3 20.8 %collective-permute-start.45 = (bf16[192,768]{1,0:T(8,128)(2,1)}, bf16[192,768]{1,0:T(8,128)(2,1)}, u32[]{:S(2)}, u32[]{:S(2)}) collective-permute-start(bf16[192,768]{1,0:T(8,128)(2,1)} %maximum_select_fusion.5), channel_id=1, source_target_pairs={{0,8},{4,12},{8,0},{12,4},{16,24},{20,28},{24,16},{28,20},{1,9},{5... | collective-permute-start | bytes 884744 | tf_op jit(solution)/shard_map/ppermute | solution.py:66
  451.5 4.7 collective-permute-start.32
  453.1 18.1 %copy-start.28 = (f32[512,768]{1,0:T(8,128)S(1)}, f32[512,768]{1,0:T(8,128)}, u32[]{:S(2)}) copy-start(f32[512,768]{1,0:T(8,128)} %get-tuple-element.175) | copy-start | bytes 4718596
  453.1 18.1 %copy-start.63 = (f32[512]{0:T(512)S(1)}, f32[512]{0:T(512)}, u32[]{:S(2)}) copy-start(f32[512]{0:T(512)} %copy-done.62) | copy-start | bytes 6148
  456.2 6.3 %collective-permute-start.33 = (f32[29,768]{1,0:T(8,128)S(1)}, f32[29,768]{1,0:T(8,128)S(1)}, u32[]{:S(2)}, u32[]{:S(2)}) collective-permute-start(f32[29,768]{1,0:T(8,128)S(1)} %add.384), channel_id=1, source_target_pairs={{0,2},{1,3},{2,0},{3,1},{4,6},{5,7},{6,4},{7,5},{8,10},{9,11},{10,... | collective-permute-start | bytes 267272 | tf_op jit(solution)/shard_map/ppermute | solution.py:62
  459.4 14.7 %collective-permute-start.46 = (bf16[384,768]{1,0:T(8,128)(2,1)S(1)}, bf16[384,768]{1,0:T(8,128)(2,1)S(1)}, u32[]{:S(2)}, u32[]{:S(2)}) collective-permute-start(bf16[384,768]{1,0:T(8,128)(2,1)S(1)} %maximum_select_fusion.3), channel_id=1, source_target_pairs={{0,4},{4,0},{8,12},{12,8},{16,20},{20,16},{24,28},{28,24},{1,5},{5... | collective-permute-start | bytes 1769480 | tf_op jit(solution)/shard_map/ppermute | solution.py:66
  462.5 6.8 %collective-permute-start.34 = (f32[29,768]{1,0:T(8,128)S(1)}, f32[29,768]{1,0:T(8,128)S(1)}, u32[]{:S(2)}, u32[]{:S(2)}) collective-permute-start(f32[29,768]{1,0:T(8,128)S(1)} %add.385), channel_id=1, source_target_pairs={{0,8},{4,12},{8,0},{12,4},{16,24},{20,28},{24,16},{28,20},{1,9},{5... | collective-permute-start | bytes 267272 | tf_op jit(solution)/shard_map/ppermute | solution.py:66
  469.2 4.7 collective-permute-start.35
  474.0 19.0 %collective-permute-start.36 = (f32[29,768]{1,0:T(8,128)S(1)}, f32[29,768]{1,0:T(8,128)S(1)}, u32[]{:S(2)}, u32[]{:S(2)}) collective-permute-start(f32[29,768]{1,0:T(8,128)S(1)} %add.387), channel_id=1, source_target_pairs={{0,4},{4,0},{8,12},{12,8},{16,20},{20,16},{24,28},{28,24},{1,5},{5... | collective-permute-start | bytes 267272 | tf_op jit(solution)/shard_map/ppermute | solution.py:66
  (57 other events, 304.4 us)
Sparse Core Ops, SparseCore 0:
  227.2 117.2 reduce-scatter.1
  346.3 125.3 all-gather.1
